TPU v7x, 32 devices: a whole 2x2x4 slice. The times are simulated.
32 devices in a mesh: dp: 8 (over z, x), seq: 4 (over y, core).
Axes of the slice: x: 2, y: 2, z: 4, core: 2. Of those that a mesh axis runs over, the one named last changes fastest.
Arguments:
- tokens: bfloat16 [16384, 768], P(('dp', 'seq')), may hold values from -6 to 6
- filled_blocks: int32 [8], P('dp'), may hold values from 25 to 32, as said below
- random_blocks: int32 [8, 32, 12, 3], P('dp', None, 'seq'), may hold values from 1 to 30, as said below
- query_weight: bfloat16 [768, 768], replicated, may hold values from -0.3125 to 0.3125
- query_bias: float32 [768], replicated, may hold values from -1.75 to 1.75
- key_weight: bfloat16 [768, 768], replicated, may hold values from -0.21875 to 0.21875
- value_weight: bfloat16 [768, 768], replicated, may hold values from -0.21875 to 0.21875
- value_bias: float32 [768], replicated, may hold values from -1.75 to 1.75
- out_weight: bfloat16 [768, 768], replicated, may hold values from -1.75 to 1.75
- out_bias: float32 [768], replicated, may hold values from -1.75 to 1.75
- attn_gain: float32 [768], replicated, may hold values from 0.1 to 1.9
- attn_shift: float32 [768], replicated, may hold values from -1.75 to 1.75
- up_weight: bfloat16 [768, 3072], replicated, may hold values from -0.21875 to 0.21875
- up_bias: float32 [3072], replicated, may hold values from -1.75 to 1.75
- down_weight: bfloat16 [3072, 768], replicated, may hold values from -0.109375 to 0.109375
- down_bias: float32 [768], replicated, may hold values from -1.75 to 1.75
- ffn_gain: float32 [768], replicated, may hold values from 0.1 to 1.9
- ffn_shift: float32 [768], replicated, may hold values from -1.75 to 1.75
- cotangent: bfloat16 [16384, 768], P(('dp', 'seq')), may hold values from -6 to 6
Outputs:
- layer_out: bfloat16 [16384, 768], P(('dp', 'seq'))
- grad_tokens: float32 [16384, 768], P(('dp', 'seq'))
- grad_query_weight: float32 [768, 768], P(('dp', 'seq'))
- grad_query_bias: float32 [768], P(('dp', 'seq'))
- grad_key_weight: float32 [768, 768], P(('dp', 'seq'))
- grad_value_weight: float32 [768, 768], P(('dp', 'seq'))
- grad_value_bias: float32 [768], P(('dp', 'seq'))
- grad_out_weight: float32 [768, 768], P(('dp', 'seq'))
- grad_out_bias: float32 [768], P(('dp', 'seq'))
- grad_attn_gain: float32 [768], P(('dp', 'seq'))
- grad_attn_shift: float32 [768], P(('dp', 'seq'))
- grad_up_weight: float32 [768, 3072], P(('dp', 'seq'))
- grad_up_bias: float32 [3072], P(('dp', 'seq'))
- grad_down_weight: float32 [3072, 768], P(('dp', 'seq'))
- grad_down_bias: float32 [768], P(('dp', 'seq'))
- grad_ffn_gain: float32 [768], P(('dp', 'seq'))
- grad_ffn_shift: float32 [768], P(('dp', 'seq'))
Inputs may be any that keep to these rules, and one draw needn't show every extreme that they name: Slot s holds 64 * filled_blocks[s] tokens of one document, the rest padding; in every draw some slot is full and some other slot has the fewest. `random_blocks`: the three entries of a slot, query block and head differ from each other, lie below the slot's filled_blocks, and are none of block 0, the slot's last filled block, the query block and its two neighbours.
All inputs are finite; a program needn't handle non-finite values.
Results may differ from a plain program's by a relative error of at most 0.015.
The roundings to bfloat16 on the way count: a program that leaves them out, or rounds other values in their place, can miss the bound.
Values may be sent and summed in bfloat16 or wider, within the bound.
A program may use at most 192 MiB of HBM per device.

v0:
```python
import jax
import jax.numpy as jnp
from jax import lax
from jax.sharding import PartitionSpec as P

HEAD_DIM = 64
BLK = 64


NORM_EPS = 1e-05
MASKED = -1e30


def key_table(filled, chosen, block_count):
    rows_at = jnp.arange(block_count, dtype=jnp.int32)[:, None]
    window = rows_at + jnp.array([-1, 0, 1], dtype=jnp.int32)[None, :]
    window_ok = (window >= 0) & (window < filled)
    window = jnp.clip(window, 0, block_count - 1)
    head_count = chosen.shape[1]
    last_block = jnp.zeros_like(rows_at) + (filled - 1)
    global_index = jnp.concatenate([jnp.zeros_like(rows_at), last_block], axis=1)
    global_ok = jnp.concatenate([rows_at >= 2, jnp.abs(rows_at - (filled - 1)) > 1], axis=1)
    index = jnp.concatenate(
        [
            jnp.broadcast_to(window[:, None, :], (block_count, head_count, 3)),
            chosen,
            jnp.broadcast_to(global_index[:, None, :], (block_count, head_count, 2)),
        ],
        axis=2,
    )
    allowed = jnp.concatenate(
        [
            jnp.broadcast_to(window_ok[:, None, :], (block_count, head_count, 3)),
            jnp.ones((block_count, head_count, 3), dtype=jnp.bool_),
            jnp.broadcast_to(global_ok[:, None, :], (block_count, head_count, 2)),
        ],
        axis=2,
    )
    return (index, allowed)


def layer_norm(values, gain, shift):
    center = jnp.mean(values, axis=-1, keepdims=True)
    centered = values - center
    variance = jnp.mean(centered * centered, axis=-1, keepdims=True)
    inv_root = lax.rsqrt(variance + NORM_EPS)
    normed = centered * inv_root
    return (normed * gain + shift, normed, inv_root)


def norm_back(grad_out, normed, inv_root, gain):
    d_normed = grad_out * gain
    grad_in = inv_root * (
        d_normed
        - jnp.mean(d_normed, axis=-1, keepdims=True)
        - normed * jnp.mean(d_normed * normed, axis=-1, keepdims=True)
    )
    return (grad_in, jnp.sum(grad_out * normed, axis=0), jnp.sum(grad_out, axis=0))


def outer_sum(left, right):
    return lax.dot_general(
        left, right, (((0,), (0,)), ((), ())), preferred_element_type=jnp.float32
    )


def back_product(grad, weight):
    return lax.dot_general(
        grad, weight, (((1,), (1,)), ((), ())), preferred_element_type=jnp.float32
    )


def split_heads(tensor, groups):
    return tensor.reshape(tensor.shape[0], groups, -1)


def head_blocks(tensor):
    return tensor.reshape(tensor.shape[0] // BLK, BLK, -1, HEAD_DIM).transpose(2, 0, 1, 3)


def join_heads(tensor):
    head_count, block_count, block_len, head_len = tensor.shape
    return tensor.transpose(1, 2, 0, 3).reshape(block_count * block_len, 1, head_count * head_len)


def projections(tokens, query_weight, query_bias, key_weight, value_weight, value_bias, groups):
    query = (jnp.dot(tokens, query_weight, preferred_element_type=jnp.float32) + query_bias).astype(
        jnp.bfloat16
    )
    keys = jnp.dot(tokens, key_weight, preferred_element_type=jnp.float32).astype(jnp.bfloat16)
    values = (
        jnp.dot(tokens, value_weight, preferred_element_type=jnp.float32) + value_bias
    ).astype(jnp.bfloat16)
    return (split_heads(query, groups), split_heads(keys, groups), split_heads(values, groups))


def gather_keys(keys, values, index, allowed, block_len):
    group_len = index.shape[0]
    head_len = keys.shape[-1]
    mask = jnp.repeat(allowed, block_len, axis=1)[:, None, :]
    return (
        keys[index].reshape(group_len, -1, head_len),
        values[index].reshape(group_len, -1, head_len),
        mask,
    )


def head_scores(query, picked_keys, mask):
    scores = jnp.einsum(
        "pqd,pkd->pqk", query, picked_keys, preferred_element_type=jnp.float32
    ) * HEAD_DIM ** (-0.5)
    return jnp.where(mask, scores, MASKED)


def forward_head(query, keys, values, index, allowed):
    picked_keys, picked_values, mask = gather_keys(keys, values, index, allowed, query.shape[1])
    scores = head_scores(query, picked_keys, mask)
    highest = jnp.max(scores, axis=-1, keepdims=True)
    weights = jnp.exp(scores - highest)
    total = jnp.sum(weights, axis=-1, keepdims=True)
    share = (weights / total).astype(jnp.bfloat16)
    output = jnp.einsum("pqk,pkd->pqd", share, picked_values, preferred_element_type=jnp.float32)
    return (output, (highest + jnp.log(total))[..., 0])


def backward_head(
    query, keys, values, index, allowed, log_total, grad_out, keys_total, values_total
):
    picked_keys, picked_values, mask = gather_keys(keys, values, index, allowed, query.shape[1])
    scores = head_scores(query, picked_keys, mask)
    share = jnp.exp(scores - log_total[..., None])
    d_share = jnp.einsum(
        "pqd,pkd->pqk", grad_out, picked_values, preferred_element_type=jnp.float32
    )
    centre = jnp.sum(share * d_share, axis=-1, keepdims=True)
    d_scores = (share * (d_share - centre)).astype(jnp.bfloat16)
    scale = HEAD_DIM ** (-0.5)
    d_query = (
        jnp.einsum("pqk,pkd->pqd", d_scores, picked_keys, preferred_element_type=jnp.float32)
        * scale
    )
    d_keys = jnp.einsum("pqk,pqd->pkd", d_scores, query, preferred_element_type=jnp.float32) * scale
    d_values = jnp.einsum(
        "pqk,pqd->pkd", share.astype(jnp.bfloat16), grad_out, preferred_element_type=jnp.float32
    )
    block_len, head_len = (query.shape[1], query.shape[2])
    flat_index = index.reshape(-1)
    keys_total = keys_total.at[flat_index].add(d_keys.reshape(-1, block_len, head_len))
    values_total = values_total.at[flat_index].add(d_values.reshape(-1, block_len, head_len))
    return (d_query, keys_total, values_total)


def group_split(query, index, allowed, per_group):
    head_count, block_count, block_len, head_len = query.shape
    groups = block_count // per_group
    query_groups = query.reshape(head_count, groups, per_group, block_len, head_len).transpose(
        1, 0, 2, 3, 4
    )
    index_groups = index.reshape(groups, per_group, head_count, -1).transpose(0, 2, 1, 3)
    allowed_groups = allowed.reshape(groups, per_group, head_count, -1).transpose(0, 2, 1, 3)
    return (query_groups, index_groups, allowed_groups)


def group_join(tensor):
    moved = jnp.moveaxis(tensor, 0, 1)
    return moved.reshape((moved.shape[0], moved.shape[1] * moved.shape[2]) + moved.shape[3:])


def run_forward(query, keys, values, index, allowed):
    per_group = min(query.shape[1], 512 // BLK)
    scanned = group_split(query, index, allowed, per_group)

    def one_group(inputs):
        return jax.vmap(forward_head)(inputs[0], keys, values, inputs[1], inputs[2])

    outputs, log_totals = lax.map(one_group, scanned)
    return (group_join(outputs), group_join(log_totals))


def run_backward(query, keys, values, index, allowed, log_total, grad_out):
    per_group = min(query.shape[1], 512 // BLK)
    query_groups, index_groups, allowed_groups = group_split(query, index, allowed, per_group)
    groups = query_groups.shape[0]
    log_groups = jnp.moveaxis(log_total.reshape(log_total.shape[0], groups, per_group, -1), 1, 0)
    grad_groups = jnp.moveaxis(
        grad_out.reshape(
            grad_out.shape[0], groups, per_group, grad_out.shape[2], grad_out.shape[3]
        ),
        1,
        0,
    )

    def one_group(totals, inputs):
        d_query, keys_total, values_total = jax.vmap(backward_head)(
            inputs[0],
            keys,
            values,
            inputs[1],
            inputs[2],
            inputs[3],
            inputs[4],
            totals[0],
            totals[1],
        )
        return ((keys_total, values_total), d_query)

    empty = jnp.zeros(keys.shape, jnp.float32)
    totals, d_query = lax.scan(
        one_group,
        (empty, empty),
        (query_groups, index_groups, allowed_groups, log_groups, grad_groups),
    )
    return (group_join(d_query), totals[0], totals[1])


def on_device(
    tokens,
    filled_blocks,
    random_blocks,
    query_weight,
    query_bias,
    key_weight,
    value_weight,
    value_bias,
    out_weight,
    out_bias,
    attn_gain,
    attn_shift,
    up_weight,
    up_bias,
    down_weight,
    down_bias,
    ffn_gain,
    ffn_shift,
    cotangent,
):
    seq_count = lax.axis_size("seq")
    row_count, feature_count = tokens.shape
    filled = filled_blocks[0]
    place = lax.axis_index("seq") * row_count + jnp.arange(row_count, dtype=jnp.int32)
    live_tokens = (place < filled * BLK).astype(jnp.float32)[:, None]
    local_query, local_keys, local_values = projections(
        tokens, query_weight, query_bias, key_weight, value_weight, value_bias, seq_count
    )
    arrived = (
        lax.all_to_all(local_query, "seq", split_axis=1, concat_axis=0, tiled=True),
        lax.all_to_all(local_keys, "seq", split_axis=1, concat_axis=0, tiled=True),
        lax.all_to_all(local_values, "seq", split_axis=1, concat_axis=0, tiled=True),
    )
    query_heads = head_blocks(arrived[0])
    key_heads = head_blocks(arrived[1])
    value_heads = head_blocks(arrived[2])
    block_count = query_heads.shape[1]
    index, allowed = key_table(filled, random_blocks[0], block_count)
    live_blocks = (jnp.arange(block_count, dtype=jnp.int32) < filled)[None, :, None, None]
    heads_out, log_total = run_forward(query_heads, key_heads, value_heads, index, allowed)
    heads_low = jnp.where(live_blocks, heads_out, 0.0).astype(jnp.bfloat16)
    merged = lax.all_to_all(
        join_heads(heads_low), "seq", split_axis=0, concat_axis=1, tiled=True
    ).reshape(row_count, feature_count)
    attn = jnp.dot(merged, out_weight, preferred_element_type=jnp.float32) + out_bias
    first, normed_one, root_one = layer_norm(
        tokens.astype(jnp.float32) + attn, attn_gain, attn_shift
    )
    first_low = first.astype(jnp.bfloat16)
    hidden = jnp.dot(first_low, up_weight, preferred_element_type=jnp.float32) + up_bias
    act, gelu_pull = jax.vjp(jax.nn.gelu, hidden)
    act_low = act.astype(jnp.bfloat16)
    ffn = jnp.dot(act_low, down_weight, preferred_element_type=jnp.float32) + down_bias
    result, normed_two, root_two = layer_norm(first + ffn, ffn_gain, ffn_shift)
    grad_result = cotangent.astype(jnp.float32) * live_tokens
    d_sum_two, grad_ffn_gain, grad_ffn_shift = norm_back(
        grad_result, normed_two, root_two, ffn_gain
    )
    d_ffn = d_sum_two.astype(jnp.bfloat16)
    grad_down_bias = jnp.sum(d_ffn, axis=0, dtype=jnp.float32)
    grad_down_weight = outer_sum(act_low, d_ffn)
    d_act = back_product(d_ffn, down_weight)
    d_hidden = gelu_pull(d_act)[0].astype(jnp.bfloat16)
    grad_up_bias = jnp.sum(d_hidden, axis=0, dtype=jnp.float32)
    grad_up_weight = outer_sum(first_low, d_hidden)
    d_first = d_sum_two + back_product(d_hidden, up_weight)
    d_sum_one, grad_attn_gain, grad_attn_shift = norm_back(d_first, normed_one, root_one, attn_gain)
    d_attn = d_sum_one.astype(jnp.bfloat16)
    grad_out_bias = jnp.sum(d_attn, axis=0, dtype=jnp.float32)
    grad_out_weight = outer_sum(merged, d_attn)
    d_merged = back_product(d_attn, out_weight).astype(jnp.bfloat16)
    d_heads = head_blocks(
        lax.all_to_all(
            split_heads(d_merged, seq_count), "seq", split_axis=1, concat_axis=0, tiled=True
        )
    )
    d_heads = jnp.where(live_blocks, d_heads, jnp.zeros((), jnp.bfloat16))
    again_query, again_keys, again_values = projections(
        tokens, query_weight, query_bias, key_weight, value_weight, value_bias, seq_count
    )
    fresh = (
        lax.all_to_all(again_query, "seq", split_axis=1, concat_axis=0, tiled=True),
        lax.all_to_all(again_keys, "seq", split_axis=1, concat_axis=0, tiled=True),
        lax.all_to_all(again_values, "seq", split_axis=1, concat_axis=0, tiled=True),
    )
    query_back = head_blocks(fresh[0])
    keys_back = head_blocks(fresh[1])
    values_back = head_blocks(fresh[2])
    d_query, d_keys, d_values = run_backward(
        query_back, keys_back, values_back, index, allowed, log_total, d_heads
    )
    returned = (
        lax.all_to_all(
            join_heads(d_query.astype(jnp.bfloat16)), "seq", split_axis=0, concat_axis=1, tiled=True
        ),
        lax.all_to_all(
            join_heads(d_keys.astype(jnp.bfloat16)), "seq", split_axis=0, concat_axis=1, tiled=True
        ),
        lax.all_to_all(
            join_heads(d_values.astype(jnp.bfloat16)),
            "seq",
            split_axis=0,
            concat_axis=1,
            tiled=True,
        ),
    )
    d_query_tok = returned[0].reshape(row_count, feature_count)
    d_keys_tok = returned[1].reshape(row_count, feature_count)
    d_values_tok = returned[2].reshape(row_count, feature_count)
    grad_tokens = (
        d_sum_one
        + back_product(d_query_tok, query_weight)
        + back_product(d_keys_tok, key_weight)
        + back_product(d_values_tok, value_weight)
    )
    grad_query_weight = outer_sum(tokens, d_query_tok)
    grad_query_bias = jnp.sum(d_query_tok, axis=0, dtype=jnp.float32)
    grad_key_weight = outer_sum(tokens, d_keys_tok)
    grad_value_weight = outer_sum(tokens, d_values_tok)
    grad_value_bias = jnp.sum(d_values_tok, axis=0, dtype=jnp.float32)
    summed = (
        lax.psum_scatter(grad_query_weight, ("dp", "seq"), scatter_dimension=0, tiled=True),
        lax.psum_scatter(grad_query_bias, ("dp", "seq"), scatter_dimension=0, tiled=True),
        lax.psum_scatter(grad_key_weight, ("dp", "seq"), scatter_dimension=0, tiled=True),
        lax.psum_scatter(grad_value_weight, ("dp", "seq"), scatter_dimension=0, tiled=True),
        lax.psum_scatter(grad_value_bias, ("dp", "seq"), scatter_dimension=0, tiled=True),
        lax.psum_scatter(grad_out_weight, ("dp", "seq"), scatter_dimension=0, tiled=True),
        lax.psum_scatter(grad_out_bias, ("dp", "seq"), scatter_dimension=0, tiled=True),
        lax.psum_scatter(grad_attn_gain, ("dp", "seq"), scatter_dimension=0, tiled=True),
        lax.psum_scatter(grad_attn_shift, ("dp", "seq"), scatter_dimension=0, tiled=True),
        lax.psum_scatter(grad_up_weight, ("dp", "seq"), scatter_dimension=0, tiled=True),
        lax.psum_scatter(grad_up_bias, ("dp", "seq"), scatter_dimension=0, tiled=True),
        lax.psum_scatter(grad_down_weight, ("dp", "seq"), scatter_dimension=0, tiled=True),
        lax.psum_scatter(grad_down_bias, ("dp", "seq"), scatter_dimension=0, tiled=True),
        lax.psum_scatter(grad_ffn_gain, ("dp", "seq"), scatter_dimension=0, tiled=True),
        lax.psum_scatter(grad_ffn_shift, ("dp", "seq"), scatter_dimension=0, tiled=True),
    )
    return (result.astype(jnp.bfloat16), grad_tokens) + tuple(summed)


def solution(mesh):
    placed = (
        P(("dp", "seq"), None),
        P("dp"),
        P("dp", None, "seq", None),
        P(),
        P(),
        P(),
        P(),
        P(),
        P(),
        P(),
        P(),
        P(),
        P(),
        P(),
        P(),
        P(),
        P(),
        P(),
        P(("dp", "seq"), None),
    )
    return jax.shard_map(
        on_device,
        mesh=mesh,
        in_specs=placed,
        out_specs=(
            P(("dp", "seq"), None),
            P(("dp", "seq"), None),
            P(("dp", "seq"), None),
            P(("dp", "seq")),
            P(("dp", "seq"), None),
            P(("dp", "seq"), None),
            P(("dp", "seq")),
            P(("dp", "seq"), None),
            P(("dp", "seq")),
            P(("dp", "seq")),
            P(("dp", "seq")),
            P(("dp", "seq"), None),
            P(("dp", "seq")),
            P(("dp", "seq"), None),
            P(("dp", "seq")),
            P(("dp", "seq")),
            P(("dp", "seq")),
        ),
        check_vma=False,
    )
```

profile of v0, /device:TPU:0, one launch (start us, length us, event | category | flops | bytes accessed | tf_op | source)
XLA Modules:
  0.0 1311.9 jit_solution(14669594389518897492)
XLA Ops:
  34.0 7.9 all-to-all-done.2
  77.1 116.1 %while.26 = (s32[]{:T(128)}, bf16[4,3,8,64,64]{4,3,2,1,0:T(8,128)(2,1)}, f32[4,3,8,64]{3,2,1,0:T(8,128)}, pred[4,3,8,8]{3,2,1,0:T(8,128)(4,1)}, bf16[4,3,8,64,64...) while((s32[]{:T(128)}, ...), condition=%wide.region_3.4_spmd, body=%wide.region_0.3_spmd.sunk | while | flops 210763776 | bytes 34410252 | solution.py:176
  84.4 5.0 gather_fusion.1
  96.6 5.0 gather_fusion
  113.4 5.0 gather_fusion.1
  125.6 5.0 gather_fusion
  130.6 4.6 fusion.127
  142.3 5.0 gather_fusion.1
  154.6 5.0 gather_fusion
  171.3 5.0 gather_fusion.1
  183.6 5.0 gather_fusion
  198.2 9.1 reshape.444
  207.8 13.6 %reduce.7 = bf16[2048,192]{1,0:T(8,128)(2,1)} reduce(bf16[2048,1,192]{2,1,0:T(2,128)(2,1)} %reshape.444, bf16[]{:T(256)} %broadcast.408), dimensions={1}, to_apply=%reshape.444.reduce_sub_computation | reduce | bytes 1572866 | tf_op jit(solution)/shard_map/reshape | solution.py:83
  229.9 11.7 all-to-all-done.3
  245.7 5.7 copy.215
  257.2 5.5 fusion.61
  271.8 7.2 convert_reduce_fusion
  294.2 7.8 all-to-all-done.4
  311.2 355.6 %while.27 = (s32[]{:T(128)}, f32[3,32,64,64]{3,2,1,0:T(8,128)}, f32[3,32,64,64]{3,2,1,0:T(8,128)}, bf16[4,3,8,64,64]{4,3,2,0,1:T(8,128)(2,1)}, s32[4,3,8,8]{2,0,...) while((s32[]{:T(128)}, f32[3,32,64,64]{3,2,1,0:T(8,128)}, ...), condition=%wide.region_16.17_spmd, body=%wide.region_12.16_spmd.sunk | while | flops 512854272 | bytes 95722944 | solution.py:208
  320.1 5.1 gather_fusion.2
  340.2 21.7 %scatter_fusion.1 = f32[3,32,64,64]{3,2,1,0:T(8,128)S(1)} fusion(f32[3,32,64,64]{3,2,1,0:T(8,128)S(1)} %copy-done.2, s32[192]{0:T(256)S(1)} %reshape.495, f32[192,64,64]{2,1,0:T(8,128)} %bitcast.241), kind=kCustom, calls=%fused_computation.5.clone.1 | custom fusion | flops 786432 | bytes 9438720 | tf_op jit(solution)/shard_map/while/body/eval_jaxpr/vmap()/scatter-add | solution.py:149
  361.9 6.6 copy.301
  368.5 31.7 %scatter_fusion = f32[3,32,64,64]{3,2,1,0:T(8,128)} fusion(f32[3,32,64,64]{3,2,1,0:T(8,128)} %get-tuple-element.522, s32[192]{0:T(256)S(1)} %reshape.495, f32[192,64,64]{2,1,0:T(8,128)} %bitcast.242), kind=kCustom, calls=%fused_computation.4.clone.1 | custom fusion | flops 786432 | bytes 9438720 | tf_op jit(solution)/shard_map/while/body/eval_jaxpr/vmap()/scatter-add | solution.py:148
  409.1 5.0 gather_fusion.2
  429.1 21.6 %scatter_fusion.1 = f32[3,32,64,64]{3,2,1,0:T(8,128)S(1)} fusion(f32[3,32,64,64]{3,2,1,0:T(8,128)S(1)} %copy-done.2, s32[192]{0:T(256)S(1)} %reshape.495, f32[192,64,64]{2,1,0:T(8,128)} %bitcast.241), kind=kCustom, calls=%fused_computation.5.clone.1 | custom fusion | flops 786432 | bytes 9438720 | tf_op jit(solution)/shard_map/while/body/eval_jaxpr/vmap()/scatter-add | solution.py:149
  450.8 6.5 copy.301
  457.3 31.6 %scatter_fusion = f32[3,32,64,64]{3,2,1,0:T(8,128)} fusion(f32[3,32,64,64]{3,2,1,0:T(8,128)} %get-tuple-element.522, s32[192]{0:T(256)S(1)} %reshape.495, f32[192,64,64]{2,1,0:T(8,128)} %bitcast.242), kind=kCustom, calls=%fused_computation.4.clone.1 | custom fusion | flops 786432 | bytes 9438720 | tf_op jit(solution)/shard_map/while/body/eval_jaxpr/vmap()/scatter-add | solution.py:148
  497.8 5.0 gather_fusion.2
  517.9 21.6 %scatter_fusion.1 = f32[3,32,64,64]{3,2,1,0:T(8,128)S(1)} fusion(f32[3,32,64,64]{3,2,1,0:T(8,128)S(1)} %copy-done.2, s32[192]{0:T(256)S(1)} %reshape.495, f32[192,64,64]{2,1,0:T(8,128)} %bitcast.241), kind=kCustom, calls=%fused_computation.5.clone.1 | custom fusion | flops 786432 | bytes 9438720 | tf_op jit(solution)/shard_map/while/body/eval_jaxpr/vmap()/scatter-add | solution.py:149
  539.5 6.5 copy.301
  546.1 31.6 %scatter_fusion = f32[3,32,64,64]{3,2,1,0:T(8,128)} fusion(f32[3,32,64,64]{3,2,1,0:T(8,128)} %get-tuple-element.522, s32[192]{0:T(256)S(1)} %reshape.495, f32[192,64,64]{2,1,0:T(8,128)} %bitcast.242), kind=kCustom, calls=%fused_computation.4.clone.1 | custom fusion | flops 786432 | bytes 9438720 | tf_op jit(solution)/shard_map/while/body/eval_jaxpr/vmap()/scatter-add | solution.py:148
  586.5 5.0 gather_fusion.2
  606.6 21.6 %scatter_fusion.1 = f32[3,32,64,64]{3,2,1,0:T(8,128)S(1)} fusion(f32[3,32,64,64]{3,2,1,0:T(8,128)S(1)} %copy-done.2, s32[192]{0:T(256)S(1)} %reshape.495, f32[192,64,64]{2,1,0:T(8,128)} %bitcast.241), kind=kCustom, calls=%fused_computation.5.clone.1 | custom fusion | flops 786432 | bytes 9438720 | tf_op jit(solution)/shard_map/while/body/eval_jaxpr/vmap()/scatter-add | solution.py:149
  628.3 6.5 copy.301
  634.8 31.6 %scatter_fusion = f32[3,32,64,64]{3,2,1,0:T(8,128)} fusion(f32[3,32,64,64]{3,2,1,0:T(8,128)} %get-tuple-element.522, s32[192]{0:T(256)S(1)} %reshape.495, f32[192,64,64]{2,1,0:T(8,128)} %bitcast.242), kind=kCustom, calls=%fused_computation.4.clone.1 | custom fusion | flops 786432 | bytes 9438720 | tf_op jit(solution)/shard_map/while/body/eval_jaxpr/vmap()/scatter-add | solution.py:148
  673.3 12.7 reduce.9
  687.3 14.1 %all_to_all.135 = bf16[4,2,49152]{2,1,0:T(2,128)(2,1)S(1)} all-to-all(bf16[4,2,49152]{2,1,0:T(2,128)(2,1)S(1)} %reshape.461), channel_id=1, replica_groups=mesh['dp'=8,'seq'=4] {'seq'}, dimensions={0} | all-to-all | bytes 1572864 | tf_op jit(solution)/shard_map/all_to_all | solution.py:309
  716.7 12.7 reduce.8
  730.8 14.2 %all_to_all.136 = bf16[4,2,49152]{2,1,0:T(2,128)(2,1)S(1)} all-to-all(bf16[4,2,49152]{2,1,0:T(2,128)(2,1)S(1)} %reshape.459), channel_id=1, replica_groups=mesh['dp'=8,'seq'=4] {'seq'}, dimensions={0} | all-to-all | bytes 1572864 | tf_op jit(solution)/shard_map/all_to_all | solution.py:312
  760.1 12.7 reduce.10
  774.2 16.2 %all_to_all.137 = bf16[4,2,49152]{2,1,0:T(2,128)(2,1)S(1)} all-to-all(bf16[4,2,49152]{2,1,0:T(2,128)(2,1)S(1)} %reshape.463), channel_id=1, replica_groups=mesh['dp'=8,'seq'=4] {'seq'}, dimensions={0} | all-to-all | bytes 1572864 | tf_op jit(solution)/shard_map/all_to_all | solution.py:315
  802.8 10.2 fusion.53
  814.4 7.2 fusion.59
  823.9 41.2 %all-reduce.10 = (f32[768]{0:T(1024)S(1)}, f32[768]{0:T(1024)S(1)}, f32[768]{0:T(1024)S(1)}, f32[768]{0:T(1024)S(1)}, f32[768]{0:T(1024)S(1)}, /*index=5*/f32[30...) all-reduce(f32[768]{0:T(1024)S(1)} %reduce_sum.184, ...), channel_id=3, replica_groups=mesh['dp'=8,'seq'=4] {'dp','seq'}, use_global_device_ids=true, to_apply=%region_19.20.clone | all-reduce | flops 9216 | bytes 73728
  876.8 40.4 %reduce-scatter.21.cloned.1.call-done = f32[24,768]{1,0:T(8,128)} async-done(((f32[768,768]{1,0:T(8,128)}), f32[24,768]{1,0:T(8,128)}) %reduce-scatter.21.cloned.1.call-update) | async-done | bytes 73744
  917.2 104.6 %reduce-scatter.23.cloned.1.call-done = f32[24,768]{1,0:T(8,128)} async-done(((f32[768,768]{1,0:T(8,128)}), f32[24,768]{1,0:T(8,128)}) %reduce-scatter.23.cloned.1.call-update) | async-done | bytes 73744
  1021.7 140.8 %reduce-scatter.17.cloned.1.call-done = f32[96,768]{1,0:T(8,128)} async-done(((f32[3072,768]{1,0:T(8,128)}), f32[96,768]{1,0:T(8,128)}) %reduce-scatter.17.cloned.1.call-update) | async-done | bytes 294928 | tf_op jit(solution)/shard_map/reduce_scatter | solution.py:349
  1162.5 142.3 %reduce-scatter.15.cloned.1.call-done = f32[24,3072]{1,0:T(8,128)} async-done(((f32[768,3072]{1,0:T(8,128)}), f32[24,3072]{1,0:T(8,128)}) %reduce-scatter.15.cloned.1.call-update) | async-done | bytes 294928 | tf_op jit(solution)/shard_map/reduce_scatter | solution.py:347
  (466 shorter events, 353.0 us)
Async XLA Ops:
  7.2 248.6 %copy-start = (bf16[768,768]{1,0:T(8,128)(2,1)S(1)}, bf16[768,768]{1,0:T(8,128)(2,1)}, u32[]{:S(2)}) copy-start(bf16[768,768]{1,0:T(8,128)(2,1)} %param.32) | copy-start | bytes 3538948
  9.6 6.1 copy-start.13
  9.6 6.1 copy-start.58
  10.8 15.9 %all-to-all-start = ((bf16[512,4,192]{0,2,1:T(8,128)(2,1)}), bf16[512,4,192]{0,2,1:T(8,128)(2,1)S(1)}, u32[]{:S(2)}, u32[]{:S(2)}) async-start(bf16[512,4,192]{0,2,1:T(8,128)(2,1)} %bitcast.19), calls=%async_computation | async-start | bytes 1572864 | tf_op jit(solution)/shard_map/all_to_all | solution.py:246
  22.3 11.5 copy-start.55
  26.7 20.1 %copy-start.48 = (s32[1,32,3,3]{1,0,3,2:T(1,128)S(1)}, s32[1,32,3,3]{1,0,3,2:T(1,128)}, u32[]{:S(2)}) copy-start(s32[1,32,3,3]{1,0,3,2:T(1,128)} %param.26) | copy-start | bytes 3460
  26.7 15.3 %all-to-all-start.2 = ((bf16[512,4,192]{0,2,1:T(8,128)(2,1)}), bf16[512,4,192]{0,2,1:T(8,128)(2,1)S(1)}, u32[]{:S(2)}, u32[]{:S(2)}) async-start(bf16[512,4,192]{0,2,1:T(8,128)(2,1)} %bitcast.259), calls=%async_computation.2 | async-start | bytes 1572864 | tf_op jit(solution)/shard_map/all_to_all | solution.py:248
  41.9 14.5 %copy-start.24 = (bf16[512,4,192]{0,2,1:T(8,128)(2,1)}, bf16[512,4,192]{0,2,1:T(8,128)(2,1)S(1)}, u32[]{:S(2)}) copy-start(bf16[512,4,192]{0,2,1:T(8,128)(2,1)S(1)} %all-to-all-done.2) | copy-start | bytes 2359300
  41.9 26.1 %all-to-all-start.1 = ((bf16[512,4,192]{0,2,1:T(8,128)(2,1)}), bf16[512,4,192]{0,2,1:T(8,128)(2,1)}, u32[]{:S(2)}, u32[]{:S(2)}) async-start(bf16[512,4,192]{0,2,1:T(8,128)(2,1)} %bitcast.258), calls=%async_computation.1 | async-start | bytes 1572864 | tf_op jit(solution)/shard_map/all_to_all | solution.py:247
  225.3 16.3 %all-to-all-start.3 = ((bf16[4,2,49152]{2,1,0:T(2,128)(2,1)}), bf16[4,2,49152]{2,1,0:T(2,128)(2,1)}, u32[]{:S(2)}, u32[]{:S(2)}) async-start(bf16[4,2,49152]{2,1,0:T(2,128)(2,1)} %reshape.457), calls=%async_computation.3 | async-start | bytes 1572864 | tf_op jit(solution)/shard_map/all_to_all | solution.py:258
  251.5 4.3 copy-start.59
  255.8 6.9 slice-start
  256.8 25.9 %copy-start.19 = (f32[512,768]{1,0:T(8,128)}, f32[512,768]{1,0:T(8,128)S(1)}, u32[]{:S(2)}) copy-start(f32[512,768]{1,0:T(8,128)S(1)} %get-tuple-element.350) | copy-start | bytes 4718596
  256.8 25.8 %copy-start.38 = (f32[512]{0:T(512)}, f32[512]{0:T(512)S(1)}, u32[]{:S(2)}) copy-start(f32[512]{0:T(512)S(1)} %broadcast_multiply_fusion.5) | copy-start | bytes 6148
  257.1 25.5 %copy-start.46 = (f32[512]{0:T(512)}, f32[512]{0:T(512)S(1)}, u32[]{:S(2)}) copy-start(f32[512]{0:T(512)S(1)} %add_rsqrt_fusion.1) | copy-start | bytes 6148
  257.1 5.6 slice-start.1
  257.2 5.6 copy-start.56
  257.2 5.6 copy-start.60
  262.8 9.0 copy-start.63
  262.8 4.6 copy-start.40
  269.6 9.4 slice-start.2
  271.8 7.2 copy-start.30
  271.8 7.2 slice-start.3
  285.7 4.7 copy-start.22
  286.9 15.1 %all-to-all-start.4 = ((bf16[512,4,192]{0,2,1:T(8,128)(2,1)}), bf16[512,4,192]{0,2,1:T(8,128)(2,1)S(1)}, u32[]{:S(2)}, u32[]{:S(2)}) async-start(bf16[512,4,192]{0,2,1:T(8,128)(2,1)} %bitcast.261), calls=%async_computation.4 | async-start | bytes 1572864 | tf_op jit(solution)/shard_map/all_to_all | solution.py:289
  290.4 586.4 %reduce-scatter.13.cloned.1.call-start = ((), (), s32[]{:S(2)}) async-start(), calls=%async_computation.14 | async-start | bytes 2433024 | tf_op jit(solution)/shard_map/reduce_scatter | solution.py:343
  294.2 582.6 %reduce-scatter.19.cloned.1.call-start = ((), (), s32[]{:S(2)}) async-start(), calls=%async_computation.17 | async-start | bytes 2433024
  311.2 5.0 copy-start.7
  361.9 6.6 copy-start.3
  368.5 31.7 %copy-start.8 = (bf16[4,3,8,64,64]{4,3,2,1,0:T(8,128)(2,1)S(1)}, bf16[4,3,8,64,64]{4,3,2,1,0:T(8,128)(2,1)}, u32[]{:S(2)}) copy-start(bf16[4,3,8,64,64]{4,3,2,1,0:T(8,128)(2,1)} %copy-done.7) | copy-start | bytes 2359300 | tf_op jit(solution)/shard_map/while
  400.2 5.0 copy-start.7
  425.4 3.7 copy-start.2
  450.8 6.6 copy-start.3
  457.3 31.6 %copy-start.8 = (bf16[4,3,8,64,64]{4,3,2,1,0:T(8,128)(2,1)S(1)}, bf16[4,3,8,64,64]{4,3,2,1,0:T(8,128)(2,1)}, u32[]{:S(2)}) copy-start(bf16[4,3,8,64,64]{4,3,2,1,0:T(8,128)(2,1)} %copy-done.7) | copy-start | bytes 2359300 | tf_op jit(solution)/shard_map/while
  488.9 5.0 copy-start.7
  514.1 3.7 copy-start.2
  539.5 6.6 copy-start.3
  546.1 31.6 %copy-start.8 = (bf16[4,3,8,64,64]{4,3,2,1,0:T(8,128)(2,1)S(1)}, bf16[4,3,8,64,64]{4,3,2,1,0:T(8,128)(2,1)}, u32[]{:S(2)}) copy-start(bf16[4,3,8,64,64]{4,3,2,1,0:T(8,128)(2,1)} %copy-done.7) | copy-start | bytes 2359300 | tf_op jit(solution)/shard_map/while
  577.7 5.0 copy-start.7
  628.2 6.6 copy-start.3
  634.8 31.6 %copy-start.8 = (bf16[4,3,8,64,64]{4,3,2,1,0:T(8,128)(2,1)S(1)}, bf16[4,3,8,64,64]{4,3,2,1,0:T(8,128)(2,1)}, u32[]{:S(2)}) copy-start(bf16[4,3,8,64,64]{4,3,2,1,0:T(8,128)(2,1)} %copy-done.7) | copy-start | bytes 2359300 | tf_op jit(solution)/shard_map/while
  711.2 205.9 %reduce-scatter.21.cloned.1.call-start = ((), (), s32[]{:S(2)}) async-start(), calls=%async_computation.18 | async-start | bytes 2433024
  754.6 267.1 %reduce-scatter.23.cloned.1.call-start = ((), (), s32[]{:S(2)}) async-start(), calls=%async_computation.19 | async-start | bytes 2433024
  801.5 361.1 %reduce-scatter.17.cloned.1.call-start = ((), (), s32[]{:S(2)}) async-start(), calls=%async_computation.16 | async-start | bytes 9732096 | tf_op jit(solution)/shard_map/reduce_scatter | solution.py:349
  813.1 491.8 %reduce-scatter.15.cloned.1.call-start = ((), (), s32[]{:S(2)}) async-start(), calls=%async_computation.15 | async-start | bytes 9732096 | tf_op jit(solution)/shard_map/reduce_scatter | solution.py:347
  821.7 48.7 %copy-start.26 = (bf16[512,4,1,192]{0,3,1,2:T(8,128)(2,1)S(1)}, bf16[512,4,1,192]{0,3,1,2:T(8,128)(2,1)}, u32[]{:S(2)}) copy-start(bf16[512,4,1,192]{0,3,1,2:T(8,128)(2,1)} %copy-done.25) | copy-start | bytes 2359300
  823.7 48.8 %copy-start.28 = (bf16[512,4,1,192]{0,3,1,2:T(8,128)(2,1)S(1)}, bf16[512,4,1,192]{0,3,1,2:T(8,128)(2,1)}, u32[]{:S(2)}) copy-start(bf16[512,4,1,192]{0,3,1,2:T(8,128)(2,1)} %copy-done.27) | copy-start | bytes 2359300
  872.5 432.3 %copy-start.1 = (bf16[768,768]{1,0:T(8,128)(2,1)S(1)}, bf16[768,768]{1,0:T(8,128)(2,1)}, u32[]{:S(2)}) copy-start(bf16[768,768]{1,0:T(8,128)(2,1)} %param.32) | copy-start | bytes 3538948
  (65 other events, 135.7 us)
Sparse Core Ops, SparseCore 0:
  297.1 101.3 reduce-scatter.12
  711.4 101.7 reduce-scatter.18
  819.1 98.0 reduce-scatter.20
  923.8 97.9 reduce-scatter.22
  1028.1 134.4 reduce-scatter.16
  1169.9 134.9 reduce-scatter.14
where the time goes:
time: 1330 us; the launch traced here: 1310 us
  waiting for transfers between devices  460 us (35%)
  other arithmetic  291 us (22%)
  local copies, waits for them, and re-layouts  290 us (22%)
  matrix products  148 us (11%)
  blocking collectives  85.6 us (6%)
  starting transfers between devices  20.6 us (2%)
  between operations  15.9 us (1%)
    unnamed x9, waiting for transfers between devices  145 us
    reduce_scatter x1, waiting for transfers between devices, on_device(): lax.psum_scatter(grad_up_weight, ('dp', 'seq'), scatter_dimension=0, tile...  142 us
    reduce_scatter x1, waiting for transfers between devices, on_device(): lax.psum_scatter(grad_down_weight, ('dp', 'seq'), scatter_dimension=0, ti...  141 us
    scatter-add x8, other arithmetic, backward_head(): keys_total.at[flat_index].add(d_keys.reshape(-1, block_len, head_len))  127 us
    scatter-add x4, other arithmetic, backward_head(): values_total.at[flat_index].add(d_values.reshape(-1, block_len, head_len))  86.6 us
    reshape x4, other arithmetic, join_heads(): tensor.transpose(1, 2, 0, 3)  51.6 us
    unnamed x1, blocking collectives  41.2 us
    gather x8, local copies, waits for them, and re-layouts, gather_keys(): values[index].reshape(group_len, -1, head_len)  40.2 us
  transfers between devices with their start and end apart: 11, of which 8 were waited for; matrix products, arithmetic and copies ran while one was open for 39% of the time, Pallas kernels for 0%

commit v1 on v0

v1 whole, which is shorter than its diff:
```python
import functools

import jax
import jax.numpy as jnp
from jax import lax
from jax.experimental import pallas as pl
from jax.experimental.pallas import tpu as pltpu
from jax.sharding import PartitionSpec as P

HEAD_DIM = 64
BLK = 64
PAIR = 2 * HEAD_DIM
TABLE = 8
NORM_EPS = 1e-05
MASKED = -1e30
SCALE = HEAD_DIM ** (-0.5)
MESH = pl.DeviceIdType.MESH
BF16 = jnp.bfloat16
F32 = jnp.float32
VMEM = pltpu.VMEM
LIMIT = 60 << 20


def whole_vmem():
    return pl.BlockSpec(memory_space=pltpu.VMEM)


def dot(left, right):
    return jnp.dot(left, right, preferred_element_type=F32)


def dot_nt(left, right):
    return lax.dot_general(left, right, (((1,), (1,)), ((), ())), preferred_element_type=F32)


def dot_tn(left, right):
    return lax.dot_general(left, right, (((0,), (0,)), ((), ())), preferred_element_type=F32)


def gather_kernel(
    rows, width, x_ref, tab_ref, wq_ref, qb_ref, wk_ref, wv_ref, vb_ref,
    q_ref, k_ref, v_ref, far_ref, tab_out, land, tab_land, sends, recvs, tab_sends, tab_recvs,
):
    parts = 4
    part = rows // parts
    dp, me = lax.axis_index("dp"), lax.axis_index("seq")
    mate, across, diagonal = (lax.bitwise_xor(me, bit) for bit in (1, 2, 3))
    barrier = pltpu.get_barrier_semaphore()
    for other in (mate, across, diagonal):
        pl.semaphore_signal(barrier, inc=1, device_id=(dp, other), device_id_type=MESH)
    pl.semaphore_wait(barrier, 3)

    def send(src, dst, slot, target):
        copy = pltpu.make_async_remote_copy(
            src_ref=src, dst_ref=dst, send_sem=sends.at[slot], recv_sem=recvs.at[slot],
            device_id=(dp, target), device_id_type=MESH,
        )
        copy.start()
        return copy

    far = [
        send(x_ref.at[pl.ds(r * part, part)], land.at[0, pl.ds(r * part, part)], r, across)
        for r in range(parts)
    ]
    near = send(x_ref, land.at[1], parts, mate)
    tables = []
    own_blocks = tab_ref.shape[0] // 4
    for slot, other in enumerate((mate, across, diagonal)):
        copy = pltpu.make_async_remote_copy(
            src_ref=tab_ref.at[pl.ds(pl.multiple_of(other * own_blocks, 8), own_blocks)],
            dst_ref=tab_land.at[slot], send_sem=tab_sends.at[slot], recv_sem=tab_recvs.at[slot],
            device_id=(dp, other), device_id_type=MESH,
        )
        copy.start()
        tables.append(copy)

    def keys_values(x, at):
        k_ref[pl.ds(at, width), :] = dot(x, wk_ref[...]).astype(BF16)
        v_ref[pl.ds(at, width), :] = (dot(x, wv_ref[...]) + vb_ref[...]).astype(BF16)

    def own(r, _):
        at = pl.multiple_of(r * width, width)
        x = x_ref[pl.ds(at, width), :]
        q_ref[pl.ds(at, width), :] = (
            (dot(x, wq_ref[...]) + qb_ref[...]).astype(BF16) * jnp.asarray(SCALE, BF16)
        )
        keys_values(x, pl.multiple_of(me * rows + at, width))
        return 0

    lax.fori_loop(0, rows // width, own, 0)

    def block(slot, owner, start, count):
        def step(r, _):
            at = pl.multiple_of(start + r * width, width)
            keys_values(land[slot, pl.ds(at, width), :], pl.multiple_of(owner * rows + at, width))
            return 0

        lax.fori_loop(0, count // width, step, 0)

    near.wait()
    block(1, mate, 0, rows)
    relayed = []
    for r in range(parts):
        far[r].wait()
        piece = pl.ds(r * part, part)
        relayed.append(send(land.at[0, piece], land.at[2, piece], parts + 1 + r, mate))
        block(0, across, r * part, part)
        if r:
            relayed[r - 1].wait()
            block(2, diagonal, (r - 1) * part, part)
    far_ref[...] = land[0]
    for copy in tables:
        copy.wait()
    relayed[-1].wait()
    block(2, diagonal, (parts - 1) * part, part)
    tab_out[pl.ds(me, 1)] = tab_ref[pl.ds(pl.multiple_of(me * own_blocks, 8), own_blocks)][None]
    for slot, other in enumerate((mate, across, diagonal)):
        tab_out[pl.ds(other, 1)] = tab_land[slot][None]


def gather_project(tokens, table, query_weight, query_bias, key_weight, value_weight, value_bias):
    rows, features = tokens.shape
    own_blocks = rows // BLK
    copies = 4 + 1 + 4
    return pl.pallas_call(
        functools.partial(gather_kernel, rows, 128),
        out_shape=(
            jax.ShapeDtypeStruct((rows, features), BF16),
            jax.ShapeDtypeStruct((4 * rows, features), BF16),
            jax.ShapeDtypeStruct((4 * rows, features), BF16),
            jax.ShapeDtypeStruct((rows, features), BF16),
            jax.ShapeDtypeStruct((4, own_blocks, 128), jnp.int32),
        ),
        in_specs=[whole_vmem()] * 7,
        out_specs=(whole_vmem(),) * 5,
        scratch_shapes=[
            VMEM((3, rows, features), BF16),
            VMEM((3, own_blocks, 128), jnp.int32),
            pltpu.SemaphoreType.DMA((copies,)),
            pltpu.SemaphoreType.DMA((copies,)),
            pltpu.SemaphoreType.DMA((3,)),
            pltpu.SemaphoreType.DMA((3,)),
        ],
        compiler_params=pltpu.CompilerParams(
            collective_id=0, has_side_effects=True, vmem_limit_bytes=LIMIT
        ),
        name="gather_project",
    )(tokens, table, query_weight, query_bias[None], key_weight, value_weight, value_bias[None])


def picks(tab_ref, filled, pair, i, at, own_blocks, last_row):
    def chosen(head, t):
        group, inner = head // 3, head % 3
        return tab_ref[(group * own_blocks + i) * 128 + inner * 3 + t]

    head = 2 * pair
    both = [(chosen(head, t), chosen(head + 1, t)) for t in range(3)]
    shared = [
        (jnp.maximum(at - 1, 0), (at >= 1) & (at - 1 < filled)),
        (at, at < filled),
        (jnp.minimum(at + 1, last_row), at + 1 < filled),
        (jnp.int32(0), at >= 2),
        (filled - 1, jnp.abs(at - (filled - 1)) > 1),
    ]
    return shared, both


def rows_of(block):
    return pl.ds(pl.multiple_of(block * BLK, BLK), BLK)


def lanes_low(rows):
    return lax.broadcasted_iota(jnp.int32, (rows, PAIR), 1) < HEAD_DIM


def split_pair(x, low):
    zero = jnp.zeros_like(x)
    return jnp.concatenate([jnp.where(low, x, zero), jnp.where(low, zero, x)], axis=0)


def gathered(ref, shared, both, low):
    tiles = [ref[rows_of(b), :] for b, _ in shared]
    for first, second in both:
        tiles.append(jnp.where(low, ref[rows_of(first), :], ref[rows_of(second), :]))
    return jnp.concatenate(tiles, axis=0)


def bias_scores(scores, shared):
    parts = []
    for slot, (_, ok) in enumerate(shared):
        parts.append(scores[slot * BLK:(slot + 1) * BLK] + jnp.where(ok, 0.0, MASKED).astype(F32))
    parts.append(scores[len(shared) * BLK:])
    return jnp.concatenate(parts, axis=0)


def forward_kernel(own_blocks, tab_ref, filled_ref, q_ref, k_ref, v_ref, out_ref, lse_ref):
    pair = pl.program_id(0)
    filled = filled_ref[0]
    first_block = lax.axis_index("seq") * own_blocks
    last_row = k_ref.shape[0] // BLK - 1
    low = lanes_low(BLK)

    def step(i, _):
        at = first_block + i
        shared, both = picks(tab_ref, filled, pair, i, at, own_blocks, last_row)
        keys = gathered(k_ref, shared, both, low)
        values = gathered(v_ref, shared, both, low)
        query = split_pair(q_ref[rows_of(i), :], low)
        scores = bias_scores(dot_nt(keys, query), shared)
        highest = jnp.max(scores, axis=0, keepdims=True)
        weights = jnp.exp(scores - highest)
        total = jnp.sum(weights, axis=0, keepdims=True)
        share = (weights * (1.0 / total)).astype(BF16)
        output = dot_tn(share, values)
        merged = jnp.where(low, output[:BLK], output[BLK:])
        merged = jnp.where(at < filled, merged, 0.0)
        out_ref[rows_of(i), :] = merged.astype(BF16)
        lse_ref[0, pl.ds(i, 1), :] = highest + jnp.log(total)
        return 0

    lax.fori_loop(0, own_blocks, step, 0, unroll=2)


def attention_forward(table, filled, query, keys, values):
    rows, features = query.shape
    own_blocks = rows // BLK
    pairs = features // PAIR
    column = lambda n: pl.BlockSpec((n, PAIR), lambda p, *_: (0, p))
    return pl.pallas_call(
        functools.partial(forward_kernel, own_blocks),
        out_shape=(
            jax.ShapeDtypeStruct((rows, features), BF16),
            jax.ShapeDtypeStruct((pairs, own_blocks, PAIR), F32),
        ),
        grid_spec=pltpu.PrefetchScalarGridSpec(
            num_scalar_prefetch=2,
            grid=(pairs,),
            in_specs=[column(rows), column(keys.shape[0]), column(keys.shape[0])],
            out_specs=(column(rows), pl.BlockSpec((1, own_blocks, PAIR), lambda p, *_: (p, 0, 0))),
        ),
        compiler_params=pltpu.CompilerParams(vmem_limit_bytes=LIMIT),
        name="attention_forward",
    )(table, filled, query, keys, values)


def backward_kernel(
    own_blocks, tab_ref, filled_ref, q_ref, k_ref, v_ref, g_ref, lse_ref,
    dq_ref, dk_ref, dv_ref, dk_sum, dv_sum,
):
    pair = pl.program_id(0)
    filled = filled_ref[0]
    first_block = lax.axis_index("seq") * own_blocks
    last_row = k_ref.shape[0] // BLK - 1
    low = lanes_low(BLK)
    dk_sum[...] = jnp.zeros_like(dk_sum)
    dv_sum[...] = jnp.zeros_like(dv_sum)

    def step(i, _):
        at = first_block + i
        shared, both = picks(tab_ref, filled, pair, i, at, own_blocks, last_row)
        keys = gathered(k_ref, shared, both, low)
        values = gathered(v_ref, shared, both, low)
        query = split_pair(q_ref[rows_of(i), :], low)
        grad = split_pair(jnp.where(at < filled, g_ref[rows_of(i), :], jnp.zeros((), BF16)), low)
        scores = bias_scores(dot_nt(keys, query), shared)
        share = jnp.exp(scores - lse_ref[0, pl.ds(i, 1), :])
        d_share = dot_nt(values, grad)
        centre = jnp.sum(share * d_share, axis=0, keepdims=True)
        d_scores = (share * (d_share - centre)).astype(BF16)
        d_query = dot_tn(d_scores, keys) * SCALE
        dq_ref[rows_of(i), :] = jnp.where(low, d_query[:BLK], d_query[BLK:]).astype(BF16)
        for total, part in ((dk_sum, dot(d_scores, query)), (dv_sum, dot(share.astype(BF16), grad))):
            for slot, (block, _) in enumerate(shared):
                total[rows_of(block), :] += part[slot * BLK:(slot + 1) * BLK]
            for t, (one, two) in enumerate(both):
                tile = part[(5 + t) * BLK:(6 + t) * BLK]
                total[rows_of(one), :] += jnp.where(low, tile, 0.0)
                total[rows_of(two), :] += jnp.where(low, 0.0, tile)
        return 0

    lax.fori_loop(0, own_blocks, step, 0)
    dk_ref[...] = dk_sum[...].astype(BF16)
    dv_ref[...] = dv_sum[...].astype(BF16)


def attention_backward(table, filled, query, keys, values, grad, lse):
    rows, features = query.shape
    slot_rows = keys.shape[0]
    own_blocks = rows // BLK
    pairs = features // PAIR
    column = lambda n: pl.BlockSpec((n, PAIR), lambda p, *_: (0, p))
    return pl.pallas_call(
        functools.partial(backward_kernel, own_blocks),
        out_shape=(
            jax.ShapeDtypeStruct((rows, features), BF16),
            jax.ShapeDtypeStruct((slot_rows, features), BF16),
            jax.ShapeDtypeStruct((slot_rows, features), BF16),
        ),
        grid_spec=pltpu.PrefetchScalarGridSpec(
            num_scalar_prefetch=2,
            grid=(pairs,),
            in_specs=[
                column(rows), column(slot_rows), column(slot_rows), column(rows),
                pl.BlockSpec((1, own_blocks, PAIR), lambda p, *_: (p, 0, 0)),
            ],
            out_specs=(column(rows), column(slot_rows), column(slot_rows)),
            scratch_shapes=[VMEM((slot_rows, PAIR), F32), VMEM((slot_rows, PAIR), F32)],
        ),
        compiler_params=pltpu.CompilerParams(vmem_limit_bytes=LIMIT),
        name="attention_backward",
    )(table, filled, query, keys, values, grad, lse)


def exchange_kernel(
    rows, width, dk_ref, dv_ref, dq_ref, base_ref, wq_ref, wk_ref, wv_ref,
    dx_ref, dko_ref, dvo_ref, dkr_ref, dvr_ref,
    land, out_far, in_far, sends, recvs,
):
    dp, me = lax.axis_index("dp"), lax.axis_index("seq")
    mate, across, diagonal = (lax.bitwise_xor(me, bit) for bit in (1, 2, 3))
    barrier = pltpu.get_barrier_semaphore()
    for other in (mate, across):
        pl.semaphore_signal(barrier, inc=1, device_id=(dp, other), device_id_type=MESH)
    pl.semaphore_wait(barrier, 2)

    def send(src, dst, slot, target):
        copy = pltpu.make_async_remote_copy(
            src_ref=src, dst_ref=dst, send_sem=sends.at[slot], recv_sem=recvs.at[slot],
            device_id=(dp, target), device_id_type=MESH,
        )
        copy.start()
        return copy

    def owned(index):
        return pl.ds(pl.multiple_of(index * rows, rows), rows)

    copies = [
        send(ref.at[owned(owner)], land.at[slot], slot, mate)
        for slot, (ref, owner) in enumerate(
            ((dk_ref, diagonal), (dv_ref, diagonal), (dk_ref, mate), (dv_ref, mate))
        )
    ]

    def summed(ref, owner, slot, to_ref):
        to_ref[...] = (ref[owned(owner), :].astype(F32) + land[slot].astype(F32)).astype(BF16)

    copies[0].wait()
    summed(dk_ref, across, 0, dkr_ref)
    copies[1].wait()
    summed(dv_ref, across, 1, dvr_ref)

    steps = rows // width
    for r in range(steps):
        at = pl.ds(r * width, width)
        out_far[at, :] = (
            dot_nt(dkr_ref[at, :], wk_ref[...]) + dot_nt(dvr_ref[at, :], wv_ref[...])
        ).astype(BF16)
    far = send(out_far, in_far, 4, across)
    copies[2].wait()
    summed(dk_ref, me, 2, dko_ref)
    copies[3].wait()
    summed(dv_ref, me, 3, dvo_ref)

    def one(r, _):
        at = pl.ds(pl.multiple_of(r * width, width), width)
        dx_ref[at, :] = (
            base_ref[at, :]
            + dot_nt(dq_ref[at, :], wq_ref[...])
            + dot_nt(dko_ref[at, :], wk_ref[...])
            + dot_nt(dvo_ref[at, :], wv_ref[...])
        )
        return 0

    lax.fori_loop(0, steps, one, 0)
    far.wait()
    dx_ref[...] += in_far[...].astype(F32)


def exchange(d_keys, d_values, d_query, base, query_weight, key_weight, value_weight):
    rows, features = d_query.shape
    small = jax.ShapeDtypeStruct((rows, features), BF16)
    return pl.pallas_call(
        functools.partial(exchange_kernel, rows, 128),
        out_shape=(jax.ShapeDtypeStruct((rows, features), F32), small, small, small, small),
        in_specs=[whole_vmem()] * 7,
        out_specs=(whole_vmem(),) * 5,
        scratch_shapes=[
            VMEM((4, rows, features), BF16),
            VMEM((rows, features), BF16),
            VMEM((rows, features), BF16),
            pltpu.SemaphoreType.DMA((5,)),
            pltpu.SemaphoreType.DMA((5,)),
        ],
        compiler_params=pltpu.CompilerParams(
            collective_id=1, has_side_effects=True, vmem_limit_bytes=LIMIT
        ),
        name="exchange",
    )(d_keys, d_values, d_query, base, query_weight, key_weight, value_weight)


def reduce_kernel(
    chunks, groups, g_ref, s_ref, out_ref, small_out, work, small, land_c, land_1, land_2, land_z,
    small_c, small_1, small_2, small_z, sends, recvs, z_sends, z_recvs, load_sem,
):
    dp, seq = lax.axis_index("dp"), lax.axis_index("seq")
    x, z = lax.rem(dp, 2), dp // 2
    core, y = lax.rem(seq, 2), seq // 2
    barrier = pltpu.get_barrier_semaphore()
    partners = {
        "core": (dp, lax.bitwise_xor(seq, 1)),
        "y": (dp, lax.bitwise_xor(seq, 2)),
        "x": (lax.bitwise_xor(dp, 1), seq),
    }
    columns = [(lax.rem(z + step, groups) * 2 + x, seq) for step in range(1, groups)]
    for target in list(partners.values()) + columns:
        pl.semaphore_signal(barrier, inc=1, device_id=target, device_id_type=MESH)
    pl.semaphore_wait(barrier, 3 + groups - 1)

    def send(src, dst, one, two, target):
        copy = pltpu.make_async_remote_copy(
            src_ref=src, dst_ref=dst, send_sem=one, recv_sem=two, device_id=target,
            device_id_type=MESH,
        )
        copy.start()
        return copy

    small[...] = s_ref[...]

    def item(k):
        if k == chunks:
            return small, small_c, small_1, small_2, small_z
        return work.at[k], land_c.at[k], land_1.at[k], land_2.at[k], land_z.at[k]

    def axes(k):
        return (("y", y), ("x", x)) if k % 2 == 0 else (("x", x), ("y", y))

    def add(total, part):
        total[...] = (total[...].astype(F32) + part[...].astype(F32)).astype(total.dtype)

    def loop_add(total, part):
        def body(r, _):
            add(total.at[r], part.at[r])
            return 0

        lax.fori_loop(0, total.shape[0], body, 0)

    loads = []
    for k in range(chunks):
        copy = pltpu.make_async_copy(g_ref.at[k], work.at[k], load_sem.at[k])
        copy.start()
        loads.append(copy)

    live = {}

    def start_core(k):
        total, land, _, _, _ = item(k)
        if k < chunks:
            loads[k].wait()
        live[k] = send(total.at[1 - core], land, sends.at[0, k], recvs.at[0, k], partners["core"])

    def end_core(k):
        total, land, land_a, _, _ = item(k)
        live[k].wait()
        (name, at), _ = axes(k)
        mine = total.at[core]
        for half in range(2):
            for other in range(2):
                loop_add(mine.at[half, other], land.at[half, other])
        live[k] = send(mine.at[1 - at], land_a, sends.at[1, k], recvs.at[1, k], partners[name])

    def end_first(k):
        total, _, land_a, land_b, _ = item(k)
        (_, at), (name, then) = axes(k)
        live[k].wait()
        mine = total.at[core, at]
        for half in range(2):
            loop_add(mine.at[half], land_a.at[half])
        live[k] = send(mine.at[1 - then], land_b, sends.at[2, k], recvs.at[2, k], partners[name])

    def end_second(k):
        total, _, _, land_b, land = item(k)
        (_, at), (_, then) = axes(k)
        live[k].wait()
        mine = total.at[core, at, then]
        loop_add(mine, land_b)
        live[k] = [
            send(mine.at[lax.rem(z + step, groups)], land.at[step - 1], z_sends.at[k, step - 1],
                 z_recvs.at[k, step - 1], columns[step - 1])
            for step in range(1, groups)
        ]

    def finish(k):
        total, _, _, _, land = item(k)
        (_, at), (_, then) = axes(k)
        result = total[core, at, then, z].astype(F32)
        for step in range(1, groups):
            live[k][step - 1].wait()
            result = result + land[step - 1].astype(F32)
        if k == chunks:
            small_out[...] = result
        else:
            out_ref[k] = result

    order = [chunks] + list(range(chunks))
    for n, k in enumerate(order[:3]):
        start_core(k)
    for n, k in enumerate(order):
        end_core(k)
        if n + 3 < len(order):
            start_core(order[n + 3])
    for n in range(len(order) + 2):
        if n < len(order):
            end_first(order[n])
        if 0 <= n - 1 < len(order):
            end_second(order[n - 1])
        if 0 <= n - 2 < len(order):
            finish(order[n - 2])


def reduce_scatter(grads, small):
    chunks, rows, features = grads.shape[0], grads.shape[-2], grads.shape[-1]
    groups = grads.shape[4]
    little = small.shape[-2:]
    return pl.pallas_call(
        functools.partial(reduce_kernel, chunks, groups),
        out_shape=(
            jax.ShapeDtypeStruct((chunks, rows, features), F32),
            jax.ShapeDtypeStruct(little, F32),
        ),
        in_specs=[pl.BlockSpec(memory_space=pl.ANY), whole_vmem()],
        out_specs=(whole_vmem(), whole_vmem()),
        scratch_shapes=[
            VMEM(grads.shape, BF16),
            VMEM(small.shape, F32),
            VMEM((chunks,) + grads.shape[2:], BF16),
            VMEM((chunks,) + grads.shape[3:], BF16),
            VMEM((chunks,) + grads.shape[4:], BF16),
            VMEM((chunks, groups - 1, rows, features), BF16),
            VMEM(small.shape[1:], F32),
            VMEM(small.shape[2:], F32),
            VMEM(small.shape[3:], F32),
            VMEM((groups - 1,) + little, F32),
            pltpu.SemaphoreType.DMA((3, chunks + 1)),
            pltpu.SemaphoreType.DMA((3, chunks + 1)),
            pltpu.SemaphoreType.DMA((chunks + 1, groups - 1)),
            pltpu.SemaphoreType.DMA((chunks + 1, groups - 1)),
            pltpu.SemaphoreType.DMA((chunks,)),
        ],
        compiler_params=pltpu.CompilerParams(
            collective_id=2, has_side_effects=True, vmem_limit_bytes=LIMIT
        ),
        name="reduce_scatter",
    )(grads, small)


def summed_on_box(square, up, down, vectors, up_bias, groups):
    features = up.shape[0]
    devices = 8 * groups
    share = features // devices
    wide = up.shape[1] // features
    low = [g.astype(BF16).reshape(devices, share, features) for g in square]
    ups = up.astype(BF16).reshape(devices, share, wide, features)
    downs = down.astype(BF16).reshape(devices, wide * share, features)
    pieces = [
        jnp.concatenate(low[:2], axis=1),
        jnp.concatenate(low[2:], axis=1),
    ]
    for j in range(0, wide, 2):
        pieces.append(jnp.concatenate([ups[:, :, j], ups[:, :, j + 1]], axis=1))
    for j in range(0, wide, 2):
        pieces.append(downs[:, j * share:(j + 2) * share])
    placed = []
    for k, piece in enumerate(pieces):
        piece = piece.reshape(groups, 2, 2, 2, 2 * share, features)
        order = (3, 2, 1, 0, 4, 5) if k % 2 == 0 else (3, 1, 2, 0, 4, 5)
        placed.append(piece.transpose(order))
    grads = jnp.stack(placed)
    count = len(vectors)
    flat = jnp.concatenate(
        [jnp.stack(vectors).reshape(count, devices, share).transpose(1, 0, 2),
         up_bias.reshape(devices, wide, share)], axis=1)
    flat = jnp.pad(flat, ((0, 0), (0, 16 - count - wide), (0, 128 - share)))
    flat = flat.reshape(groups, 2, 2, 2, 16, 128).transpose(3, 2, 1, 0, 4, 5)
    big, little = reduce_scatter(grads, flat)
    out_square = [big[0, :share], big[0, share:], big[1, :share], big[1, share:]]
    out_up = jnp.concatenate(
        [big[2 + j // 2, (j % 2) * share:(j % 2 + 1) * share] for j in range(wide)], axis=1)
    out_down = jnp.concatenate([big[2 + wide // 2 + j] for j in range(wide // 2)], axis=0)
    out_vectors = [little[n, :share] for n in range(count)]
    out_up_bias = little[count:count + wide, :share].reshape(-1)
    return out_square, out_up, out_down, out_vectors, out_up_bias


def summed_anywhere(square, up, down, vectors, up_bias):
    def one(g):
        return lax.psum_scatter(g, ("dp", "seq"), scatter_dimension=0, tiled=True)

    return [one(g) for g in square], one(up), one(down), [one(v) for v in vectors], one(up_bias)


def layer_norm(values, gain, shift):
    center = jnp.mean(values, axis=-1, keepdims=True)
    centered = values - center
    variance = jnp.mean(centered * centered, axis=-1, keepdims=True)
    inv_root = lax.rsqrt(variance + NORM_EPS)
    normed = centered * inv_root
    return (normed * gain + shift, normed, inv_root)


def norm_back(grad_out, normed, inv_root, gain):
    d_normed = grad_out * gain
    grad_in = inv_root * (
        d_normed
        - jnp.mean(d_normed, axis=-1, keepdims=True)
        - normed * jnp.mean(d_normed * normed, axis=-1, keepdims=True)
    )
    return (grad_in, jnp.sum(grad_out * normed, axis=0), jnp.sum(grad_out, axis=0))


def on_device(
    groups,
    tokens, filled_blocks, random_blocks, query_weight, query_bias, key_weight, value_weight,
    value_bias, out_weight, out_bias, attn_gain, attn_shift, up_weight, up_bias, down_weight,
    down_bias, ffn_gain, ffn_shift, cotangent,
):
    row_count, feature_count = tokens.shape
    filled = filled_blocks[0]
    place = lax.axis_index("seq") * row_count + jnp.arange(row_count, dtype=jnp.int32)
    live_tokens = (place < filled * BLK).astype(F32)[:, None]

    table = random_blocks[0].reshape(random_blocks.shape[1], -1)
    table = jnp.pad(table, ((0, 0), (0, 128 - table.shape[1])))
    query, keys, values, far_tokens, table = gather_project(
        tokens, table, query_weight, query_bias, key_weight, value_weight, value_bias
    )
    table = table.reshape(-1)
    merged, lse = attention_forward(table, filled_blocks, query, keys, values)

    attn = dot(merged, out_weight) + out_bias
    first, normed_one, root_one = layer_norm(tokens.astype(F32) + attn, attn_gain, attn_shift)
    first_low = first.astype(BF16)
    hidden = dot(first_low, up_weight) + up_bias
    act, gelu_pull = jax.vjp(jax.nn.gelu, hidden)
    act_low = act.astype(BF16)
    ffn = dot(act_low, down_weight) + down_bias
    result, normed_two, root_two = layer_norm(first + ffn, ffn_gain, ffn_shift)
    grad_result = cotangent.astype(F32) * live_tokens
    d_sum_two, grad_ffn_gain, grad_ffn_shift = norm_back(
        grad_result, normed_two, root_two, ffn_gain
    )
    d_ffn = d_sum_two.astype(BF16)
    grad_down_bias = jnp.sum(d_ffn, axis=0, dtype=F32)
    grad_down_weight = dot_tn(act_low, d_ffn)
    d_act = dot_nt(d_ffn, down_weight)
    d_hidden = gelu_pull(d_act)[0].astype(BF16)
    grad_up_bias = jnp.sum(d_hidden, axis=0, dtype=F32)
    grad_up_weight = dot_tn(first_low, d_hidden)
    d_first = d_sum_two + dot_nt(d_hidden, up_weight)
    d_sum_one, grad_attn_gain, grad_attn_shift = norm_back(d_first, normed_one, root_one, attn_gain)
    d_attn = d_sum_one.astype(BF16)
    grad_out_bias = jnp.sum(d_attn, axis=0, dtype=F32)
    grad_out_weight = dot_tn(merged, d_attn)
    d_merged = dot_nt(d_attn, out_weight).astype(BF16)

    d_query, d_keys, d_values = attention_backward(
        table, filled_blocks, query, keys, values, d_merged, lse
    )
    grad_tokens, dk_own, dv_own, dk_far, dv_far = exchange(
        d_keys, d_values, d_query, d_sum_one, query_weight, key_weight, value_weight
    )
    grad_query_weight = dot_tn(tokens, d_query)
    grad_query_bias = jnp.sum(d_query, axis=0, dtype=F32)
    grad_key_weight = dot_tn(tokens, dk_own) + dot_tn(far_tokens, dk_far)
    grad_value_weight = dot_tn(tokens, dv_own) + dot_tn(far_tokens, dv_far)
    grad_value_bias = jnp.sum(dv_own, axis=0, dtype=F32) + jnp.sum(dv_far, axis=0, dtype=F32)

    square = (grad_query_weight, grad_key_weight, grad_value_weight, grad_out_weight)
    vectors = (
        grad_query_bias, grad_value_bias, grad_out_bias, grad_attn_gain, grad_attn_shift,
        grad_down_bias, grad_ffn_gain, grad_ffn_shift,
    )
    if groups:
        square, up, down, vectors, up_sum = summed_on_box(
            square, grad_up_weight, grad_down_weight, vectors, grad_up_bias, groups)
    else:
        square, up, down, vectors, up_sum = summed_anywhere(
            square, grad_up_weight, grad_down_weight, vectors, grad_up_bias)
    return (
        result.astype(BF16), grad_tokens, square[0], vectors[0], square[1], square[2], vectors[1],
        square[3], vectors[2], vectors[3], vectors[4], up, up_sum, down, vectors[5], vectors[6],
        vectors[7],
    )


def solution(mesh):
    both = P(("dp", "seq"), None)
    line = P(("dp", "seq"))
    placed = (both, P("dp"), P("dp", None, "seq", None)) + (P(),) * 15 + (both,)
    groups = 4 if mesh.shape["dp"] == 8 and mesh.shape["seq"] == 4 else 0
    return jax.shard_map(
        functools.partial(on_device, groups),
        mesh=mesh,
        in_specs=placed,
        out_specs=(
            both, both, both, line, both, both, line, both, line, line, line, both, line, both,
            line, line, line,
        ),
        check_vma=False,
    )
```

time: 1330 us -> 347 us (0.26)
  waiting for transfers between devices: 460 us -> 0 us
  other arithmetic: 291 us -> 21.1 us
  local copies, waits for them, and re-layouts: 290 us -> 55.1 us
  Pallas kernels: 0 us -> 219 us
  matrix products: 148 us -> 43.7 us
  blocking collectives: 85.6 us -> 0 us
  starting transfers between devices: 20.6 us -> 0 us
  between operations: 15.9 us -> 2.18 us
    reduce_scatter x3 -> x0, waiting for transfers between devices: 283 us -> none  [the longest x1 142 us: on_device(): lax.psum_scatter(grad_up_weight, ('dp', 'seq'), scatter_dimension=0, tile...]
    pallas_call x0 -> x5, Pallas kernels: none -> 219 us  [the longest x1 98.7 us: reduce_scatter(): pl.pallas_call(functools.partial(reduce_kernel, chunks, groups), out_shap...]
    scatter-add x12 -> x0, other arithmetic: 213 us -> none  [the longest x8 127 us: backward_head(): keys_total.at[flat_index].add(d_keys.reshape(-1, block_len, head_len))]
    unnamed x9 -> x0, waiting for transfers between devices: 145 us -> none
    dot_general x42 -> x14, matrix products: 133 us -> 43.7 us  [the longest x8 18.7 us: dot_tn(): lax.dot_general(left, right, (((0,), (0,)), ((), ())), preferred_element_...]
    gather x24 -> x0, local copies, waits for them, and re-layouts: 78 us -> none  [the longest x8 40.2 us: gather_keys(): values[index].reshape(group_len, -1, head_len)]
    reshape x22 -> x5, local copies, waits for them, and re-layouts: 67.2 us -> 14.1 us  [the longest x1 9.76 us: summed_on_box(): ups = up.astype(BF16).reshape(devices, share, wide, features)]
    reshape x4 -> x0, other arithmetic: 51.6 us -> none  [join_heads(): tensor.transpose(1, 2, 0, 3)]
  transfers between devices with their start and end apart: 11 -> 0, of which waited for: 8 -> 0; matrix products, arithmetic and copies ran while one was open for 39% -> 0% of each run, Pallas kernels for 0% -> 0%
where the time goes in v1:
time: 347 us; the launch traced here: 341 us
  Pallas kernels  219 us (63%)
  local copies, waits for them, and re-layouts  55.1 us (16%)
  matrix products  43.7 us (13%)
  other arithmetic  21.1 us (6%)
    pallas_call x1, Pallas kernels, reduce_scatter(): pl.pallas_call(functools.partial(reduce_kernel, chunks, groups), out_shap...  98.7 us
    pallas_call x1, Pallas kernels, attention_backward(): pl.pallas_call(functools.partial(backward_kernel, own_blocks), out_shape=...  33.3 us
    pallas_call x1, Pallas kernels, exchange(): pl.pallas_call(functools.partial(exchange_kernel, rows, 128), out_shape=(...  33.1 us
    pallas_call x1, Pallas kernels, gather_project(): pl.pallas_call(functools.partial(gather_kernel, rows, 128), out_shape=(ja...  28 us
    pallas_call x1, Pallas kernels, attention_forward(): pl.pallas_call(functools.partial(forward_kernel, own_blocks), out_shape=(...  26.3 us
    dot_general x8, matrix products, dot_tn(): lax.dot_general(left, right, (((0,), (0,)), ((), ())), preferred_element_...  18.7 us
    dot_general x3, matrix products, dot_nt(): lax.dot_general(left, right, (((1,), (1,)), ((), ())), preferred_element_...  16 us
    unnamed x95, local copies, waits for them, and re-layouts  11.8 us

profile of v1, /device:TPU:0, one launch (start us, length us, event | category | flops | bytes accessed | tf_op | source)
XLA Modules:
  0.0 341.5 jit_solution(7416937759395461271)
XLA Ops:
  1.4 1.3 broadcast_in_dim.4.qb_ref
  2.7 1.3 broadcast_in_dim.5.vb_ref
  5.4 28.0 %gather_project.1 = (bf16[512,768]{1,0:T(8,128)(2,1)}, bf16[2048,768]{1,0:T(8,128)(2,1)}, bf16[2048,768]{1,0:T(8,128)(2,1)}, bf16[512,768]{1,0:T(8,128)(2,1)}, s32[4,8,128]{2,1,0:T(8,128)}) custom-call(bf16[512,768]{1,0:T(8,128)(2,1)} %x_ref.1, s32[32,128]{1,0:T(8,128)} %pad.8.tab_ref, bf16[768,768]{1,0:T(8,128)(2,1)} %wq_ref.3, ...), custom_call_target="tpu_custom_call" | custom-call | tf_op jit(solution)/shard_map/gather_project/pallas_call | solution.py:125
  33.4 26.3 %attention_forward.1 = (bf16[512,768]{1,0:T(8,128)(2,1)}, f32[6,8,128]{2,1,0:T(8,128)}) custom-call(s32[4096]{0:T(1024)} %bitcast.126, s32[1]{0:T(128)S(6)} %copy.87.filled_ref, bf16[512,768]{1,0:T(8,128)(2,1)} %get-tuple-element.35.q_ref, bf16[2048,768]{1,0:T(8,128)(2,1)} %get-tuple-element.36.k_ref, bf16[2048,768]{1,0:T(8,128)(2,1)} %get-tuple-element.37.v_ref), custom_call_target="tpu_custom_call" | custom-call | tf_op jit(solution)/shard_map/attention_forward/pallas_call | solution.py:229
  59.8 2.2 fusion.26
  62.4 2.7 fusion.22
  65.2 4.2 %fusion.27 = (f32[512]{0:T(512)S(1)}, f32[512,768]{1,0:T(8,128)S(1)}) fusion(f32[768]{0:T(1024)S(1)} %copy-done.31, bf16[3072,768]{1,0:T(8,128)(2,1)S(1)} %bitcast.129, f32[512,3072]{1,0:T(8,128)S(1)} %fusion.22, f32[3072]{0:T(1024)S(1)} %copy-done.28, f32[768]{0:T(1024)S(1)} %copy-done.32, f32[768]{0:T(1024)S(1)} %copy-done.25, ...), kind=kOutput, calls=%fused_computation.107 | convolution fusion | flops 2434399744 | bytes 14183424 | tf_op jit(solution)/shard_map/dot_general | solution.py:29
  69.8 1.4 multiply_reduce_fusion
  73.2 3.9 %convert_reduce_fusion.1 = (f32[768]{0:T(1024)}, f32[512,768]{1,0:T(8,128)}, bf16[512,768]{1,0:T(8,128)(2,1)}) fusion(f32[512]{0:T(512)} %get-tuple-element.95, f32[512,768]{1,0:T(8,128)S(1)} %get-tuple-element.91, f32[512]{0:T(512)} %copy-done.17, f32[512]{0:T(512)} %get-tuple-element.96, f32[768]{0:T(1024)} %param.35, f32[512]{0:T(512)} %copy-done.18, ...), kind=kLoop, calls=%fused_computation.28 | loop fusion | flops 5897472 | bytes 4738048 | tf_op jit(solution)/shard_map/reduce_sum | solution.py:652
  77.1 1.4 stack.57
  78.4 10.6 %convert_reduce_fusion = (f32[3072]{0:T(1024)}, bf16[512,3072]{1,0:T(8,128)(2,1)S(1)}) fusion(f32[512,3072]{1,0:T(8,128)} %copy-done.34, f32[3072]{0:T(1024)} %param.32, bf16[3072,768]{1,0:T(8,128)(2,1)} %param.33, f32[512,768]{1,0:T(8,128)} %get-tuple-element.60), kind=kOutput, calls=%fused_computation.9 | convolution fusion | flops 2452485120 | bytes 15753216 | tf_op jit(solution)/shard_map/dot_general | solution.py:33
  89.0 6.7 %convolution_convert_fusion = bf16[3072,768]{1,0:T(8,128)(2,1)S(1)} fusion(f32[512,768]{1,0:T(8,128)S(1)} %copy-done.14, f32[512,3072]{1,0:T(8,128)} %copy-done.34, f32[3072]{0:T(1024)S(1)} %copy-done.29), kind=kOutput, calls=%fused_computation.11 | convolution fusion | flops 2434400256 | bytes 12595200 | tf_op jit(solution)/shard_map/dot_general | solution.py:37
  95.7 2.5 fusion.24
  98.2 3.6 %multiply_reduce_fusion.1 = (f32[768]{0:T(1024)}, f32[512]{0:T(512)S(1)}, f32[512]{0:T(512)S(1)}, f32[768]{0:T(1024)}, f32[512,768]{1,0:T(8,128)S(1)}) fusion(f32[512,768]{1,0:T(8,128)S(1)} %copy-done.6, f32[512]{0:T(512)S(1)} %copy-done.24, f32[512]{0:T(512)S(1)} %copy-done.21, f32[768]{0:T(1024)S(1)} %copy-done.26, f32[512,768]{1,0:T(8,128)S(1)} %copy-done.14, ...), kind=kOutput, calls=%fused_computation.29 | convolution fusion | flops 2419848704 | bytes 12600320 | tf_op jit(solution)/shard_map/dot_general | solution.py:33
  101.9 1.1 convert_reduce_fusion.2
  103.0 4.9 %convolution_convert_fusion.1 = bf16[768,3072]{1,0:T(8,128)(2,1)} fusion(bf16[512,3072]{1,0:T(8,128)(2,1)S(1)} %get-tuple-element.94, f32[512,768]{1,0:T(8,128)S(1)} %copy-done.6, f32[768]{0:T(1024)S(1)} %copy-done.33, f32[768]{0:T(1024)S(1)} %copy-done.26, f32[512]{0:T(512)S(1)} %copy-done.24, f32[512]{0:T(512)S(1)} %copy-done.21), kind=kOutput, calls=%fused_computation.12 | convolution fusion | flops 2420244480 | bytes 9447424 | tf_op jit(solution)/shard_map/dot_general | solution.py:37
  107.9 9.8 %reshape.174 = bf16[32,24,4,768]{3,2,1,0:T(4,128)(2,1)} reshape(bf16[768,3072]{1,0:T(8,128)(2,1)} %convolution_convert_fusion.1) | data formatting | bytes 9437184 | tf_op jit(solution)/shard_map/reshape | solution.py:562
  117.6 1.4 stack.54
  119.0 1.4 stack.55
  120.4 1.4 stack.56
  121.7 1.5 reshape.178
  123.2 1.5 copy.52
  124.7 3.0 convolution_convert_fusion.2
  127.7 1.8 convolution_convert_fusion.4.g_ref
  129.4 33.3 %attention_backward.1 = (bf16[512,768]{1,0:T(8,128)(2,1)}, bf16[2048,768]{1,0:T(8,128)(2,1)}, bf16[2048,768]{1,0:T(8,128)(2,1)}) custom-call(s32[4096]{0:T(1024)} %bitcast.127, s32[1]{0:T(128)S(6)} %copy.87.filled_ref, bf16[512,768]{1,0:T(8,128)(2,1)} %get-tuple-element.35.q_ref, bf16[2048,768]{1,0:T(8,128)(2,1)} %get-tuple-element.36.k_ref, ...), custom_call_target="tpu_custom_call" | custom-call | tf_op jit(solution)/shard_map/attention_backward/pallas_call | solution.py:292
  162.8 33.1 %exchange.1 = (f32[512,768]{1,0:T(8,128)}, bf16[512,768]{1,0:T(8,128)(2,1)}, bf16[512,768]{1,0:T(8,128)(2,1)}, bf16[512,768]{1,0:T(8,128)(2,1)}, bf16[512,768]{1,0:T(8,128)(2,1)}) custom-call(bf16[2048,768]{1,0:T(8,128)(2,1)} %get-tuple-element.40.dk_ref, bf16[2048,768]{1,0:T(8,128)(2,1)} %get-tuple-element.41.dv_ref, ...), custom_call_target="tpu_custom_call" | custom-call | tf_op jit(solution)/shard_map/exchange/pallas_call | solution.py:382
  195.8 1.3 convert_reduce_fusion.4
  197.1 1.3 convert_reduce_fusion.3
  199.8 1.4 stack.53
  201.2 1.4 add.128
  207.6 0.9 select_maximum_fusion
  208.5 0.9 copy.73
  211.6 0.9 fusion.7
  214.0 0.9 fusion.8
  214.9 6.9 %fusion.25 = (bf16[32,24,1,768]{3,2,1,0:T(2,128)(2,1)S(1)}, bf16[32,24,1,768]{3,2,1,0:T(2,128)(2,1)S(1)}, bf16[32,24,1,768]{3,2,1,0:T(2,128)(2,1)S(1)}, bf16[32,24,1,768]{3,2,1,0:T(2,128)(2,1)S(1)}) fusion(bf16[32,24,4,768]{3,2,1,0:T(4,128)(2,1)S(1)} %bitcast.111), kind=kLoop, calls=%fused_computation.105 | loop fusion | bytes 9437184 | tf_op jit(solution)/shard_map/slice | solution.py:569
  222.6 1.6 bitcast_dynamic-update-slice_fusion.5
  224.2 1.6 bitcast_dynamic-update-slice_fusion.4
  225.8 1.6 bitcast_dynamic-update-slice_fusion.3
  227.5 1.7 bitcast_dynamic-update-slice_fusion.2
  229.2 0.8 copy-done.3
  230.0 1.6 bitcast_dynamic-update-slice_fusion.1
  231.6 0.9 copy-done.2
  232.5 1.7 bitcast_dynamic-update-slice_fusion.g_ref
  234.2 98.7 %reduce_scatter.1 = (f32[6,48,768]{2,1,0:T(8,128)}, f32[16,128]{1,0:T(8,128)}) custom-call(bf16[6,2,2,2,4,48,768]{6,5,4,3,2,1,0:T(8,128)(2,1)} %bitcast_dynamic-update-slice_fusion.g_ref, f32[2,2,2,4,16,128]{5,4,3,2,1,0:T(8,128)} %bitcast.123), custom_call_target="tpu_custom_call" | custom-call | tf_op jit(solution)/shard_map/reduce_scatter/pallas_call | solution.py:524
  333.7 1.5 slice_bitcast_fusion.10
  335.8 1.0 slice_bitcast_fusion.1
  336.8 1.9 slice_bitcast_fusion.5
  340.1 1.1 copy.88
  (120 shorter events, 18.1 us)
Async XLA Ops:
  0.7 59.0 %copy-start = (bf16[768,768]{1,0:T(8,128)(2,1)S(1)}, bf16[768,768]{1,0:T(8,128)(2,1)}, u32[]{:S(2)}) copy-start(bf16[768,768]{1,0:T(8,128)(2,1)} %param.27) | copy-start | bytes 3538948
  1.4 68.3 %copy-start.18 = (f32[512]{0:T(512)}, f32[512]{0:T(512)S(1)}, u32[]{:S(2)}) copy-start(f32[512]{0:T(512)S(1)} %fusion.13) | copy-start | bytes 6148
  33.4 26.3 %copy-start.4 = (bf16[512,768]{1,0:T(8,128)(2,1)S(1)}, bf16[512,768]{1,0:T(8,128)(2,1)}, u32[]{:S(2)}) copy-start(bf16[512,768]{1,0:T(8,128)(2,1)} %x_ref.1) | copy-start | bytes 2359300
  33.4 26.3 %copy-start.30 = (f32[768]{0:T(1024)S(1)}, f32[768]{0:T(1024)}, u32[]{:S(2)}) copy-start(f32[768]{0:T(1024)} %param.28) | copy-start | bytes 9220
  59.7 2.6 copy-start.25
  59.7 2.6 copy-start.27
  59.8 2.6 copy-start.32
  61.9 3.2 copy-start.5
  61.9 3.2 copy-start.20
  62.0 3.2 slice-start.2
  62.3 2.8 copy-start.23
  62.3 2.8 slice-start.3
  62.3 2.8 copy-start.28
  62.3 2.8 copy-start.31
  65.2 4.2 %copy-start.34 = (f32[512,3072]{1,0:T(8,128)}, f32[512,3072]{1,0:T(8,128)S(1)}, u32[]{:S(2)}) copy-start(f32[512,3072]{1,0:T(8,128)S(1)} %fusion.22) | copy-start | bytes 18874372
  65.2 4.5 %copy-start.12 = (bf16[512,768]{1,0:T(8,128)(2,1)S(1)}, bf16[512,768]{1,0:T(8,128)(2,1)}, u32[]{:S(2)}) copy-start(bf16[512,768]{1,0:T(8,128)(2,1)} %param.37) | copy-start | bytes 2359300
  65.2 4.5 %copy-start.22 = (f32[768]{0:T(1024)S(1)}, f32[768]{0:T(1024)}, u32[]{:S(2)}) copy-start(f32[768]{0:T(1024)} %param.35) | copy-start | bytes 9220
  69.4 1.7 copy-start.17
  69.7 1.4 copy-start.19
  78.4 10.6 %copy-start.14 = (f32[512,768]{1,0:T(8,128)S(1)}, f32[512,768]{1,0:T(8,128)}, u32[]{:S(2)}) copy-start(f32[512,768]{1,0:T(8,128)} %get-tuple-element.60) | copy-start | bytes 4718596
  78.4 10.6 %copy-start.29 = (f32[3072]{0:T(1024)S(1)}, f32[3072]{0:T(1024)}, u32[]{:S(2)}) copy-start(f32[3072]{0:T(1024)} %param.32) | copy-start | bytes 36868
  78.4 19.7 %slice-start.4 = ((s8[4718592]{0:T(1024)(128)(4,1)}), s8[4194304]{0:T(1024)(128)(4,1)S(1)}, s32[]{:S(2)}) async-start(s8[4718592]{0:T(1024)(128)(4,1)} %bitcast.130), calls=%async_computation.4 | async-start | bytes 8388608
  89.0 9.2 %slice-start.5 = ((s8[4718592]{0:T(1024)(128)(4,1)}), s8[524288]{0:T(1024)(128)(4,1)S(1)}, s32[]{:S(2)}) async-start(s8[4718592]{0:T(1024)(128)(4,1)} %bitcast.130), calls=%async_computation.5 | async-start | bytes 1048576
  95.7 2.5 copy-start.6
  95.7 2.5 copy-start.21
  95.7 2.5 copy-start.24
  95.7 2.5 copy-start.26
  101.9 1.1 copy-start.33
  103.0 24.7 %copy-start.1 = (f32[512,768]{1,0:T(8,128)}, f32[512,768]{1,0:T(8,128)S(1)}, u32[]{:S(2)}) copy-start(f32[512,768]{1,0:T(8,128)S(1)} %get-tuple-element.62.base_ref) | copy-start | bytes 4718596
  162.8 36.3 %copy-start.10 = (bf16[512,768]{1,0:T(8,128)(2,1)S(1)}, bf16[512,768]{1,0:T(8,128)(2,1)}, u32[]{:S(2)}) copy-start(bf16[512,768]{1,0:T(8,128)(2,1)} %get-tuple-element.42.dq_ref) | copy-start | bytes 2359300
  199.7 10.4 %copy-start.7 = (bf16[512,768]{1,0:T(8,128)(2,1)S(1)}, bf16[512,768]{1,0:T(8,128)(2,1)}, u32[]{:S(2)}) copy-start(bf16[512,768]{1,0:T(8,128)(2,1)} %get-tuple-element.47) | copy-start | bytes 2359300
  210.2 1.1 copy-start.9
  210.2 1.4 copy-start.11
  211.5 1.1 copy-start.13
  212.4 2.5 slice-start
  212.7 1.3 copy-start.16
  212.7 2.3 slice-start.1
  222.6 1.6 copy-start.8
  227.5 2.5 copy-start.3
  230.0 2.5 copy-start.2
  332.9 7.2 %copy-start.15 = (f32[512,768]{1,0:T(8,128)S(1)}, f32[512,768]{1,0:T(8,128)}, u32[]{:S(2)}) copy-start(f32[512,768]{1,0:T(8,128)} %get-tuple-element.115) | copy-start | bytes 4718596

commit v2 on v1

--- a/solution.py
+++ b/solution.py
@@ -148,19 +148,15 @@
     )(tokens, table, query_weight, query_bias[None], key_weight, value_weight, value_bias[None])
 
 
-def picks(tab_ref, filled, pair, i, at, own_blocks, last_row):
+def key_blocks(tab_ref, end, pair, i, at, own_blocks, last_row):
     def chosen(head, t):
-        group, inner = head // 3, head % 3
+        group, inner = lax.div(head, 3), lax.rem(head, 3)
         return tab_ref[(group * own_blocks + i) * 128 + inner * 3 + t]
 
     head = 2 * pair
     both = [(chosen(head, t), chosen(head + 1, t)) for t in range(3)]
     shared = [
-        (jnp.maximum(at - 1, 0), (at >= 1) & (at - 1 < filled)),
-        (at, at < filled),
-        (jnp.minimum(at + 1, last_row), at + 1 < filled),
-        (jnp.int32(0), at >= 2),
-        (filled - 1, jnp.abs(at - (filled - 1)) > 1),
+        jnp.maximum(at - 1, 0), at, jnp.minimum(at + 1, last_row), jnp.int32(0), end,
     ]
     return shared, both
 
@@ -178,35 +174,32 @@
     return jnp.concatenate([jnp.where(low, x, zero), jnp.where(low, zero, x)], axis=0)
 
 
-def gathered(ref, shared, both, low):
-    tiles = [ref[rows_of(b), :] for b, _ in shared]
+def gathered(ref, shared, both, low, lanes=slice(None)):
+    tiles = [ref[b, :, lanes] for b in shared]
     for first, second in both:
-        tiles.append(jnp.where(low, ref[rows_of(first), :], ref[rows_of(second), :]))
+        tiles.append(jnp.where(low, ref[first, :, lanes], ref[second, :, lanes]))
     return jnp.concatenate(tiles, axis=0)
 
 
-def bias_scores(scores, shared):
-    parts = []
-    for slot, (_, ok) in enumerate(shared):
-        parts.append(scores[slot * BLK:(slot + 1) * BLK] + jnp.where(ok, 0.0, MASKED).astype(F32))
-    parts.append(scores[len(shared) * BLK:])
-    return jnp.concatenate(parts, axis=0)
-
-
-def forward_kernel(own_blocks, tab_ref, filled_ref, q_ref, k_ref, v_ref, out_ref, lse_ref):
+def masked_scores(scores, mask_ref, i):
+    parts = [scores[n * BLK:(n + 1) * BLK] + mask_ref[i * 8 + n] for n in range(5)]
+    return jnp.concatenate(parts + [scores[5 * BLK:]], axis=0)
+
+
+def forward_kernel(own_blocks, tab_ref, filled_ref, mask_ref, q_ref, k_ref, v_ref, out_ref, lse_ref):
     pair = pl.program_id(0)
     filled = filled_ref[0]
     first_block = lax.axis_index("seq") * own_blocks
-    last_row = k_ref.shape[0] // BLK - 1
+    last_row = k_ref.shape[0] - 1
     low = lanes_low(BLK)
 
     def step(i, _):
         at = first_block + i
-        shared, both = picks(tab_ref, filled, pair, i, at, own_blocks, last_row)
+        shared, both = key_blocks(tab_ref, filled - 1, pair, i, at, own_blocks, last_row)
         keys = gathered(k_ref, shared, both, low)
         values = gathered(v_ref, shared, both, low)
         query = split_pair(q_ref[rows_of(i), :], low)
-        scores = bias_scores(dot_nt(keys, query), shared)
+        scores = masked_scores(dot_nt(keys, query), mask_ref, i)
         highest = jnp.max(scores, axis=0, keepdims=True)
         weights = jnp.exp(scores - highest)
         total = jnp.sum(weights, axis=0, keepdims=True)
@@ -218,14 +211,16 @@
         lse_ref[0, pl.ds(i, 1), :] = highest + jnp.log(total)
         return 0
 
-    lax.fori_loop(0, own_blocks, step, 0, unroll=2)
-
-
-def attention_forward(table, filled, query, keys, values):
+    lax.fori_loop(0, own_blocks, step, 0, unroll=own_blocks)
+
+
+def attention_forward(table, filled, mask, query, keys, values):
     rows, features = query.shape
     own_blocks = rows // BLK
+    slot_blocks = keys.shape[0]
     pairs = features // PAIR
     column = lambda n: pl.BlockSpec((n, PAIR), lambda p, *_: (0, p))
+    blocks = lambda n: pl.BlockSpec((n, BLK, PAIR), lambda p, *_: (0, 0, p))
     return pl.pallas_call(
         functools.partial(forward_kernel, own_blocks),
         out_shape=(
@@ -233,36 +228,36 @@
             jax.ShapeDtypeStruct((pairs, own_blocks, PAIR), F32),
         ),
         grid_spec=pltpu.PrefetchScalarGridSpec(
-            num_scalar_prefetch=2,
+            num_scalar_prefetch=3,
             grid=(pairs,),
-            in_specs=[column(rows), column(keys.shape[0]), column(keys.shape[0])],
+            in_specs=[column(rows), blocks(slot_blocks), blocks(slot_blocks)],
             out_specs=(column(rows), pl.BlockSpec((1, own_blocks, PAIR), lambda p, *_: (p, 0, 0))),
         ),
         compiler_params=pltpu.CompilerParams(vmem_limit_bytes=LIMIT),
         name="attention_forward",
-    )(table, filled, query, keys, values)
+    )(table, filled, mask, query, keys, values)
 
 
 def backward_kernel(
-    own_blocks, tab_ref, filled_ref, q_ref, k_ref, v_ref, g_ref, lse_ref,
+    own_blocks, tab_ref, filled_ref, mask_ref, q_ref, k_ref, v_ref, g_ref, lse_ref,
     dq_ref, dk_ref, dv_ref, dk_sum, dv_sum,
 ):
     pair = pl.program_id(0)
     filled = filled_ref[0]
     first_block = lax.axis_index("seq") * own_blocks
-    last_row = k_ref.shape[0] // BLK - 1
+    last_row = k_ref.shape[0] - 1
     low = lanes_low(BLK)
     dk_sum[...] = jnp.zeros_like(dk_sum)
     dv_sum[...] = jnp.zeros_like(dv_sum)
 
     def step(i, _):
         at = first_block + i
-        shared, both = picks(tab_ref, filled, pair, i, at, own_blocks, last_row)
+        shared, both = key_blocks(tab_ref, filled - 1, pair, i, at, own_blocks, last_row)
         keys = gathered(k_ref, shared, both, low)
         values = gathered(v_ref, shared, both, low)
         query = split_pair(q_ref[rows_of(i), :], low)
         grad = split_pair(jnp.where(at < filled, g_ref[rows_of(i), :], jnp.zeros((), BF16)), low)
-        scores = bias_scores(dot_nt(keys, query), shared)
+        scores = masked_scores(dot_nt(keys, query), mask_ref, i)
         share = jnp.exp(scores - lse_ref[0, pl.ds(i, 1), :])
         d_share = dot_nt(values, grad)
         centre = jnp.sum(share * d_share, axis=0, keepdims=True)
@@ -270,7 +265,7 @@
         d_query = dot_tn(d_scores, keys) * SCALE
         dq_ref[rows_of(i), :] = jnp.where(low, d_query[:BLK], d_query[BLK:]).astype(BF16)
         for total, part in ((dk_sum, dot(d_scores, query)), (dv_sum, dot(share.astype(BF16), grad))):
-            for slot, (block, _) in enumerate(shared):
+            for slot, block in enumerate(shared):
                 total[rows_of(block), :] += part[slot * BLK:(slot + 1) * BLK]
             for t, (one, two) in enumerate(both):
                 tile = part[(5 + t) * BLK:(6 + t) * BLK]
@@ -278,16 +273,18 @@
                 total[rows_of(two), :] += jnp.where(low, 0.0, tile)
         return 0
 
-    lax.fori_loop(0, own_blocks, step, 0)
+    lax.fori_loop(0, own_blocks, step, 0, unroll=own_blocks)
     dk_ref[...] = dk_sum[...].astype(BF16)
     dv_ref[...] = dv_sum[...].astype(BF16)
 
 
-def attention_backward(table, filled, query, keys, values, grad, lse):
+def attention_backward(table, filled, mask, query, keys, values, grad, lse):
     rows, features = query.shape
-    slot_rows = keys.shape[0]
+    slot_blocks = keys.shape[0]
+    slot_rows = slot_blocks * BLK
     own_blocks = rows // BLK
     pairs = features // PAIR
+    blocks = lambda n: pl.BlockSpec((n, BLK, PAIR), lambda p, *_: (0, 0, p))
     column = lambda n: pl.BlockSpec((n, PAIR), lambda p, *_: (0, p))
     return pl.pallas_call(
         functools.partial(backward_kernel, own_blocks),
@@ -297,10 +294,10 @@
             jax.ShapeDtypeStruct((slot_rows, features), BF16),
         ),
         grid_spec=pltpu.PrefetchScalarGridSpec(
-            num_scalar_prefetch=2,
+            num_scalar_prefetch=3,
             grid=(pairs,),
             in_specs=[
-                column(rows), column(slot_rows), column(slot_rows), column(rows),
+                column(rows), blocks(slot_blocks), blocks(slot_blocks), column(rows),
                 pl.BlockSpec((1, own_blocks, PAIR), lambda p, *_: (p, 0, 0)),
             ],
             out_specs=(column(rows), column(slot_rows), column(slot_rows)),
@@ -308,7 +305,7 @@
         ),
         compiler_params=pltpu.CompilerParams(vmem_limit_bytes=LIMIT),
         name="attention_backward",
-    )(table, filled, query, keys, values, grad, lse)
+    )(table, filled, mask, query, keys, values, grad, lse)
 
 
 def exchange_kernel(
@@ -398,204 +395,678 @@
     )(d_keys, d_values, d_query, base, query_weight, key_weight, value_weight)
 
 
-def reduce_kernel(
-    chunks, groups, g_ref, s_ref, out_ref, small_out, work, small, land_c, land_1, land_2, land_z,
-    small_c, small_1, small_2, small_z, sends, recvs, z_sends, z_recvs, load_sem,
+def summed_anywhere(square, up, down, vectors, up_bias):
+    def one(g):
+        return lax.psum_scatter(g, ("dp", "seq"), scatter_dimension=0, tiled=True)
+
+    return [one(g) for g in square], one(up), one(down), [one(v) for v in vectors], one(up_bias)
+
+
+GELU_A = 0.044715
+GELU_C = 0.7978845608028654
+
+
+def normed_rows(values):
+    center = jnp.mean(values, axis=-1, keepdims=True)
+    centered = values - center
+    variance = jnp.mean(centered * centered, axis=-1, keepdims=True)
+    inv_root = lax.rsqrt(variance + NORM_EPS)
+    return centered * inv_root, inv_root
+
+
+def norm_pull(grad_out, normed, inv_root, gain):
+    d_normed = grad_out * gain
+    return inv_root * (
+        d_normed
+        - jnp.mean(d_normed, axis=-1, keepdims=True)
+        - normed * jnp.mean(d_normed * normed, axis=-1, keepdims=True)
+    )
+
+
+def column_sum(values):
+    return jnp.sum(values, axis=0, keepdims=True)
+
+
+def dense_kernel(
+    rows, tile, filled_ref, x_ref, merged_ref, cot_ref, bo_ref, g1_ref, s1_ref, bu_ref, bd_ref,
+    g2_ref, s2_ref, wo_any, wu_any, wd_any,
+    result_ref, base_ref, d_attn_ref, d_merged_ref, vec_ref, up_vec_ref, sum_ref,
+    wo, wu, wd, normed_one, root_one, first, first_low, act, slope, ffn, d_ffn, tmp,
+    down, up, down_in, up_in, loads, sends, recvs,
 ):
+    features = x_ref.shape[1]
+    wide = wu.shape[1] // features
+    share = 24 * wide
+    dp, seq = lax.axis_index("dp"), lax.axis_index("seq")
+    core = lax.rem(seq, 2)
+    mate = lax.bitwise_xor(seq, 1)
+    copies = []
+    for n, (src, dst) in enumerate(((wo_any, wo), (wu_any, wu), (wd_any, wd))):
+        copy = pltpu.make_async_copy(src, dst, loads.at[n])
+        copy.start()
+        copies.append(copy)
+    barrier = pltpu.get_barrier_semaphore()
+    pl.semaphore_signal(barrier, inc=1, device_id=(dp, mate), device_id_type=MESH)
+    pl.semaphore_wait(barrier, 1)
+
+    def send(src, dst, slot):
+        copy = pltpu.make_async_remote_copy(
+            src_ref=src, dst_ref=dst, send_sem=sends.at[slot], recv_sem=recvs.at[slot],
+            device_id=(dp, mate), device_id_type=MESH,
+        )
+        copy.start()
+        return copy
+
+    def tiles(body):
+        def step(r, _):
+            body(pl.ds(pl.multiple_of(r * tile, tile), tile), r)
+            return 0
+
+        lax.fori_loop(0, rows // tile, step, 0)
+
+    def columns(j):
+        return pl.ds(pl.multiple_of(j * features, features), features)
+
+    copies[0].wait()
+    ffn[...] = dot(merged_ref[...], wo[...])
+
+    def norm_one(at, r):
+        normed, inv_root = normed_rows(x_ref[at, :].astype(F32) + (ffn[at, :] + bo_ref[...]))
+        normed_one[at, :] = normed
+        root_one[at, :] = inv_root
+        value = normed * g1_ref[...] + s1_ref[...]
+        first[at, :] = value
+        first_low[at, :] = value.astype(BF16)
+
+    tiles(norm_one)
+
+    copies[1].wait()
+    copies[2].wait()
+    ffn[...] = jnp.zeros_like(ffn)
+
+    def forward(j, _):
+        at = columns(j)
+        u = dot(first_low[...], wu[:, at]) + bu_ref[:, at]
+        square = u * u
+        t = jnp.tanh(GELU_C * (u + GELU_A * (square * u)))
+        half = 0.5 * (1.0 + t)
+        act[j] = (u * half).astype(BF16)
+        slope[j] = half + (0.5 * GELU_C) * u * (1.0 - t * t) * (1.0 + (3.0 * GELU_A) * square)
+        ffn[...] += dot(act[j], wd[columns(j), :])
+        return 0
+
+    lax.fori_loop(0, wide, forward, 0)
+
+    vec_ref[...] = jnp.zeros_like(vec_ref)
+    limit = filled_ref[0] * BLK - seq * rows
+
+    def norm_two(at, r):
+        normed, inv_root = normed_rows(first[at, :] + (ffn[at, :] + bd_ref[...]))
+        result_ref[at, :] = (normed * g2_ref[...] + s2_ref[...]).astype(BF16)
+        place = lax.broadcasted_iota(jnp.int32, (tile, 1), 0) + r * tile
+        grad = cot_ref[at, :].astype(F32) * (place < limit).astype(F32)
+        pulled = norm_pull(grad, normed, inv_root, g2_ref[...])
+        low = pulled.astype(BF16)
+        ffn[at, :] = pulled
+        d_ffn[at, :] = low
+        vec_ref[0:1, :] += column_sum(grad * normed)
+        vec_ref[1:2, :] += column_sum(grad)
+        vec_ref[2:3, :] += column_sum(low.astype(F32))
+
+    tiles(norm_two)
+
+    moving = []
+    for j in range(wide):
+        grad = dot_tn(act[j], d_ffn[...]).astype(BF16)
+        for n in range(8):
+            down[n % 2, j, n // 4, (n // 2) % 2] = grad[n * share:(n + 1) * share]
+        moving.append(send(down.at[1 - core, j], down_in.at[j], j))
+
+    def backward(j, _):
+        d_hidden = (dot_nt(d_ffn[...], wd[columns(j), :]) * slope[j]).astype(BF16)
+        act[j] = d_hidden
+        up_vec_ref[:, columns(j)] = column_sum(d_hidden.astype(F32))
+        return 0
+
+    lax.fori_loop(0, wide, backward, 0)
+
+    for half in range(wide // 2):
+        for part in range(2):
+            tmp[part] = dot_tn(first_low[...], act[2 * half + part])
+
+        def regroup(s, _):
+            for n in range(2):
+                at = pl.ds(pl.multiple_of((2 * s + n) * 24, 8), 24)
+                up[n, half, s] = jnp.concatenate([tmp[0, at, :], tmp[1, at, :]], axis=0).astype(BF16)
+            return 0
+
+        lax.fori_loop(0, up.shape[2], regroup, 0)
+        moving.append(send(up.at[1 - core, half], up_in.at[half], wide + half))
+
+    for j in range(wide):
+        ffn[...] += dot_nt(act[j], wu[:, j * features:(j + 1) * features])
+
+    def pull_one(at, r):
+        grad = ffn[at, :]
+        normed = normed_one[at, :]
+        pulled = norm_pull(grad, normed, root_one[at, :], g1_ref[...])
+        low = pulled.astype(BF16)
+        base_ref[at, :] = pulled
+        d_attn_ref[at, :] = low
+        vec_ref[3:4, :] += column_sum(grad * normed)
+        vec_ref[4:5, :] += column_sum(grad)
+        vec_ref[5:6, :] += column_sum(low.astype(F32))
+
+    tiles(pull_one)
+    live = lax.broadcasted_iota(jnp.int32, (rows, 1), 0) < limit
+    d_merged_ref[...] = jnp.where(live, dot_nt(d_attn_ref[...], wo[...]), 0.0).astype(BF16)
+
+    def added(mine, other):
+        return (mine.astype(F32) + other.astype(F32)).astype(BF16)
+
+    def put(k, x, y, z, value):
+        if KINDS[k] == "A":
+            sum_ref[k, y, x, z] = value
+        else:
+            sum_ref[k, x, y, z] = value
+
+    for j in range(wide):
+        moving[j].wait()
+
+    def sum_down(s, _):
+        z, x, y = s // 4, lax.rem(s // 2, 2), lax.rem(s, 2)
+        total = added(down[core, z, x, y], down_in[z, x, y])
+        put(0, x, y, z, total[:share // 2])
+        put(1, x, y, z, total[share // 2:])
+        return 0
+
+    lax.fori_loop(0, up.shape[2], sum_down, 0)
+    for copy in moving[wide:]:
+        copy.wait()
+
+    def sum_up(s, _):
+        z, x, y = s // 4, lax.rem(s // 2, 2), lax.rem(s, 2)
+        put(2, x, y, z, added(up[core, 0, s], up_in[0, s]))
+        put(3, x, y, z, added(up[core, 1, s], up_in[1, s]))
+        return 0
+
+    lax.fori_loop(0, up.shape[2], sum_up, 0)
+
+
+def dense(
+    filled, tokens, merged, cotangent, out_weight, out_bias, attn_gain, attn_shift, up_weight,
+    up_bias, down_weight, down_bias, ffn_gain, ffn_shift,
+):
+    rows, features = tokens.shape
+    hidden = up_weight.shape[1]
+    wide = hidden // features
+    low = jax.ShapeDtypeStruct((rows, features), BF16)
+    shards = 16
+    piece = (2 * 24, features)
+    any_space = pl.BlockSpec(memory_space=pl.ANY)
+    return pl.pallas_call(
+        functools.partial(dense_kernel, rows, 128),
+        out_shape=(
+            low, jax.ShapeDtypeStruct((rows, features), F32), low, low,
+            jax.ShapeDtypeStruct((8, features), F32), jax.ShapeDtypeStruct((1, hidden), F32),
+            jax.ShapeDtypeStruct((4, 2, 2, 4) + piece, BF16),
+        ),
+        in_specs=[pl.BlockSpec(memory_space=pltpu.SMEM)] + [whole_vmem()] * 10 + [any_space] * 3,
+        out_specs=(whole_vmem(),) * 7,
+        scratch_shapes=[
+            VMEM((features, features), BF16),
+            VMEM((features, hidden), BF16),
+            VMEM((hidden, features), BF16),
+            VMEM((rows, features), F32),
+            VMEM((rows, 1), F32),
+            VMEM((rows, features), F32),
+            VMEM((rows, features), BF16),
+            VMEM((wide, rows, features), BF16),
+            VMEM((wide, rows, features), F32),
+            VMEM((rows, features), F32),
+            VMEM((rows, features), BF16),
+            VMEM((2, features, features), F32),
+            VMEM((2, 4, 2, 2, 24 * wide, features), BF16),
+            VMEM((2, wide // 2, shards) + piece, BF16),
+            VMEM((4, 2, 2, 24 * wide, features), BF16),
+            VMEM((wide // 2, shards) + piece, BF16),
+            pltpu.SemaphoreType.DMA((3,)),
+            pltpu.SemaphoreType.DMA((wide + wide // 2,)),
+            pltpu.SemaphoreType.DMA((wide + wide // 2,)),
+        ],
+        compiler_params=pltpu.CompilerParams(
+            collective_id=3, has_side_effects=True, vmem_limit_bytes=LIMIT
+        ),
+        name="dense",
+    )(
+        filled, tokens, merged, cotangent, out_bias[None], attn_gain[None], attn_shift[None],
+        up_bias[None], down_bias[None], ffn_gain[None], ffn_shift[None], out_weight, up_weight,
+        down_weight,
+    )
+
+
+KINDS = "ABBBBA"
+
+
+def masks(filled, seq, own_blocks):
+    at = seq * own_blocks + jnp.arange(own_blocks, dtype=jnp.int32)[:, None]
+    kind = jnp.arange(8, dtype=jnp.int32)[None, :]
+    window = at + kind - 1
+    ok = jnp.where(
+        kind < 3, (window >= 0) & (window < filled),
+        jnp.where(kind == 3, at >= 2, jnp.abs(at - (filled - 1)) > 1))
+    last = jnp.arange(4 * own_blocks, dtype=jnp.int32) == filled - 1
+    return jnp.concatenate([jnp.where(ok, 0.0, MASKED).astype(F32).reshape(-1), last.astype(F32)])
+
+
+def links(table, filled, own_blocks):
+    mine = table.reshape(4, own_blocks, 128)[:, :, :9].reshape(4, own_blocks, 3, 3)
+    blocks = mine.transpose(0, 2, 1, 3).reshape(12, own_blocks * 3)
+    count = blocks.shape[1]
+    at = jnp.arange(count, dtype=jnp.int32)
+    same = (blocks[:, :, None] == blocks[:, None, :]) & (at[None, None, :] < at[None, :, None])
+    before = jnp.max(jnp.where(same, at[None, None, :], -1), axis=2)
+    where = jnp.arange(32, dtype=jnp.int32)[None, :, None] == blocks[:, None, :]
+    tail = jnp.max(jnp.where(where, at[None, None, :], -1), axis=2)
+    both = jnp.concatenate([before.reshape(-1), tail.reshape(-1)])
+    return jnp.concatenate([jnp.where(both < 0, count, both), (filled - 1)[None]])
+
+
+def final_kernel(
+    rows, own_blocks, groups, tab_ref, link_ref, mask_ref, vec_in, up_vec, lse_ref,
+    sum_any, q_any, k_any, v_any, g_any, wk_any, wv_any, wq_any, x_any, far_any, merged_any,
+    d_attn_any, base_any,
+    dx_ref, gq_ref, gk_ref, gv_ref, go_ref, up_ref, down_ref, vec_ref,
+    work_f, work_q, land_c, land_1, land_2, land_z, small, small_in, small_z,
+    q_ref, g_ref, dq_ref, wq, wk, wv, x_ref, far_ref, merged_ref, d_attn_ref,
+    acc, last, picked, buf, land, dko, dvo, dkr, dvr, out_far, in_far,
+    loads, sends, recvs, z_sends, z_recvs, s_sends, s_recvs, d_sends, d_recvs, far_sems,
+):
+    features = q_ref.shape[1]
+    pairs = features // PAIR
+    picks_count = own_blocks * 3
     dp, seq = lax.axis_index("dp"), lax.axis_index("seq")
     x, z = lax.rem(dp, 2), dp // 2
     core, y = lax.rem(seq, 2), seq // 2
+    mate, across, diagonal = (lax.bitwise_xor(seq, bit) for bit in (1, 2, 3))
+    end = link_ref[2 * pairs * (picks_count + 4 * own_blocks)]
+    first_block = seq * own_blocks
+    low = lanes_low(BLK)
+    to_mate, to_y, to_x = (dp, mate), (dp, across), (lax.bitwise_xor(dp, 1), seq)
+    to_z = [(lax.rem(z + step, groups) * 2 + x, seq) for step in range(1, groups)]
+
+    loading = {}
+
+    def load(name, src, dst):
+        copy = pltpu.make_async_copy(src, dst, loads.at[len(loading)])
+        copy.start()
+        loading[name] = copy
+
+    load("sum", sum_any, work_f)
+    load("q", q_any, q_ref)
+    load("g", g_any, g_ref)
+
     barrier = pltpu.get_barrier_semaphore()
-    partners = {
-        "core": (dp, lax.bitwise_xor(seq, 1)),
-        "y": (dp, lax.bitwise_xor(seq, 2)),
-        "x": (lax.bitwise_xor(dp, 1), seq),
-    }
-    columns = [(lax.rem(z + step, groups) * 2 + x, seq) for step in range(1, groups)]
-    for target in list(partners.values()) + columns:
+    for target in [to_mate, to_y, to_x] + to_z:
         pl.semaphore_signal(barrier, inc=1, device_id=target, device_id_type=MESH)
     pl.semaphore_wait(barrier, 3 + groups - 1)
 
-    def send(src, dst, one, two, target):
-        copy = pltpu.make_async_remote_copy(
+    def remote(src, dst, one, two, target):
+        return pltpu.make_async_remote_copy(
             src_ref=src, dst_ref=dst, send_sem=one, recv_sem=two, device_id=target,
             device_id_type=MESH,
         )
-        copy.start()
-        return copy
-
-    small[...] = s_ref[...]
-
-    def item(k):
-        if k == chunks:
-            return small, small_c, small_1, small_2, small_z
-        return work.at[k], land_c.at[k], land_1.at[k], land_2.at[k], land_z.at[k]
-
-    def axes(k):
-        return (("y", y), ("x", x)) if k % 2 == 0 else (("x", x), ("y", y))
+
+    ffn_chunks = work_f.shape[0]
+
+    def own_half(k):
+        return work_f.at[k] if k < ffn_chunks else work_q.at[k - ffn_chunks, core]
+
+    def way(k):
+        return ((y, to_y), (x, to_x)) if KINDS[k] == "A" else ((x, to_x), (y, to_y))
+
+    def copy_core(k):
+        return remote(work_q.at[k - ffn_chunks, 1 - core], land_c.at[k - ffn_chunks],
+                      sends.at[0, k], recvs.at[0, k], to_mate)
+
+    def copy_one(k):
+        (at, target), _ = way(k)
+        return remote(own_half(k).at[1 - at], land_1.at[k], sends.at[1, k], recvs.at[1, k], target)
+
+    def copy_two(k):
+        (at, _), (then, target) = way(k)
+        return remote(own_half(k).at[at, 1 - then], land_2.at[k], sends.at[2, k], recvs.at[2, k],
+                      target)
+
+    def copy_z(k, step):
+        (at, _), (then, _) = way(k)
+        return remote(own_half(k).at[at, then, lax.rem(z + step, groups)], land_z.at[k, step - 1],
+                      z_sends.at[k, step - 1], z_recvs.at[k, step - 1], to_z[step - 1])
 
     def add(total, part):
         total[...] = (total[...].astype(F32) + part[...].astype(F32)).astype(total.dtype)
 
-    def loop_add(total, part):
-        def body(r, _):
-            add(total.at[r], part.at[r])
+    def end_core(k):
+        copy_core(k).wait()
+        mine, other = own_half(k), land_c.at[k - ffn_chunks]
+
+        def body(n, _):
+            for one in range(2):
+                for two in range(2):
+                    add(mine.at[one, two, n], other.at[one, two, n])
             return 0
 
-        lax.fori_loop(0, total.shape[0], body, 0)
-
-    loads = []
-    for k in range(chunks):
-        copy = pltpu.make_async_copy(g_ref.at[k], work.at[k], load_sem.at[k])
-        copy.start()
-        loads.append(copy)
-
-    live = {}
-
-    def start_core(k):
-        total, land, _, _, _ = item(k)
-        if k < chunks:
-            loads[k].wait()
-        live[k] = send(total.at[1 - core], land, sends.at[0, k], recvs.at[0, k], partners["core"])
-
-    def end_core(k):
-        total, land, land_a, _, _ = item(k)
-        live[k].wait()
-        (name, at), _ = axes(k)
-        mine = total.at[core]
-        for half in range(2):
-            for other in range(2):
-                loop_add(mine.at[half, other], land.at[half, other])
-        live[k] = send(mine.at[1 - at], land_a, sends.at[1, k], recvs.at[1, k], partners[name])
-
-    def end_first(k):
-        total, _, land_a, land_b, _ = item(k)
-        (_, at), (name, then) = axes(k)
-        live[k].wait()
-        mine = total.at[core, at]
-        for half in range(2):
-            loop_add(mine.at[half], land_a.at[half])
-        live[k] = send(mine.at[1 - then], land_b, sends.at[2, k], recvs.at[2, k], partners[name])
-
-    def end_second(k):
-        total, _, _, land_b, land = item(k)
-        (_, at), (_, then) = axes(k)
-        live[k].wait()
-        mine = total.at[core, at, then]
-        loop_add(mine, land_b)
-        live[k] = [
-            send(mine.at[lax.rem(z + step, groups)], land.at[step - 1], z_sends.at[k, step - 1],
-                 z_recvs.at[k, step - 1], columns[step - 1])
-            for step in range(1, groups)
+        lax.fori_loop(0, groups, body, 0)
+        copy_one(k).start()
+
+    def end_one(k):
+        (at, _), _ = way(k)
+        copy_one(k).wait()
+        mine, other = own_half(k).at[at], land_1.at[k]
+
+        def body(n, _):
+            for one in range(2):
+                add(mine.at[one, n], other.at[one, n])
+            return 0
+
+        lax.fori_loop(0, groups, body, 0)
+        copy_two(k).start()
+
+    def end_two(k):
+        (at, _), (then, _) = way(k)
+        copy_two(k).wait()
+        mine, other = own_half(k).at[at, then], land_2.at[k]
+
+        def body(n, _):
+            add(mine.at[n], other.at[n])
+            return 0
+
+        lax.fori_loop(0, groups, body, 0)
+        for step in range(1, groups):
+            copy_z(k, step).start()
+
+    def finish(k):
+        (at, _), (then, _) = way(k)
+        total = own_half(k)[at, then, z].astype(F32)
+        for step in range(1, groups):
+            copy_z(k, step).wait()
+            total = total + land_z[k, step - 1].astype(F32)
+        half = total.shape[0] // 2
+        if k < 2:
+            down_ref[2 * half * k:2 * half * (k + 1), :] = total
+        elif k < 4:
+            up_ref[:, (2 * k - 4) * features:(2 * k - 3) * features] = total[:half]
+            up_ref[:, (2 * k - 3) * features:(2 * k - 2) * features] = total[half:]
+        else:
+            one, two = (gq_ref, gk_ref) if k == 4 else (gv_ref, go_ref)
+            one[...] = total[:half]
+            two[...] = total[half:]
+
+    loading["sum"].wait()
+    copy_one(0).start()
+    copy_one(1).start()
+    for name, src, dst in (
+        ("wk", wk_any, wk), ("wv", wv_any, wv), ("wq", wq_any, wq), ("x", x_any, x_ref),
+        ("far", far_any, far_ref), ("merged", merged_any, merged_ref),
+        ("d_attn", d_attn_any, d_attn_ref), ("base", base_any, dx_ref),
+    ):
+        load(name, src, dst)
+
+    def copy_pair(p, slot, owner):
+        return remote(buf.at[p, owner], land.at[p, slot], d_sends.at[p, slot], d_recvs.at[p, slot],
+                      to_mate)
+
+    def lanes_of(p):
+        return pl.ds(pl.multiple_of(p * PAIR, PAIR), PAIR)
+
+    def sum_pair(p):
+        lanes = lanes_of(p)
+        for slot, owner, keys_to, values_to in ((0, across, dkr, dvr), (1, seq, dko, dvo)):
+            copy_pair(p, slot, diagonal if slot == 0 else mate).wait()
+            for n, to in ((0, keys_to), (1, values_to)):
+                to[:, lanes] = (
+                    buf[p, owner, n].astype(F32) + land[p, slot, n].astype(F32)
+                ).astype(BF16)
+
+    for n in range(2):
+        picked[n, picks_count] = jnp.zeros((BLK, PAIR), F32)
+
+    def attention(k_ref, v_ref, kv_sems):
+        fetch = [
+            pltpu.make_async_copy(k_any, k_ref, kv_sems.at[0]),
+            pltpu.make_async_copy(v_any, v_ref, kv_sems.at[1]),
         ]
-
-    def finish(k):
-        total, _, _, _, land = item(k)
-        (_, at), (_, then) = axes(k)
-        result = total[core, at, then, z].astype(F32)
-        for step in range(1, groups):
-            live[k][step - 1].wait()
-            result = result + land[step - 1].astype(F32)
-        if k == chunks:
-            small_out[...] = result
-        else:
-            out_ref[k] = result
-
-    order = [chunks] + list(range(chunks))
-    for n, k in enumerate(order[:3]):
-        start_core(k)
-    for n, k in enumerate(order):
-        end_core(k)
-        if n + 3 < len(order):
-            start_core(order[n + 3])
-    for n in range(len(order) + 2):
-        if n < len(order):
-            end_first(order[n])
-        if 0 <= n - 1 < len(order):
-            end_second(order[n - 1])
-        if 0 <= n - 2 < len(order):
-            finish(order[n - 2])
-
-
-def reduce_scatter(grads, small):
-    chunks, rows, features = grads.shape[0], grads.shape[-2], grads.shape[-1]
-    groups = grads.shape[4]
-    little = small.shape[-2:]
+        for copy in fetch:
+            copy.start()
+        loading["q"].wait()
+        loading["g"].wait()
+        for copy in fetch:
+            copy.wait()
+        last_row = k_ref.shape[0] - 1
+
+        def one_pair(p, _):
+            lanes = lanes_of(p)
+            acc[...] = jnp.zeros_like(acc)
+            last[...] = jnp.zeros_like(last)
+
+            def step(i, _):
+                at = first_block + i
+                shared, both = key_blocks(tab_ref, end, p, i, at, own_blocks, last_row)
+                keys = gathered(k_ref, shared, both, low, lanes)
+                values = gathered(v_ref, shared, both, low, lanes)
+                query = split_pair(q_ref[rows_of(i), lanes], low)
+                grad = split_pair(g_ref[rows_of(i), lanes], low)
+                scores = masked_scores(dot_nt(keys, query), mask_ref, i)
+                share = jnp.exp(scores - lse_ref[p, pl.ds(i, 1), :])
+                d_share = dot_nt(values, grad)
+                centre = jnp.sum(share * d_share, axis=0, keepdims=True)
+                d_scores = (share * (d_share - centre)).astype(BF16)
+                d_query = dot_tn(d_scores, keys) * SCALE
+                dq_ref[rows_of(i), lanes] = jnp.where(low, d_query[:BLK], d_query[BLK:]).astype(BF16)
+                parts = (dot(d_scores, query), dot(share.astype(BF16), grad))
+                for n, part in enumerate(parts):
+                    for slot in range(3):
+                        acc[n, rows_of(at + slot), :] += part[slot * BLK:(slot + 1) * BLK]
+                    acc[n, BLK:2 * BLK, :] += part[3 * BLK:4 * BLK]
+                    last[n] += part[4 * BLK:5 * BLK]
+                for t in range(3):
+                    one = link_ref[2 * p * picks_count + i * 3 + t]
+                    two = link_ref[(2 * p + 1) * picks_count + i * 3 + t]
+                    for n, part in enumerate(parts):
+                        picked[n, i * 3 + t] = part[(5 + t) * BLK:(6 + t) * BLK] + jnp.where(
+                            low, picked[n, one], picked[n, two])
+                return 0
+
+            lax.fori_loop(0, own_blocks, step, 0, unroll=own_blocks)
+            tails = 2 * pairs * picks_count
+
+            def gather(owner, _):
+                for inner in range(own_blocks):
+                    block = owner * own_blocks + inner
+                    one = link_ref[tails + 2 * p * (last_row + 1) + block]
+                    two = link_ref[tails + (2 * p + 1) * (last_row + 1) + block]
+                    for n in range(2):
+                        total = acc[n, rows_of(block + 1), :]
+                        total = total + jnp.where(low, picked[n, one], picked[n, two])
+                        total = total + last[n] * mask_ref[own_blocks * 8 + block]
+                        buf[p, owner, n, inner * BLK:(inner + 1) * BLK] = total.astype(BF16)
+                return 0
+
+            lax.fori_loop(0, 4, gather, 0)
+            copy_pair(p, 0, diagonal).start()
+            copy_pair(p, 1, mate).start()
+
+            @pl.when(p > 0)
+            def _():
+                sum_pair(p - 1)
+
+            @pl.when(p == 2)
+            def _():
+                copy_one(2).start()
+
+            @pl.when(p == 3)
+            def _():
+                end_one(0)
+                end_one(1)
+
+            return 0
+
+        lax.fori_loop(0, pairs, one_pair, 0)
+
+    slot = (4 * own_blocks, BLK, features)
+    pl.run_scoped(
+        attention, VMEM(slot, BF16), VMEM(slot, BF16),
+        pltpu.SemaphoreType.DMA((2,)),
+    )
+    copy_one(3).start()
+    sum_pair(pairs - 1)
+
+    loading["wk"].wait()
+    loading["wv"].wait()
+    out_far[...] = (dot_nt(dkr[...], wk[...]) + dot_nt(dvr[...], wv[...])).astype(BF16)
+    far = remote(out_far, in_far, far_sems.at[0], far_sems.at[1], to_y)
+    far.start()
+    end_two(1)
+    for name in ("wq", "x", "far", "merged", "d_attn", "base"):
+        loading[name].wait()
+
+    def weights(tmp):
+        def regroup(k):
+            def body(s, _):
+                third, rest = s // 4, lax.rem(s, 4)
+                sx, sy = rest // 2, lax.rem(rest, 2)
+                a, b = (sy, sx) if KINDS[k] == "A" else (sx, sy)
+                for n in range(2):
+                    at = pl.ds(pl.multiple_of((2 * s + n) * 24, 8), 24)
+                    work_q[k - ffn_chunks, n, a, b, third] = jnp.concatenate(
+                        [tmp[0, at, :], tmp[1, at, :]], axis=0).astype(BF16)
+                return 0
+
+            lax.fori_loop(0, 4 * groups, body, 0)
+            copy_core(k).start()
+
+        tmp[0] = dot_tn(x_ref[...], dq_ref[...])
+        tmp[1] = dot_tn(x_ref[...], dko[...]) + dot_tn(far_ref[...], dkr[...])
+        regroup(4)
+        end_one(2)
+        end_two(0)
+        tmp[0] = dot_tn(x_ref[...], dvo[...]) + dot_tn(far_ref[...], dvr[...])
+        tmp[1] = dot_tn(merged_ref[...], d_attn_ref[...])
+        regroup(5)
+
+    pl.run_scoped(weights, VMEM((2, features, features), F32))
+    end_core(4)
+
+    small[...] = jnp.zeros_like(small)
+    small[0:6, :] = vec_in[0:6, :]
+    small[6:7, :] = jnp.sum(dq_ref[...].astype(F32), axis=0, keepdims=True)
+    small[7:8, :] = (
+        jnp.sum(dvo[...].astype(F32), axis=0, keepdims=True)
+        + jnp.sum(dvr[...].astype(F32), axis=0, keepdims=True)
+    )
+    for n in range(up_vec.shape[1] // features):
+        small[8 + n:9 + n, :] = up_vec[:, n * features:(n + 1) * features]
+
+    def copy_small(stage):
+        target = (to_mate, to_y, to_x)[stage]
+        return remote(small, small_in.at[stage], s_sends.at[stage], s_recvs.at[stage], target)
+
+    def copy_small_z(step):
+        return remote(small, small_z.at[step - 1], s_sends.at[2 + step], s_recvs.at[2 + step],
+                      to_z[step - 1])
+
+    copy_small(0).start()
+    dx_ref[...] += (
+        dot_nt(dq_ref[...], wq[...]) + dot_nt(dko[...], wk[...]) + dot_nt(dvo[...], wv[...])
+    )
+    end_core(5)
+    copy_small(0).wait()
+    small[...] += small_in[0]
+    copy_small(1).start()
+    end_one(3)
+    end_two(2)
+    finish(0)
+    finish(1)
+    copy_small(1).wait()
+    small[...] += small_in[1]
+    copy_small(2).start()
+    far.wait()
+    dx_ref[...] += in_far[...].astype(F32)
+    end_one(4)
+    copy_small(2).wait()
+    small[...] += small_in[2]
+    for step in range(1, groups):
+        copy_small_z(step).start()
+    end_two(3)
+    finish(2)
+    end_one(5)
+    finish(3)
+    end_two(4)
+    total = small[...]
+    for step in range(1, groups):
+        copy_small_z(step).wait()
+        total = total + small_z[step - 1]
+    vec_ref[...] = total
+    end_two(5)
+    finish(4)
+    finish(5)
+
+
+def final(
+    groups, table, link, mask, vectors, up_vector, lse, sums, query, keys, values, grad,
+    key_weight, value_weight, query_weight, tokens, far_tokens, merged, d_attn, base,
+):
+    rows, features = tokens.shape
+    own_blocks = rows // BLK
+    pairs = features // PAIR
+    piece = sums.shape[-2:]
+    share = features // (8 * groups)
+    wide = up_vector.shape[1] // features
+    low = VMEM((rows, features), BF16)
+    square = VMEM((features, features), BF16)
+    line = jax.ShapeDtypeStruct((share, features), F32)
+    any_space = pl.BlockSpec(memory_space=pl.ANY)
+    in_smem = pl.BlockSpec(memory_space=pltpu.SMEM)
+    dma = pltpu.SemaphoreType.DMA
     return pl.pallas_call(
-        functools.partial(reduce_kernel, chunks, groups),
+        functools.partial(final_kernel, rows, own_blocks, groups),
         out_shape=(
-            jax.ShapeDtypeStruct((chunks, rows, features), F32),
-            jax.ShapeDtypeStruct(little, F32),
+            jax.ShapeDtypeStruct((rows, features), F32), line, line, line, line,
+            jax.ShapeDtypeStruct((share, wide * features), F32),
+            jax.ShapeDtypeStruct((wide * share, features), F32),
+            jax.ShapeDtypeStruct((16, features), F32),
         ),
-        in_specs=[pl.BlockSpec(memory_space=pl.ANY), whole_vmem()],
-        out_specs=(whole_vmem(), whole_vmem()),
+        in_specs=[in_smem] * 3 + [whole_vmem()] * 3 + [any_space] * 13,
+        out_specs=(whole_vmem(),) * 8,
         scratch_shapes=[
-            VMEM(grads.shape, BF16),
-            VMEM(small.shape, F32),
-            VMEM((chunks,) + grads.shape[2:], BF16),
-            VMEM((chunks,) + grads.shape[3:], BF16),
-            VMEM((chunks,) + grads.shape[4:], BF16),
-            VMEM((chunks, groups - 1, rows, features), BF16),
-            VMEM(small.shape[1:], F32),
-            VMEM(small.shape[2:], F32),
-            VMEM(small.shape[3:], F32),
-            VMEM((groups - 1,) + little, F32),
-            pltpu.SemaphoreType.DMA((3, chunks + 1)),
-            pltpu.SemaphoreType.DMA((3, chunks + 1)),
-            pltpu.SemaphoreType.DMA((chunks + 1, groups - 1)),
-            pltpu.SemaphoreType.DMA((chunks + 1, groups - 1)),
-            pltpu.SemaphoreType.DMA((chunks,)),
+            VMEM(sums.shape, BF16),
+            VMEM((2, 2, 2, 2, groups) + piece, BF16),
+            VMEM((2, 2, 2, groups) + piece, BF16),
+            VMEM((6, 2, groups) + piece, BF16),
+            VMEM((6, groups) + piece, BF16),
+            VMEM((6, groups - 1) + piece, BF16),
+            VMEM((16, features), F32),
+            VMEM((3, 16, features), F32),
+            VMEM((groups - 1, 16, features), F32),
+            low, low, low, square, square, square, low, low, low, low,
+            VMEM((2, (4 * own_blocks + 2) * BLK, PAIR), F32),
+            VMEM((2, BLK, PAIR), F32),
+            VMEM((2, own_blocks * 3 + 1, BLK, PAIR), F32),
+            VMEM((pairs, 4, 2, rows, PAIR), BF16),
+            VMEM((pairs, 2, 2, rows, PAIR), BF16),
+            low, low, low, low, low, low,
+            dma((11,)),
+            dma((3, 6)), dma((3, 6)), dma((6, groups - 1)), dma((6, groups - 1)),
+            dma((2 + groups,)), dma((2 + groups,)), dma((pairs, 2)), dma((pairs, 2)), dma((2,)),
         ],
         compiler_params=pltpu.CompilerParams(
-            collective_id=2, has_side_effects=True, vmem_limit_bytes=LIMIT
+            collective_id=4, has_side_effects=True, vmem_limit_bytes=LIMIT
         ),
-        name="reduce_scatter",
-    )(grads, small)
-
-
-def summed_on_box(square, up, down, vectors, up_bias, groups):
-    features = up.shape[0]
-    devices = 8 * groups
-    share = features // devices
-    wide = up.shape[1] // features
-    low = [g.astype(BF16).reshape(devices, share, features) for g in square]
-    ups = up.astype(BF16).reshape(devices, share, wide, features)
-    downs = down.astype(BF16).reshape(devices, wide * share, features)
-    pieces = [
-        jnp.concatenate(low[:2], axis=1),
-        jnp.concatenate(low[2:], axis=1),
-    ]
-    for j in range(0, wide, 2):
-        pieces.append(jnp.concatenate([ups[:, :, j], ups[:, :, j + 1]], axis=1))
-    for j in range(0, wide, 2):
-        pieces.append(downs[:, j * share:(j + 2) * share])
-    placed = []
-    for k, piece in enumerate(pieces):
-        piece = piece.reshape(groups, 2, 2, 2, 2 * share, features)
-        order = (3, 2, 1, 0, 4, 5) if k % 2 == 0 else (3, 1, 2, 0, 4, 5)
-        placed.append(piece.transpose(order))
-    grads = jnp.stack(placed)
-    count = len(vectors)
-    flat = jnp.concatenate(
-        [jnp.stack(vectors).reshape(count, devices, share).transpose(1, 0, 2),
-         up_bias.reshape(devices, wide, share)], axis=1)
-    flat = jnp.pad(flat, ((0, 0), (0, 16 - count - wide), (0, 128 - share)))
-    flat = flat.reshape(groups, 2, 2, 2, 16, 128).transpose(3, 2, 1, 0, 4, 5)
-    big, little = reduce_scatter(grads, flat)
-    out_square = [big[0, :share], big[0, share:], big[1, :share], big[1, share:]]
-    out_up = jnp.concatenate(
-        [big[2 + j // 2, (j % 2) * share:(j % 2 + 1) * share] for j in range(wide)], axis=1)
-    out_down = jnp.concatenate([big[2 + wide // 2 + j] for j in range(wide // 2)], axis=0)
-    out_vectors = [little[n, :share] for n in range(count)]
-    out_up_bias = little[count:count + wide, :share].reshape(-1)
-    return out_square, out_up, out_down, out_vectors, out_up_bias
-
-
-def summed_anywhere(square, up, down, vectors, up_bias):
-    def one(g):
-        return lax.psum_scatter(g, ("dp", "seq"), scatter_dimension=0, tiled=True)
-
-    return [one(g) for g in square], one(up), one(down), [one(v) for v in vectors], one(up_bias)
+        name="final",
+    )(
+        table, link, mask, vectors, up_vector, lse, sums, query, keys, values, grad, key_weight,
+        value_weight, query_weight, tokens, far_tokens, merged, d_attn, base,
+    )
 
 
 def layer_norm(values, gain, shift):
@@ -634,7 +1105,30 @@
         tokens, table, query_weight, query_bias, key_weight, value_weight, value_bias
     )
     table = table.reshape(-1)
-    merged, lse = attention_forward(table, filled_blocks, query, keys, values)
+    mask = masks(filled, lax.axis_index("seq"), row_count // BLK)
+    keys, values = (t.reshape(-1, BLK, feature_count) for t in (keys, values))
+    merged, lse = attention_forward(table, filled_blocks, mask, query, keys, values)
+
+    if groups:
+        seq = lax.axis_index("seq")
+        result, base, d_attn, d_merged, vectors, up_vector, sums = dense(
+            filled_blocks, tokens, merged, cotangent, out_weight, out_bias, attn_gain, attn_shift,
+            up_weight, up_bias, down_weight, down_bias, ffn_gain, ffn_shift)
+        grad_tokens, gq, gk, gv, go, up, down, vectors = final(
+            groups, table, links(table, filled, row_count // BLK),
+            mask, vectors, up_vector,
+            lse, sums, query, keys, values, d_merged, key_weight, value_weight, query_weight,
+            tokens, far_tokens, merged, d_attn, base)
+        shard = lax.axis_index("dp") * 4 + seq
+        share = gq.shape[0]
+        mine = lax.dynamic_slice(vectors, (0, shard * share), (8, share))
+        wide = up.shape[1] // feature_count
+        up_sum = lax.dynamic_slice(
+            vectors[8:8 + wide].reshape(-1), (shard * wide * share,), (wide * share,))
+        return (
+            result, grad_tokens, gq, mine[6], gk, gv, mine[7], go, mine[5], mine[3], mine[4], up,
+            up_sum, down, mine[2], mine[0], mine[1],
+        )
 
     attn = dot(merged, out_weight) + out_bias
     first, normed_one, root_one = layer_norm(tokens.astype(F32) + attn, attn_gain, attn_shift)
@@ -663,7 +1157,7 @@
     d_merged = dot_nt(d_attn, out_weight).astype(BF16)
 
     d_query, d_keys, d_values = attention_backward(
-        table, filled_blocks, query, keys, values, d_merged, lse
+        table, filled_blocks, mask, query, keys, values, d_merged, lse
     )
     grad_tokens, dk_own, dv_own, dk_far, dv_far = exchange(
         d_keys, d_values, d_query, d_sum_one, query_weight, key_weight, value_weight
@@ -679,12 +1173,8 @@
         grad_query_bias, grad_value_bias, grad_out_bias, grad_attn_gain, grad_attn_shift,
         grad_down_bias, grad_ffn_gain, grad_ffn_shift,
     )
-    if groups:
-        square, up, down, vectors, up_sum = summed_on_box(
-            square, grad_up_weight, grad_down_weight, vectors, grad_up_bias, groups)
-    else:
-        square, up, down, vectors, up_sum = summed_anywhere(
-            square, grad_up_weight, grad_down_weight, vectors, grad_up_bias)
+    square, up, down, vectors, up_sum = summed_anywhere(
+        square, grad_up_weight, grad_down_weight, vectors, grad_up_bias)
     return (
         result.astype(BF16), grad_tokens, square[0], vectors[0], square[1], square[2], vectors[1],
         square[3], vectors[2], vectors[3], vectors[4], up, up_sum, down, vectors[5], vectors[6],

time: 347 us -> 207 us (0.60); the launches traced: 341 us -> 206 us
  matrix products: 43.7 us -> 0 us
  local copies, waits for them, and re-layouts: 55.1 us -> 16.1 us
  Pallas kernels: 219 us -> 186 us
  other arithmetic: 21.1 us -> 2.66 us
    dot_general x14 -> x0, matrix products: 43.7 us -> none  [the longest x8 18.7 us: dot_tn(): lax.dot_general(left, right, (((0,), (0,)), ((), ())), preferred_element_...]
    pallas_call x3 -> x2, Pallas kernels: 165 us -> 146 us  [the longest x1 107 us: final(): pl.pallas_call(functools.partial(final_kernel, rows, own_blocks, groups),...]
    pallas_call x1, Pallas kernels: 26.3 us -> 11.9 us  [attention_forward(): pl.pallas_call(functools.partial(forward_kernel, own_blocks), out_shape=(...]
    reshape x5 -> x3, local copies, waits for them, and re-layouts: 14.1 us -> 0.17 us  [the longest x2 0.16 us: links(): both = jnp.concatenate([before.reshape(-1), tail.reshape(-1)])]
    reduce_sum x8 -> x0, other arithmetic: 10.3 us -> none  [the longest x1 3.89 us: on_device(): grad_down_bias = jnp.sum(d_ffn, axis=0, dtype=F32)]
    another operation x9 -> x0, local copies, waits for them, and re-layouts: 10.1 us -> none  [the longest x8 8.38 us: summed_on_box(): jnp.stack(vectors).reshape(count, devices, share).transpose(1, 0, 2)]
    slice x3 -> x2, local copies, waits for them, and re-layouts: 10.1 us -> 0.84 us  [the longest x1 0.74 us: on_device(): vectors[8:8 + wide].reshape(-1)]
    unnamed x8 -> x1, other arithmetic: 7.28 us -> 0.72 us
where the time goes in v2:
time: 207 us; the launch traced here: 206 us
  Pallas kernels  186 us (90%)
  local copies, waits for them, and re-layouts  16.1 us (8%)
  other arithmetic  2.66 us (1%)
    pallas_call x1, Pallas kernels, final(): pl.pallas_call(functools.partial(final_kernel, rows, own_blocks, groups),...  107 us
    pallas_call x1, Pallas kernels, dense(): pl.pallas_call(functools.partial(dense_kernel, rows, 128), out_shape=(low...  38.7 us
    pallas_call x1, Pallas kernels, gather_project(): pl.pallas_call(functools.partial(gather_kernel, rows, 128), out_shape=(ja...  28 us
    pallas_call x1, Pallas kernels, attention_forward(): pl.pallas_call(functools.partial(forward_kernel, own_blocks), out_shape=(...  11.9 us
    unnamed x38, local copies, waits for them, and re-layouts  6.05 us

profile of v2, /device:TPU:0, one launch (start us, length us, event | category | flops | bytes accessed | tf_op | source)
XLA Modules:
  0.0 206.1 jit_solution(10909333374000941071)
XLA Ops:
  1.3 0.7 reduce
  2.0 0.1 copy.40
  2.1 0.6 pad.4.tab_ref
  2.7 1.3 broadcast_in_dim.107.qb_ref
  4.0 1.3 broadcast_in_dim.108.vb_ref
  5.3 28.0 %gather_project.1 = (bf16[512,768]{1,0:T(8,128)(2,1)}, bf16[2048,768]{1,0:T(8,128)(2,1)}, bf16[2048,768]{1,0:T(8,128)(2,1)}, bf16[512,768]{1,0:T(8,128)(2,1)}, s32[4,8,128]{2,1,0:T(8,128)}) custom-call(bf16[512,768]{1,0:T(8,128)(2,1)} %x_any.1, s32[32,128]{1,0:T(8,128)} %pad.4.tab_ref, bf16[768,768]{1,0:T(8,128)(2,1)} %wq_any.1, ...), custom_call_target="tpu_custom_call" | custom-call | tf_op jit(solution)/shard_map/gather_project/pallas_call | solution.py:125
  33.3 0.1 fusion.4
  33.4 0.1 reshape.123
  33.5 0.6 pad_maximum_fusion.mask_ref
  34.1 0.0 copy-start.13
  34.1 0.0 copy-start.14
  34.1 11.9 %attention_forward.1 = (bf16[512,768]{1,0:T(8,128)(2,1)}, f32[6,8,128]{2,1,0:T(8,128)}) custom-call(s32[4096]{0:T(1024)} %bitcast.36, s32[1]{0:T(128)} %copy.52.filled_ref, f32[96]{0:T(128)} %pad_maximum_fusion.mask_ref, bf16[512,768]{1,0:T(8,128)(2,1)} %get-tuple-element.40.q_ref.q_any, bf16[32,64,768]{2,1,0:T(8,128)(2,1)} %bitcast.32, ...), custom_call_target="tpu_custom_call" | custom-call | tf_op jit(solution)/shard_map/attention_forward/pallas_call | solution.py:224
  46.0 0.0 copy-done.9
  46.0 0.6 broadcast_in_dim.116.bo_ref
  46.6 0.6 broadcast_in_dim.117.g1_ref
  47.2 0.6 broadcast_in_dim.118.s1_ref
  47.8 0.0 copy-done.12
  47.8 0.6 broadcast_in_dim.120.bd_ref
  48.4 0.6 broadcast_in_dim.121.g2_ref
  49.0 0.6 broadcast_in_dim.122.s2_ref
  49.5 38.7 %dense.1 = (bf16[512,768]{1,0:T(8,128)(2,1)}, f32[512,768]{1,0:T(8,128)}, bf16[512,768]{1,0:T(8,128)(2,1)}, bf16[512,768]{1,0:T(8,128)(2,1)}, f32[8,768]{1,0:T(8...) custom-call(s32[1]{0:T(128)} %copy.52.filled_ref, bf16[512,768]{1,0:T(8,128)(2,1)} %x_any.1, ...), custom_call_target="tpu_custom_call" | custom-call | tf_op jit(solution)/shard_map/dense/pallas_call | solution.py:607
  88.2 0.1 copy.41
  88.3 0.1 copy.42
  88.5 0.1 eq.45
  88.6 0.1 select_reduce_fusion
  88.7 0.1 reshape.118
  88.8 0.4 select_reduce_fusion.1
  89.2 0.1 reshape.117
  89.2 0.1 compare_select_fusion
  89.3 0.7 pad_add_fusion.link_ref
  90.0 107.3 %final.1 = (f32[512,768]{1,0:T(8,128)}, f32[24,768]{1,0:T(8,128)}, f32[24,768]{1,0:T(8,128)}, f32[24,768]{1,0:T(8,128)}, f32[24,768]{1,0:T(8,128)}, /*index=5*/f...) custom-call(s32[4096]{0:T(1024)} %bitcast.37, s32[673]{0:T(1024)} %pad_add_fusion.link_ref, ...), custom_call_target="tpu_custom_call" | custom-call | tf_op jit(solution)/shard_map/final/pallas_call | solution.py:1031
  197.3 0.0 copy-start
  197.3 0.9 constant_dynamic-slice_fusion
  198.2 0.5 slice_bitcast_fusion
  198.7 0.7 slice.36
  199.5 0.6 dynamic_slice.7
  200.1 0.9 copy.53
  201.0 0.0 copy-start.5
  201.0 0.0 copy-start.3
  201.0 0.0 copy-start.2
  201.0 1.1 copy.54
  202.2 0.6 copy.55
  202.8 0.0 copy-done.7
  202.8 0.6 copy.56
  203.4 0.6 copy.57
  204.1 0.6 copy.58
  204.7 0.7 copy.59
  205.4 0.7 copy.60
  (28 shorter events, 0.1 us)
Async XLA Ops:
  34.1 12.0 %copy-start.9 = (f32[768]{0:T(1024)S(1)}, f32[768]{0:T(1024)}, u32[]{:S(2)}) copy-start(f32[768]{0:T(1024)} %param.28) | copy-start | bytes 9220
  34.1 12.6 %copy-start.10 = (f32[768]{0:T(1024)S(1)}, f32[768]{0:T(1024)}, u32[]{:S(2)}) copy-start(f32[768]{0:T(1024)} %param.29) | copy-start | bytes 9220
  34.1 13.1 %copy-start.11 = (f32[768]{0:T(1024)S(1)}, f32[768]{0:T(1024)}, u32[]{:S(2)}) copy-start(f32[768]{0:T(1024)} %param.30) | copy-start | bytes 9220
  34.1 13.7 %copy-start.12 = (f32[768]{0:T(1024)S(1)}, f32[768]{0:T(1024)}, u32[]{:S(2)}) copy-start(f32[768]{0:T(1024)} %param.34) | copy-start | bytes 9220
  34.1 14.3 %copy-start.13 = (f32[768]{0:T(1024)S(1)}, f32[768]{0:T(1024)}, u32[]{:S(2)}) copy-start(f32[768]{0:T(1024)} %param.35) | copy-start | bytes 9220
  34.1 14.9 %copy-start.14 = (f32[768]{0:T(1024)S(1)}, f32[768]{0:T(1024)}, u32[]{:S(2)}) copy-start(f32[768]{0:T(1024)} %param.36) | copy-start | bytes 9220
  49.5 38.7 %copy-start.4 = (s32[4,8,128]{2,1,0:T(8,128)S(1)}, s32[4,8,128]{2,1,0:T(8,128)}, u32[]{:S(2)}) copy-start(s32[4,8,128]{2,1,0:T(8,128)} %get-tuple-element.39) | copy-start | bytes 49156
  90.0 110.1 %copy-start.1 = (bf16[512,768]{1,0:T(8,128)(2,1)S(1)}, bf16[512,768]{1,0:T(8,128)(2,1)}, u32[]{:S(2)}) copy-start(bf16[512,768]{1,0:T(8,128)(2,1)} %get-tuple-element.90) | copy-start | bytes 2359300
  197.3 3.7 %copy-start = (f32[512,768]{1,0:T(8,128)S(1)}, f32[512,768]{1,0:T(8,128)}, u32[]{:S(2)}) copy-start(f32[512,768]{1,0:T(8,128)} %get-tuple-element.91) | copy-start | bytes 4718596
  201.0 1.2 copy-start.8
  201.0 1.8 copy-start.7
  201.0 2.5 %copy-start.6 = (f32[24,768]{1,0:T(8,128)S(1)}, f32[24,768]{1,0:T(8,128)}, u32[]{:S(2)}) copy-start(f32[24,768]{1,0:T(8,128)} %get-tuple-element.95) | copy-start | bytes 221188
  201.0 3.1 %copy-start.5 = (f32[24,768]{1,0:T(8,128)S(1)}, f32[24,768]{1,0:T(8,128)}, u32[]{:S(2)}) copy-start(f32[24,768]{1,0:T(8,128)} %get-tuple-element.97) | copy-start | bytes 221188
  201.0 3.7 %copy-start.3 = (f32[24,3072]{1,0:T(8,128)S(1)}, f32[24,3072]{1,0:T(8,128)}, u32[]{:S(2)}) copy-start(f32[24,3072]{1,0:T(8,128)} %get-tuple-element.101) | copy-start | bytes 884740
  201.0 4.4 %copy-start.2 = (f32[96,768]{1,0:T(8,128)S(1)}, f32[96,768]{1,0:T(8,128)}, u32[]{:S(2)}) copy-start(f32[96,768]{1,0:T(8,128)} %get-tuple-element.103) | copy-start | bytes 884740

commit v3 on v1

v3 whole, which is shorter than its diff:
```python
import functools

import jax
import jax.numpy as jnp
from jax import lax
from jax.experimental import pallas as pl
from jax.experimental.pallas import tpu as pltpu
from jax.sharding import PartitionSpec as P

HEAD_DIM = 64
BLK = 64
PAIR = 2 * HEAD_DIM
TABLE = 8
NORM_EPS = 1e-05
MASKED = -1e30
SCALE = HEAD_DIM ** (-0.5)
MESH = pl.DeviceIdType.MESH
BF16 = jnp.bfloat16
F32 = jnp.float32
VMEM = pltpu.VMEM
LIMIT = 63 << 20


def whole_vmem():
    return pl.BlockSpec(memory_space=pltpu.VMEM)


def dot(left, right):
    return jnp.dot(left, right, preferred_element_type=F32)


def dot_nt(left, right):
    return lax.dot_general(left, right, (((1,), (1,)), ((), ())), preferred_element_type=F32)


def dot_tn(left, right):
    return lax.dot_general(left, right, (((0,), (0,)), ((), ())), preferred_element_type=F32)


def gather_kernel(
    rows, width, x_ref, tab_ref, wq_ref, wk_ref, wv_ref, bias_ref,
    q_ref, k_ref, v_ref, far_ref, tab_out, land, tab_land, sends, recvs, tab_sends, tab_recvs,
):
    parts = 4
    part = rows // parts
    dp, me = lax.axis_index("dp"), lax.axis_index("seq")
    mate, across, diagonal = (lax.bitwise_xor(me, bit) for bit in (1, 2, 3))
    barrier = pltpu.get_barrier_semaphore()
    for other in (mate, across, diagonal):
        pl.semaphore_signal(barrier, inc=1, device_id=(dp, other), device_id_type=MESH)
    pl.semaphore_wait(barrier, 3)

    def send(src, dst, slot, target):
        copy = pltpu.make_async_remote_copy(
            src_ref=src, dst_ref=dst, send_sem=sends.at[slot], recv_sem=recvs.at[slot],
            device_id=(dp, target), device_id_type=MESH,
        )
        copy.start()
        return copy

    far = [
        send(x_ref.at[pl.ds(r * part, part)], land.at[0, pl.ds(r * part, part)], r, across)
        for r in range(parts)
    ]
    near = send(x_ref, land.at[1], parts, mate)
    tables = []
    own_blocks = tab_ref.shape[0] // 4
    for slot, other in enumerate((mate, across, diagonal)):
        copy = pltpu.make_async_remote_copy(
            src_ref=tab_ref.at[pl.ds(pl.multiple_of(other * own_blocks, 8), own_blocks)],
            dst_ref=tab_land.at[slot], send_sem=tab_sends.at[slot], recv_sem=tab_recvs.at[slot],
            device_id=(dp, other), device_id_type=MESH,
        )
        copy.start()
        tables.append(copy)

    def keys_values(x, at):
        k_ref[pl.ds(at, width), :] = dot(x, wk_ref[...]).astype(BF16)
        v_ref[pl.ds(at, width), :] = (dot(x, wv_ref[...]) + bias_ref[1:2, :]).astype(BF16)

    def own(r, _):
        at = pl.multiple_of(r * width, width)
        x = x_ref[pl.ds(at, width), :]
        q_ref[pl.ds(at, width), :] = (
            (dot(x, wq_ref[...]) + bias_ref[0:1, :]).astype(BF16) * jnp.asarray(SCALE, BF16)
        )
        keys_values(x, pl.multiple_of(me * rows + at, width))
        return 0

    lax.fori_loop(0, rows // width, own, 0)

    def block(slot, owner, start, count):
        def step(r, _):
            at = pl.multiple_of(start + r * width, width)
            keys_values(land[slot, pl.ds(at, width), :], pl.multiple_of(owner * rows + at, width))
            return 0

        lax.fori_loop(0, count // width, step, 0)

    near.wait()
    block(1, mate, 0, rows)
    relayed = []
    for r in range(parts):
        far[r].wait()
        piece = pl.ds(r * part, part)
        relayed.append(send(land.at[0, piece], land.at[2, piece], parts + 1 + r, mate))
        block(0, across, r * part, part)
        if r:
            relayed[r - 1].wait()
            block(2, diagonal, (r - 1) * part, part)
    far_ref[...] = land[0]
    for copy in tables:
        copy.wait()
    relayed[-1].wait()
    block(2, diagonal, (parts - 1) * part, part)
    tab_out[pl.ds(me, 1)] = tab_ref[pl.ds(pl.multiple_of(me * own_blocks, 8), own_blocks)][None]
    for slot, other in enumerate((mate, across, diagonal)):
        tab_out[pl.ds(other, 1)] = tab_land[slot][None]


def gather_project(tokens, table, query_weight, key_weight, value_weight, biases):
    rows, features = tokens.shape
    own_blocks = rows // BLK
    copies = 4 + 1 + 4
    return pl.pallas_call(
        functools.partial(gather_kernel, rows, 128),
        out_shape=(
            jax.ShapeDtypeStruct((rows, features), BF16),
            jax.ShapeDtypeStruct((4 * rows, features), BF16),
            jax.ShapeDtypeStruct((4 * rows, features), BF16),
            jax.ShapeDtypeStruct((rows, features), BF16),
            jax.ShapeDtypeStruct((4, own_blocks, 128), jnp.int32),
        ),
        in_specs=[whole_vmem()] * 6,
        out_specs=(whole_vmem(),) * 5,
        scratch_shapes=[
            VMEM((3, rows, features), BF16),
            VMEM((3, own_blocks, 128), jnp.int32),
            pltpu.SemaphoreType.DMA((copies,)),
            pltpu.SemaphoreType.DMA((copies,)),
            pltpu.SemaphoreType.DMA((3,)),
            pltpu.SemaphoreType.DMA((3,)),
        ],
        compiler_params=pltpu.CompilerParams(
            collective_id=0, has_side_effects=True, vmem_limit_bytes=LIMIT
        ),
        name="gather_project",
    )(tokens, table, query_weight, key_weight, value_weight, biases)


def key_blocks(tab_ref, end, pair, i, at, own_blocks, last_row):
    def chosen(head, t):
        group, inner = lax.div(head, 3), lax.rem(head, 3)
        return tab_ref[(group * own_blocks + i) * 128 + inner * 3 + t]

    head = 2 * pair
    both = [(chosen(head, t), chosen(head + 1, t)) for t in range(3)]
    shared = [
        jnp.maximum(at - 1, 0), at, jnp.minimum(at + 1, last_row), jnp.int32(0), end,
    ]
    return shared, both


def rows_of(block):
    return pl.ds(pl.multiple_of(block * BLK, BLK), BLK)


def lanes_low(rows):
    return lax.broadcasted_iota(jnp.int32, (rows, PAIR), 1) < HEAD_DIM


def split_pair(x, low):
    zero = jnp.zeros_like(x)
    return jnp.concatenate([jnp.where(low, x, zero), jnp.where(low, zero, x)], axis=0)


def gathered(ref, shared, both, low, lanes=slice(None)):
    tiles = [ref[b, :, lanes] for b in shared]
    for first, second in both:
        tiles.append(jnp.where(low, ref[first, :, lanes], ref[second, :, lanes]))
    return jnp.concatenate(tiles, axis=0)


def masked_scores(scores, mask_ref, i):
    parts = [scores[n * BLK:(n + 1) * BLK] + mask_ref[i * 8 + n] for n in range(5)]
    return jnp.concatenate(parts + [scores[5 * BLK:]], axis=0)


def forward_kernel(own_blocks, tab_ref, filled_ref, mask_ref, q_ref, k_ref, v_ref, out_ref, lse_ref):
    pair = pl.program_id(0)
    filled = filled_ref[0]
    first_block = lax.axis_index("seq") * own_blocks
    last_row = k_ref.shape[0] - 1
    low = lanes_low(BLK)

    def step(i, _):
        at = first_block + i
        shared, both = key_blocks(tab_ref, filled - 1, pair, i, at, own_blocks, last_row)
        keys = gathered(k_ref, shared, both, low)
        values = gathered(v_ref, shared, both, low)
        query = split_pair(q_ref[rows_of(i), :], low)
        scores = masked_scores(dot_nt(keys, query), mask_ref, i)
        highest = jnp.max(scores, axis=0, keepdims=True)
        weights = jnp.exp(scores - highest)
        total = jnp.sum(weights, axis=0, keepdims=True)
        share = (weights * (1.0 / total)).astype(BF16)
        output = dot_tn(share, values)
        merged = jnp.where(low, output[:BLK], output[BLK:])
        merged = jnp.where(at < filled, merged, 0.0)
        out_ref[rows_of(i), :] = merged.astype(BF16)
        lse_ref[0, pl.ds(i, 1), :] = highest + jnp.log(total)
        return 0

    lax.fori_loop(0, own_blocks, step, 0, unroll=own_blocks)


def attention_forward(table, filled, mask, query, keys, values):
    rows, features = query.shape
    own_blocks = rows // BLK
    slot_blocks = keys.shape[0]
    pairs = features // PAIR
    column = lambda n: pl.BlockSpec((n, PAIR), lambda p, *_: (0, p))
    blocks = lambda n: pl.BlockSpec((n, BLK, PAIR), lambda p, *_: (0, 0, p))
    return pl.pallas_call(
        functools.partial(forward_kernel, own_blocks),
        out_shape=(
            jax.ShapeDtypeStruct((rows, features), BF16),
            jax.ShapeDtypeStruct((pairs, own_blocks, PAIR), F32),
        ),
        grid_spec=pltpu.PrefetchScalarGridSpec(
            num_scalar_prefetch=3,
            grid=(pairs,),
            in_specs=[column(rows), blocks(slot_blocks), blocks(slot_blocks)],
            out_specs=(column(rows), pl.BlockSpec((1, own_blocks, PAIR), lambda p, *_: (p, 0, 0))),
        ),
        compiler_params=pltpu.CompilerParams(vmem_limit_bytes=LIMIT),
        name="attention_forward",
    )(table, filled, mask, query, keys, values)


def backward_kernel(
    own_blocks, tab_ref, filled_ref, mask_ref, q_ref, k_ref, v_ref, g_ref, lse_ref,
    dq_ref, dk_ref, dv_ref, dk_sum, dv_sum,
):
    pair = pl.program_id(0)
    filled = filled_ref[0]
    first_block = lax.axis_index("seq") * own_blocks
    last_row = k_ref.shape[0] - 1
    low = lanes_low(BLK)
    dk_sum[...] = jnp.zeros_like(dk_sum)
    dv_sum[...] = jnp.zeros_like(dv_sum)

    def step(i, _):
        at = first_block + i
        shared, both = key_blocks(tab_ref, filled - 1, pair, i, at, own_blocks, last_row)
        keys = gathered(k_ref, shared, both, low)
        values = gathered(v_ref, shared, both, low)
        query = split_pair(q_ref[rows_of(i), :], low)
        grad = split_pair(jnp.where(at < filled, g_ref[rows_of(i), :], jnp.zeros((), BF16)), low)
        scores = masked_scores(dot_nt(keys, query), mask_ref, i)
        share = jnp.exp(scores - lse_ref[0, pl.ds(i, 1), :])
        d_share = dot_nt(values, grad)
        centre = jnp.sum(share * d_share, axis=0, keepdims=True)
        d_scores = (share * (d_share - centre)).astype(BF16)
        d_query = dot_tn(d_scores, keys) * SCALE
        dq_ref[rows_of(i), :] = jnp.where(low, d_query[:BLK], d_query[BLK:]).astype(BF16)
        for total, part in ((dk_sum, dot(d_scores, query)), (dv_sum, dot(share.astype(BF16), grad))):
            for slot, block in enumerate(shared):
                total[rows_of(block), :] += part[slot * BLK:(slot + 1) * BLK]
            for t, (one, two) in enumerate(both):
                tile = part[(5 + t) * BLK:(6 + t) * BLK]
                total[rows_of(one), :] += jnp.where(low, tile, 0.0)
                total[rows_of(two), :] += jnp.where(low, 0.0, tile)
        return 0

    lax.fori_loop(0, own_blocks, step, 0, unroll=own_blocks)
    dk_ref[...] = dk_sum[...].astype(BF16)
    dv_ref[...] = dv_sum[...].astype(BF16)


def attention_backward(table, filled, mask, query, keys, values, grad, lse):
    rows, features = query.shape
    slot_blocks = keys.shape[0]
    slot_rows = slot_blocks * BLK
    own_blocks = rows // BLK
    pairs = features // PAIR
    blocks = lambda n: pl.BlockSpec((n, BLK, PAIR), lambda p, *_: (0, 0, p))
    column = lambda n: pl.BlockSpec((n, PAIR), lambda p, *_: (0, p))
    return pl.pallas_call(
        functools.partial(backward_kernel, own_blocks),
        out_shape=(
            jax.ShapeDtypeStruct((rows, features), BF16),
            jax.ShapeDtypeStruct((slot_rows, features), BF16),
            jax.ShapeDtypeStruct((slot_rows, features), BF16),
        ),
        grid_spec=pltpu.PrefetchScalarGridSpec(
            num_scalar_prefetch=3,
            grid=(pairs,),
            in_specs=[
                column(rows), blocks(slot_blocks), blocks(slot_blocks), column(rows),
                pl.BlockSpec((1, own_blocks, PAIR), lambda p, *_: (p, 0, 0)),
            ],
            out_specs=(column(rows), column(slot_rows), column(slot_rows)),
            scratch_shapes=[VMEM((slot_rows, PAIR), F32), VMEM((slot_rows, PAIR), F32)],
        ),
        compiler_params=pltpu.CompilerParams(vmem_limit_bytes=LIMIT),
        name="attention_backward",
    )(table, filled, mask, query, keys, values, grad, lse)


def exchange_kernel(
    rows, width, dk_ref, dv_ref, dq_ref, base_ref, wq_ref, wk_ref, wv_ref,
    dx_ref, dko_ref, dvo_ref, dkr_ref, dvr_ref,
    land, out_far, in_far, sends, recvs,
):
    dp, me = lax.axis_index("dp"), lax.axis_index("seq")
    mate, across, diagonal = (lax.bitwise_xor(me, bit) for bit in (1, 2, 3))
    barrier = pltpu.get_barrier_semaphore()
    for other in (mate, across):
        pl.semaphore_signal(barrier, inc=1, device_id=(dp, other), device_id_type=MESH)
    pl.semaphore_wait(barrier, 2)

    def send(src, dst, slot, target):
        copy = pltpu.make_async_remote_copy(
            src_ref=src, dst_ref=dst, send_sem=sends.at[slot], recv_sem=recvs.at[slot],
            device_id=(dp, target), device_id_type=MESH,
        )
        copy.start()
        return copy

    def owned(index):
        return pl.ds(pl.multiple_of(index * rows, rows), rows)

    copies = [
        send(ref.at[owned(owner)], land.at[slot], slot, mate)
        for slot, (ref, owner) in enumerate(
            ((dk_ref, diagonal), (dv_ref, diagonal), (dk_ref, mate), (dv_ref, mate))
        )
    ]

    def summed(ref, owner, slot, to_ref):
        to_ref[...] = (ref[owned(owner), :].astype(F32) + land[slot].astype(F32)).astype(BF16)

    copies[0].wait()
    summed(dk_ref, across, 0, dkr_ref)
    copies[1].wait()
    summed(dv_ref, across, 1, dvr_ref)

    steps = rows // width
    for r in range(steps):
        at = pl.ds(r * width, width)
        out_far[at, :] = (
            dot_nt(dkr_ref[at, :], wk_ref[...]) + dot_nt(dvr_ref[at, :], wv_ref[...])
        ).astype(BF16)
    far = send(out_far, in_far, 4, across)
    copies[2].wait()
    summed(dk_ref, me, 2, dko_ref)
    copies[3].wait()
    summed(dv_ref, me, 3, dvo_ref)

    def one(r, _):
        at = pl.ds(pl.multiple_of(r * width, width), width)
        dx_ref[at, :] = (
            base_ref[at, :]
            + dot_nt(dq_ref[at, :], wq_ref[...])
            + dot_nt(dko_ref[at, :], wk_ref[...])
            + dot_nt(dvo_ref[at, :], wv_ref[...])
        )
        return 0

    lax.fori_loop(0, steps, one, 0)
    far.wait()
    dx_ref[...] += in_far[...].astype(F32)


def exchange(d_keys, d_values, d_query, base, query_weight, key_weight, value_weight):
    rows, features = d_query.shape
    small = jax.ShapeDtypeStruct((rows, features), BF16)
    return pl.pallas_call(
        functools.partial(exchange_kernel, rows, 128),
        out_shape=(jax.ShapeDtypeStruct((rows, features), F32), small, small, small, small),
        in_specs=[whole_vmem()] * 7,
        out_specs=(whole_vmem(),) * 5,
        scratch_shapes=[
            VMEM((4, rows, features), BF16),
            VMEM((rows, features), BF16),
            VMEM((rows, features), BF16),
            pltpu.SemaphoreType.DMA((5,)),
            pltpu.SemaphoreType.DMA((5,)),
        ],
        compiler_params=pltpu.CompilerParams(
            collective_id=1, has_side_effects=True, vmem_limit_bytes=LIMIT
        ),
        name="exchange",
    )(d_keys, d_values, d_query, base, query_weight, key_weight, value_weight)


def summed_anywhere(square, up, down, vectors, up_bias):
    def one(g):
        return lax.psum_scatter(g, ("dp", "seq"), scatter_dimension=0, tiled=True)

    return [one(g) for g in square], one(up), one(down), [one(v) for v in vectors], one(up_bias)


GELU_A = 0.044715
GELU_C = 0.7978845608028654
UNIT = (48, 384)
KINDS = "ABACABBCBABB"
AXES = {"A": "yxz", "B": "xyz", "C": "zxy"}
DOWN, UP, SQUARE = 0, 4, 8
BETWEEN = (
    (),
    ((0, 0), (2, 0)),
    ((3, 0), (1, 1)),
    ((5, 0), (6, 0), (4, 0)),
    ((7, 0), (11, 0), (0, 1), (2, 1)),
    ((3, 1), (1, 2)),
)
AFTER = ((5, 1), (6, 1), (4, 1), (7, 1), (11, 1), (0, 2), (2, 2), (3, 2))
LAST = (
    (5, 2), (6, 2), (4, 2), (7, 2), (11, 2), (9, 0), (10, 0), (8, 0), (9, 1), (10, 1), (8, 1),
    (9, 2), (10, 2), (8, 2),
)


def normed_rows(values):
    center = jnp.mean(values, axis=-1, keepdims=True)
    centered = values - center
    variance = jnp.mean(centered * centered, axis=-1, keepdims=True)
    inv_root = lax.rsqrt(variance + NORM_EPS)
    return centered * inv_root, inv_root


def norm_pull(grad_out, normed, inv_root, gain):
    d_normed = grad_out * gain
    return inv_root * (
        d_normed
        - jnp.mean(d_normed, axis=-1, keepdims=True)
        - normed * jnp.mean(d_normed * normed, axis=-1, keepdims=True)
    )


def column_sum(values):
    return jnp.sum(values, axis=0, keepdims=True)


def masks(filled, seq, own_blocks):
    at = seq * own_blocks + jnp.arange(own_blocks, dtype=jnp.int32)[:, None]
    kind = jnp.arange(8, dtype=jnp.int32)[None, :]
    window = at + kind - 1
    ok = jnp.where(
        kind < 3, (window >= 0) & (window < filled),
        jnp.where(kind == 3, at >= 2, jnp.abs(at - (filled - 1)) > 1))
    last = jnp.arange(4 * own_blocks, dtype=jnp.int32) == filled - 1
    return jnp.concatenate([jnp.where(ok, 0.0, MASKED).astype(F32).reshape(-1), last.astype(F32)])


def links(table, filled, own_blocks):
    mine = table.reshape(4, own_blocks, 128)[:, :, :9].reshape(4, own_blocks, 3, 3)
    blocks = mine.transpose(0, 2, 1, 3).reshape(12, own_blocks * 3)
    count = blocks.shape[1]
    at = jnp.arange(count, dtype=jnp.int32)
    same = (blocks[:, :, None] == blocks[:, None, :]) & (at[None, None, :] < at[None, :, None])
    before = jnp.max(jnp.where(same, at[None, None, :], -1), axis=2)
    where = jnp.arange(32, dtype=jnp.int32)[None, :, None] == blocks[:, None, :]
    tail = jnp.max(jnp.where(where, at[None, None, :], -1), axis=2)
    both = jnp.concatenate([before.reshape(-1), tail.reshape(-1)])
    return jnp.concatenate([jnp.where(both < 0, count, both), (filled - 1)[None]])


def layer_kernel(
    rows, tile, own_blocks, groups, tab_ref, link_ref, mask_ref, bias_ref, bu_ref, lse_ref,
    x_any, merged_any, cot_any, wo_any, wu_any, wd_any, q_any, k_any, v_any, wk_any, wv_any, wq_any,
    far_any,
    result_ref, dx_ref, gq_ref, gk_ref, gv_ref, go_ref, up_ref, down_ref, vec_ref,
    work, land, core_down, core_up, core_out, pair_in, in_far, small, small_in, small_z,
    x_ref, merged_ref, d_attn_ref, d_merged_ref,
    loads, sends, recvs, c_sends, c_recvs, p_sends, p_recvs, s_sends, s_recvs, far_sems,
):
    features = x_ref.shape[1]
    hidden = bu_ref.shape[1]
    wide = hidden // features
    pairs = features // PAIR
    picks_count = own_blocks * 3
    share = features // (8 * groups)
    shards = 4 * groups
    half = features // 2
    dp, seq = lax.axis_index("dp"), lax.axis_index("seq")
    x, z = lax.rem(dp, 2), dp // 2
    core, y = lax.rem(seq, 2), seq // 2
    mate, across, diagonal = (lax.bitwise_xor(seq, bit) for bit in (1, 2, 3))
    end = link_ref[2 * pairs * (picks_count + 4 * own_blocks)]
    first_block = seq * own_blocks
    low = lanes_low(BLK)
    to_mate, to_y = (dp, mate), (dp, across)
    place_of = {"x": (x, 2), "y": (y, 2), "z": (z, groups)}

    def device(axis, index):
        if axis == "x":
            return (2 * z + index, seq)
        if axis == "y":
            return (dp, 2 * index + core)
        return (2 * index + x, seq)

    neighbours = [to_mate, to_y, device("x", 1 - x)] + [
        device("z", lax.rem(z + step, groups)) for step in range(1, groups)]

    loading = {}

    def load(name, src, dst):
        copy = pltpu.make_async_copy(src, dst, loads.at[len(loading)])
        copy.start()
        loading[name] = copy

    def remote(src, dst, one, two, target):
        return pltpu.make_async_remote_copy(
            src_ref=src, dst_ref=dst, send_sem=one, recv_sem=two, device_id=target,
            device_id_type=MESH,
        )

    def lanes_of(p):
        return pl.ds(pl.multiple_of(p * PAIR, PAIR), PAIR)

    def columns(j):
        return pl.ds(pl.multiple_of(j * features, features), features)

    def tiles(body):
        def step(r, _):
            body(pl.ds(pl.multiple_of(r * tile, tile), tile), r)
            return 0

        lax.fori_loop(0, rows // tile, step, 0)


    def index_of(u, at_x, at_y, at_z):
        at = {"x": at_x, "y": at_y, "z": at_z}
        flat = 0
        for axis in AXES[KINDS[u]]:
            flat = flat * place_of[axis][1] + at[axis]
        return flat

    def shard_of(s):
        return s // 4, lax.rem(s // 2, 2), lax.rem(s, 2)

    def stage_of(u, stage):
        sizes = [place_of[axis][1] for axis in AXES[KINDS[u]]] + [1]
        base, offset, sem, block = 0, 0, 0, shards
        for n, axis in enumerate(AXES[KINDS[u]]):
            block = block // sizes[n]
            if n == stage:
                return axis, place_of[axis][0], sizes[n], block, base, offset, sem
            base = base + place_of[axis][0] * block
            offset += (sizes[n] - 1) * block
            sem += sizes[n] - 1
        return None

    def stage_copies(u, stage):
        axis, mine, size, block, base, offset, sem = stage_of(u, stage)
        copies = []
        for step in range(1, size):
            index = lax.rem(mine + step, size)
            copies.append(remote(
                work.at[u, pl.ds(base + index * block, block)],
                land.at[u, pl.ds(offset + (step - 1) * block, block)],
                sends.at[u, sem + step - 1], recvs.at[u, sem + step - 1], device(axis, index)))
        return copies

    def begin(u, stage):
        for copy in stage_copies(u, stage):
            copy.start()

    def finish(u, stage):
        _, mine, size, block, base, offset, _ = stage_of(u, stage)
        for copy in stage_copies(u, stage):
            copy.wait()

        def total(r):
            value = work[u, base + mine * block + r].astype(F32)
            for step in range(size - 1):
                value = value + land[u, offset + step * block + r].astype(F32)
            return value

        if stage < 2:
            def body(r, _):
                work[u, base + mine * block + r] = total(r).astype(BF16)
                return 0

            lax.fori_loop(0, block, body, 0)
            begin(u, stage + 1)
            return
        value = total(0)
        if u < UP:
            down_ref[(u // 2) * UNIT[0]:(u // 2 + 1) * UNIT[0], (u % 2) * half:(u % 2 + 1) * half] = value
        else:
            to = up_ref if u < SQUARE else (gq_ref, gk_ref, gv_ref, go_ref)[u - SQUARE]
            at = (u - UP) * features if u < SQUARE else 0
            to[:, at:at + half] = value[:share]
            to[:, at + half:at + features] = value[share:]

    def folded(source, at, count):
        return jnp.concatenate(
            [source[pl.ds(at, count), 0:half], source[pl.ds(at, count), half:features]], axis=0)

    def square_pieces(u, source, other):
        def body(s, _):
            at_z, at_x, at_y = shard_of(s)
            index = index_of(u, at_x, at_y, at_z)
            for own in (True, False):
                row = 2 * s + (core if own else 1 - core)
                value = folded(source, pl.multiple_of(row * share, 8), share).astype(BF16)
                if own:
                    work[u, index] = value
                else:
                    other[index // 4, lax.rem(index, 4)] = value
            return 0

        lax.fori_loop(0, shards, body, 0)

    def add_core(u, landed):
        def body(n, _):
            work[u, n] = (
                work[u, n].astype(F32) + landed[n // 4, lax.rem(n, 4)].astype(F32)
            ).astype(BF16)
            return 0

        lax.fori_loop(0, shards, body, 0)

    def core_copy(src, dst, slot):
        return remote(src, dst, c_sends.at[slot], c_recvs.at[slot], to_mate)

    load("x", x_any, x_ref)
    load("merged", merged_any, merged_ref)


    def dense(
        wo, wu, wd, cot_ref, normed_one, root_one, first_low, act, slope, ffn, d_ffn, tmp,
        other_down, other_up,
    ):
        load("wo", wo_any, wo)
        load("wu", wu_any, wu)
        load("wd", wd_any, wd)
        load("cot", cot_any, cot_ref)
        barrier = pltpu.get_barrier_semaphore()
        for target in neighbours:
            pl.semaphore_signal(barrier, inc=1, device_id=target, device_id_type=MESH)
        pl.semaphore_wait(barrier, len(neighbours))
        bo, g1, s1, bd, g2, s2 = (bias_ref.at[n:n + 1, :] for n in range(2, 8))

        for name in ("x", "merged", "wo"):
            loading[name].wait()
        ffn[...] = dot(merged_ref[...], wo[...])

        def norm_one(at, r):
            normed, inv_root = normed_rows(x_ref[at, :].astype(F32) + (ffn[at, :] + bo[...]))
            normed_one[at, :] = normed
            root_one[at, :] = inv_root
            first_low[at, :] = (normed * g1[...] + s1[...]).astype(BF16)

        tiles(norm_one)

        loading["wu"].wait()
        loading["wd"].wait()
        ffn[...] = jnp.zeros_like(ffn)

        def forward(j, _):
            at = columns(j)
            u = dot(first_low[...], wu[:, at]) + bu_ref[:, at]
            square = u * u
            t = jnp.tanh(GELU_C * (u + GELU_A * (square * u)))
            upper = 0.5 * (1.0 + t)
            act[j] = (u * upper).astype(BF16)
            slope[j] = (
                upper + (0.5 * GELU_C) * u * (1.0 - t * t) * (1.0 + (3.0 * GELU_A) * square)
            ).astype(slope.dtype)
            ffn[...] += dot(act[j], wd[at, :])
            return 0

        lax.fori_loop(0, wide, forward, 0)

        small[...] = jnp.zeros_like(small)
        limit = (end + 1) * BLK - seq * rows
        loading["cot"].wait()

        def norm_two(at, r):
            first = normed_one[at, :] * g1[...] + s1[...]
            normed, inv_root = normed_rows(first + (ffn[at, :] + bd[...]))
            result_ref[at, :] = (normed * g2[...] + s2[...]).astype(BF16)
            place = lax.broadcasted_iota(jnp.int32, (tile, 1), 0) + r * tile
            grad = cot_ref[at, :].astype(F32) * (place < limit).astype(F32)
            pulled = norm_pull(grad, normed, inv_root, g2[...])
            rounded = pulled.astype(BF16)
            ffn[at, :] = pulled
            d_ffn[at, :] = rounded
            small[0:1, :] += column_sum(grad * normed)
            small[1:2, :] += column_sum(grad)
            small[2:3, :] += column_sum(rounded.astype(F32))

        tiles(norm_two)

        down_copies = []
        for j in range(wide):
            tmp[...] = dot_tn(act[j], d_ffn[...])

            def pieces(n, _):
                at_x, at_y = n // 2, lax.rem(n, 2)
                for own in (True, False):
                    row = 2 * n + (core if own else 1 - core)
                    at = pl.multiple_of(row * (wide * share), 8)
                    for u in range(4):
                        value = tmp[
                            pl.ds(pl.multiple_of(at + (u // 2) * UNIT[0], 8), UNIT[0]),
                            (u % 2) * half:(u % 2 + 1) * half].astype(BF16)
                        if own:
                            work[u, index_of(u, at_x, at_y, j)] = value
                        else:
                            other_down[j, u, n] = value
                return 0

            lax.fori_loop(0, 4, pieces, 0)
            down_copies.append(core_copy(other_down.at[j], core_down.at[j], j))
            down_copies[-1].start()

        def backward(j, _):
            d_hidden = (dot_nt(d_ffn[...], wd[columns(j), :]) * slope[j].astype(F32)).astype(BF16)
            act[j] = d_hidden
            for n in range(wide):
                @pl.when(j == n)
                def _():
                    small[8 + n:9 + n, :] = column_sum(d_hidden.astype(F32))
            return 0

        lax.fori_loop(0, wide, backward, 0)

        for copy in down_copies:
            copy.wait()

        def sum_down(s, _):
            at_z, at_x, at_y = shard_of(s)
            for u in range(4):
                index = index_of(u, at_x, at_y, at_z)
                work[u, index] = (
                    work[u, index].astype(F32) + core_down[at_z, u, at_x * 2 + at_y].astype(F32)
                ).astype(BF16)
            return 0

        lax.fori_loop(0, shards, sum_down, 0)
        for u in range(4):
            begin(u, 0)

        up_copies = []
        for j in range(wide):
            tmp[...] = dot_tn(first_low[...], act[j])
            square_pieces(UP + j, tmp, other_up.at[j])
            up_copies.append(core_copy(other_up.at[j], core_up.at[j], wide + j))
            up_copies[-1].start()

        for j in range(wide):
            ffn[...] += dot_nt(act[j], wu[:, j * features:(j + 1) * features])
        for j in range(wide):
            up_copies[j].wait()
            add_core(UP + j, core_up.at[j])
            begin(UP + j, 0)
        finish(1, 0)

        def pull_one(at, r):
            grad = ffn[at, :]
            normed = normed_one[at, :]
            pulled = norm_pull(grad, normed, root_one[at, :], g1[...])
            rounded = pulled.astype(BF16)
            dx_ref[at, :] = pulled
            d_attn_ref[at, :] = rounded
            small[3:4, :] += column_sum(grad * normed)
            small[4:5, :] += column_sum(grad)
            small[5:6, :] += column_sum(rounded.astype(F32))

        tiles(pull_one)
        live = lax.broadcasted_iota(jnp.int32, (rows, 1), 0) < limit
        d_merged_ref[...] = jnp.where(live, dot_nt(d_attn_ref[...], wo[...]), 0.0).astype(BF16)

    low_rows = VMEM((rows, features), BF16)
    full_rows = VMEM((rows, features), F32)
    square_low = VMEM((features, features), BF16)
    pl.run_scoped(
        dense, square_low, VMEM((features, hidden), BF16), VMEM((hidden, features), BF16),
        low_rows, full_rows, VMEM((rows, 1), F32), low_rows, VMEM((wide, rows, features), BF16),
        VMEM((wide, rows, features), SLOPE), full_rows, low_rows, VMEM((features, features), F32),
        VMEM((4, 4, 4) + UNIT, BF16), VMEM((4, 4, 4) + UNIT, BF16),
    )


    def attention(
        k_ref, v_ref, q_ref, dq_ref, far_ref, wk, wv, wq, acc, last, picked, buf, dko, dvo, dkr,
        dvr, out_far, other, tmp,
    ):
        for name, src, dst in (
            ("q", q_any, q_ref), ("k", k_any, k_ref), ("v", v_any, v_ref), ("wk", wk_any, wk),
            ("wv", wv_any, wv), ("wq", wq_any, wq), ("far", far_any, far_ref),
        ):
            load(name, src, dst)
        square_copies = {
            u: core_copy(other.at[u - SQUARE],
                         core_out if u == SQUARE + 3 else core_down.at[u - SQUARE], u)
            for u in range(SQUARE, SQUARE + 4)
        }

        def square(u, source):
            square_pieces(u, source, other.at[u - SQUARE])
            square_copies[u].start()

        def end_square(u):
            square_copies[u].wait()
            add_core(u, core_out if u == SQUARE + 3 else core_down.at[u - SQUARE])
            begin(u, 0)

        def copy_pair(p, slot, owner):
            return remote(buf.at[p, owner], pair_in.at[p, slot], p_sends.at[p, slot],
                          p_recvs.at[p, slot], to_mate)

        def sum_pair(p):
            lanes = lanes_of(p)
            for slot, owner, keys_to, values_to in ((0, across, dkr, dvr), (1, seq, dko, dvo)):
                copy_pair(p, slot, diagonal if slot == 0 else mate).wait()
                for n, to in ((0, keys_to), (1, values_to)):
                    to[:, lanes] = (
                        buf[p, owner, n].astype(F32) + pair_in[p, slot, n].astype(F32)
                    ).astype(BF16)

        def heads():
            for n in range(2):
                picked[n, picks_count] = jnp.zeros((BLK, PAIR), F32)
            last_row = k_ref.shape[0] - 1
            for name in ("q", "k", "v"):
                loading[name].wait()

            def one_pair(p, _):
                lanes = lanes_of(p)
                acc[...] = jnp.zeros_like(acc)
                last[...] = jnp.zeros_like(last)

                def step(i, _):
                    at = first_block + i
                    shared, both = key_blocks(tab_ref, end, p, i, at, own_blocks, last_row)
                    keys = gathered(k_ref, shared, both, low, lanes)
                    values = gathered(v_ref, shared, both, low, lanes)
                    query = split_pair(q_ref[rows_of(i), lanes], low)
                    grad = split_pair(d_merged_ref[rows_of(i), lanes], low)
                    scores = masked_scores(dot_nt(keys, query), mask_ref, i)
                    share_of = jnp.exp(scores - lse_ref[p, pl.ds(i, 1), :])
                    d_share = dot_nt(values, grad)
                    centre = jnp.sum(share_of * d_share, axis=0, keepdims=True)
                    d_scores = (share_of * (d_share - centre)).astype(BF16)
                    d_query = dot_tn(d_scores, keys) * SCALE
                    dq_ref[rows_of(i), lanes] = jnp.where(
                        low, d_query[:BLK], d_query[BLK:]).astype(BF16)
                    parts = (dot(d_scores, query), dot(share_of.astype(BF16), grad))
                    for n, part in enumerate(parts):
                        for slot in range(3):
                            acc[n, rows_of(at + slot), :] += part[slot * BLK:(slot + 1) * BLK]
                        acc[n, BLK:2 * BLK, :] += part[3 * BLK:4 * BLK]
                        last[n] += part[4 * BLK:5 * BLK]
                    for t in range(3):
                        one = link_ref[2 * p * picks_count + i * 3 + t]
                        two = link_ref[(2 * p + 1) * picks_count + i * 3 + t]
                        for n, part in enumerate(parts):
                            picked[n, i * 3 + t] = part[(5 + t) * BLK:(6 + t) * BLK] + jnp.where(
                                low, picked[n, one], picked[n, two])
                    return 0

                lax.fori_loop(0, own_blocks, step, 0, unroll=own_blocks)
                tails = 2 * pairs * picks_count

                def gather(owner, _):
                    for inner in range(own_blocks):
                        block = owner * own_blocks + inner
                        one = link_ref[tails + 2 * p * (last_row + 1) + block]
                        two = link_ref[tails + (2 * p + 1) * (last_row + 1) + block]
                        for n in range(2):
                            total = acc[n, rows_of(block + 1), :]
                            total = total + jnp.where(low, picked[n, one], picked[n, two])
                            total = total + last[n] * mask_ref[own_blocks * 8 + block]
                            buf[p, owner, n, inner * BLK:(inner + 1) * BLK] = total.astype(BF16)
                    return 0

                lax.fori_loop(0, 4, gather, 0)
                copy_pair(p, 0, diagonal).start()
                copy_pair(p, 1, mate).start()

                @pl.when(p > 0)
                def _():
                    sum_pair(p - 1)

                for n, events in enumerate(BETWEEN):
                    @pl.when(p == n)
                    def _():
                        if n == 0:
                            end_square(SQUARE + 3)
                        for u, stage in events:
                            finish(u, stage)

                return 0

            lax.fori_loop(0, pairs, one_pair, 0)

        tmp[...] = dot_tn(merged_ref[...], d_attn_ref[...])
        square(SQUARE + 3, tmp)
        heads()
        sum_pair(pairs - 1)

        loading["wk"].wait()
        loading["wv"].wait()
        out_far[...] = (dot_nt(dkr[...], wk[...]) + dot_nt(dvr[...], wv[...])).astype(BF16)
        far = remote(out_far, in_far, far_sems.at[0], far_sems.at[1], to_y)
        far.start()
        loading["wq"].wait()
        loading["far"].wait()

        tmp[...] = dot_tn(x_ref[...], dko[...]) + dot_tn(far_ref[...], dkr[...])
        square(SQUARE + 1, tmp)
        for u, stage in AFTER[:4]:
            finish(u, stage)
        tmp[...] = dot_tn(x_ref[...], dvo[...]) + dot_tn(far_ref[...], dvr[...])
        square(SQUARE + 2, tmp)
        end_square(SQUARE + 1)
        tmp[...] = dot_tn(x_ref[...], dq_ref[...])
        square(SQUARE, tmp)
        end_square(SQUARE + 2)
        for u, stage in AFTER[4:]:
            finish(u, stage)
        end_square(SQUARE)

        small[6:7, :] = column_sum(dq_ref[...].astype(F32))
        small[7:8, :] = column_sum(dvo[...].astype(F32)) + column_sum(dvr[...].astype(F32))

        def small_copies(stage):
            axis = ("core", "y", "x", "z")[stage]
            if axis == "z":
                return [
                    remote(small, small_z.at[step - 1], s_sends.at[2 + step], s_recvs.at[2 + step],
                           device("z", lax.rem(z + step, groups)))
                    for step in range(1, groups)
                ]
            target = {"core": to_mate, "y": to_y, "x": device("x", 1 - x)}[axis]
            return [remote(small, small_in.at[stage], s_sends.at[stage], s_recvs.at[stage], target)]

        def small_begin(stage):
            for copy in small_copies(stage):
                copy.start()

        def small_end(stage):
            for copy in small_copies(stage):
                copy.wait()
            if stage < 3:
                small[...] += small_in[stage]
                small_begin(stage + 1)
            else:
                total = small[...]
                for step in range(1, groups):
                    total = total + small_z[step - 1]
                vec_ref[...] = total

        small_begin(0)
        dx_ref[...] += (
            dot_nt(dq_ref[...], wq[...]) + dot_nt(dko[...], wk[...]) + dot_nt(dvo[...], wv[...])
        )
        for n, (u, stage) in enumerate(LAST):
            if n in (2, 5, 6, 8):
                small_end((2, 5, 6, 8).index(n))
            if n == 6:
                far.wait()
                dx_ref[...] += in_far[...].astype(F32)
            finish(u, stage)

    pl.run_scoped(
        attention, VMEM((4 * own_blocks, BLK, features), BF16),
        VMEM((4 * own_blocks, BLK, features), BF16), low_rows, low_rows, low_rows, square_low, square_low, square_low,
        VMEM((2, (4 * own_blocks + 2) * BLK, PAIR), F32), VMEM((2, BLK, PAIR), F32),
        VMEM((2, picks_count + 1, BLK, PAIR), F32), VMEM((pairs, 4, 2, rows, PAIR), BF16),
        low_rows, low_rows, low_rows, low_rows, low_rows, VMEM((4, 4, 4) + UNIT, BF16),
        VMEM((features, features), F32),
    )


SLOPE = F32


def layer_tail(
    groups, table, link, mask, biases, up_bias, lse, tokens, merged, cotangent, out_weight,
    up_weight, down_weight, query, keys, values, key_weight, value_weight, query_weight, far_tokens,
):
    rows, features = tokens.shape
    hidden = up_weight.shape[1]
    own_blocks = rows // BLK
    pairs = features // PAIR
    share = features // (8 * groups)
    wide = hidden // features
    low = VMEM((rows, features), BF16)
    line = jax.ShapeDtypeStruct((share, features), F32)
    any_space = pl.BlockSpec(memory_space=pl.ANY)
    in_smem = pl.BlockSpec(memory_space=pltpu.SMEM)
    dma = pltpu.SemaphoreType.DMA
    return pl.pallas_call(
        functools.partial(layer_kernel, rows, 128, own_blocks, groups),
        out_shape=(
            jax.ShapeDtypeStruct((rows, features), BF16),
            jax.ShapeDtypeStruct((rows, features), F32), line, line, line, line,
            jax.ShapeDtypeStruct((share, hidden), F32),
            jax.ShapeDtypeStruct((wide * share, features), F32),
            jax.ShapeDtypeStruct((16, features), F32),
        ),
        in_specs=[in_smem] * 3 + [whole_vmem()] * 3 + [any_space] * 13,
        out_specs=(whole_vmem(),) * 9,
        scratch_shapes=[
            VMEM((12, 4 * groups) + UNIT, BF16),
            VMEM((12, 4 * groups - 1) + UNIT, BF16),
            VMEM((4, 4, 4) + UNIT, BF16),
            VMEM((4, 4, 4) + UNIT, BF16),
            VMEM((4, 4) + UNIT, BF16),
            VMEM((pairs, 2, 2, rows, PAIR), BF16),
            low,
            VMEM((16, features), F32),
            VMEM((3, 16, features), F32),
            VMEM((groups - 1, 16, features), F32),
            low, low, low, low,
            dma((13,)), dma((12, groups + 1)), dma((12, groups + 1)), dma((12,)), dma((12,)),
            dma((pairs, 2)), dma((pairs, 2)), dma((groups + 2,)), dma((groups + 2,)), dma((2,)),
        ],
        compiler_params=pltpu.CompilerParams(
            collective_id=3, has_side_effects=True, vmem_limit_bytes=LIMIT
        ),
        name="layer_tail",
    )(
        table, link, mask, biases, up_bias, lse, tokens, merged, cotangent, out_weight, up_weight,
        down_weight, query, keys, values, key_weight, value_weight, query_weight, far_tokens,
    )


def layer_norm(values, gain, shift):
    center = jnp.mean(values, axis=-1, keepdims=True)
    centered = values - center
    variance = jnp.mean(centered * centered, axis=-1, keepdims=True)
    inv_root = lax.rsqrt(variance + NORM_EPS)
    normed = centered * inv_root
    return (normed * gain + shift, normed, inv_root)


def norm_back(grad_out, normed, inv_root, gain):
    d_normed = grad_out * gain
    grad_in = inv_root * (
        d_normed
        - jnp.mean(d_normed, axis=-1, keepdims=True)
        - normed * jnp.mean(d_normed * normed, axis=-1, keepdims=True)
    )
    return (grad_in, jnp.sum(grad_out * normed, axis=0), jnp.sum(grad_out, axis=0))


def on_device(
    groups,
    tokens, filled_blocks, random_blocks, query_weight, query_bias, key_weight, value_weight,
    value_bias, out_weight, out_bias, attn_gain, attn_shift, up_weight, up_bias, down_weight,
    down_bias, ffn_gain, ffn_shift, cotangent,
):
    row_count, feature_count = tokens.shape
    filled = filled_blocks[0]
    place = lax.axis_index("seq") * row_count + jnp.arange(row_count, dtype=jnp.int32)
    live_tokens = (place < filled * BLK).astype(F32)[:, None]

    table = random_blocks[0].reshape(random_blocks.shape[1], -1)
    table = jnp.pad(table, ((0, 0), (0, 128 - table.shape[1])))
    biases = jnp.stack([
        query_bias, value_bias, out_bias, attn_gain, attn_shift, down_bias, ffn_gain, ffn_shift])
    query, keys, values, far_tokens, table = gather_project(
        tokens, table, query_weight, key_weight, value_weight, biases
    )
    table = table.reshape(-1)
    mask = masks(filled, lax.axis_index("seq"), row_count // BLK)
    keys, values = (t.reshape(-1, BLK, feature_count) for t in (keys, values))
    merged, lse = attention_forward(table, filled_blocks, mask, query, keys, values)

    if groups:
        seq = lax.axis_index("seq")
        result, grad_tokens, gq, gk, gv, go, up, down, vectors = layer_tail(
            groups, table, links(table, filled, row_count // BLK), mask, biases, up_bias[None], lse,
            tokens, merged, cotangent, out_weight, up_weight, down_weight, query, keys, values,
            key_weight, value_weight, query_weight, far_tokens)
        shard = lax.axis_index("dp") * 4 + seq
        share = gq.shape[0]
        mine = lax.dynamic_slice(vectors, (0, shard * share), (8, share))
        wide = up.shape[1] // feature_count
        up_sum = lax.dynamic_slice(
            vectors[8:8 + wide].reshape(-1), (shard * wide * share,), (wide * share,))
        return (
            result, grad_tokens, gq, mine[6], gk, gv, mine[7], go, mine[5], mine[3], mine[4], up,
            up_sum, down, mine[2], mine[0], mine[1],
        )

    attn = dot(merged, out_weight) + out_bias
    first, normed_one, root_one = layer_norm(tokens.astype(F32) + attn, attn_gain, attn_shift)
    first_low = first.astype(BF16)
    hidden = dot(first_low, up_weight) + up_bias
    act, gelu_pull = jax.vjp(jax.nn.gelu, hidden)
    act_low = act.astype(BF16)
    ffn = dot(act_low, down_weight) + down_bias
    result, normed_two, root_two = layer_norm(first + ffn, ffn_gain, ffn_shift)
    grad_result = cotangent.astype(F32) * live_tokens
    d_sum_two, grad_ffn_gain, grad_ffn_shift = norm_back(
        grad_result, normed_two, root_two, ffn_gain
    )
    d_ffn = d_sum_two.astype(BF16)
    grad_down_bias = jnp.sum(d_ffn, axis=0, dtype=F32)
    grad_down_weight = dot_tn(act_low, d_ffn)
    d_act = dot_nt(d_ffn, down_weight)
    d_hidden = gelu_pull(d_act)[0].astype(BF16)
    grad_up_bias = jnp.sum(d_hidden, axis=0, dtype=F32)
    grad_up_weight = dot_tn(first_low, d_hidden)
    d_first = d_sum_two + dot_nt(d_hidden, up_weight)
    d_sum_one, grad_attn_gain, grad_attn_shift = norm_back(d_first, normed_one, root_one, attn_gain)
    d_attn = d_sum_one.astype(BF16)
    grad_out_bias = jnp.sum(d_attn, axis=0, dtype=F32)
    grad_out_weight = dot_tn(merged, d_attn)
    d_merged = dot_nt(d_attn, out_weight).astype(BF16)

    d_query, d_keys, d_values = attention_backward(
        table, filled_blocks, mask, query, keys, values, d_merged, lse
    )
    grad_tokens, dk_own, dv_own, dk_far, dv_far = exchange(
        d_keys, d_values, d_query, d_sum_one, query_weight, key_weight, value_weight
    )
    grad_query_weight = dot_tn(tokens, d_query)
    grad_query_bias = jnp.sum(d_query, axis=0, dtype=F32)
    grad_key_weight = dot_tn(tokens, dk_own) + dot_tn(far_tokens, dk_far)
    grad_value_weight = dot_tn(tokens, dv_own) + dot_tn(far_tokens, dv_far)
    grad_value_bias = jnp.sum(dv_own, axis=0, dtype=F32) + jnp.sum(dv_far, axis=0, dtype=F32)

    square = (grad_query_weight, grad_key_weight, grad_value_weight, grad_out_weight)
    vectors = (
        grad_query_bias, grad_value_bias, grad_out_bias, grad_attn_gain, grad_attn_shift,
        grad_down_bias, grad_ffn_gain, grad_ffn_shift,
    )
    square, up, down, vectors, up_sum = summed_anywhere(
        square, grad_up_weight, grad_down_weight, vectors, grad_up_bias)
    return (
        result.astype(BF16), grad_tokens, square[0], vectors[0], square[1], square[2], vectors[1],
        square[3], vectors[2], vectors[3], vectors[4], up, up_sum, down, vectors[5], vectors[6],
        vectors[7],
    )


def solution(mesh):
    both = P(("dp", "seq"), None)
    line = P(("dp", "seq"))
    placed = (both, P("dp"), P("dp", None, "seq", None)) + (P(),) * 15 + (both,)
    groups = 4 if mesh.shape["dp"] == 8 and mesh.shape["seq"] == 4 else 0
    return jax.shard_map(
        functools.partial(on_device, groups),
        mesh=mesh,
        in_specs=placed,
        out_specs=(
            both, both, both, line, both, both, line, both, line, line, line, both, line, both,
            line, line, line,
        ),
        check_vma=False,
    )
```

time: 347 us -> 184 us (0.53); the launches traced: 341 us -> 183 us
  Pallas kernels: 219 us -> 161 us
  matrix products: 43.7 us -> 0 us
  local copies, waits for them, and re-layouts: 55.1 us -> 18.1 us
  other arithmetic: 21.1 us -> 2.67 us
    dot_general x14 -> x0, matrix products: 43.7 us -> none  [the longest x8 18.7 us: dot_tn(): lax.dot_general(left, right, (((0,), (0,)), ((), ())), preferred_element_...]
    pallas_call x3 -> x1, Pallas kernels: 165 us -> 121 us  [layer_tail(): pl.pallas_call(functools.partial(layer_kernel, rows, 128, own_blocks, gro...]
    pallas_call x1, Pallas kernels: 26.3 us -> 11.8 us  [attention_forward(): pl.pallas_call(functools.partial(forward_kernel, own_blocks), out_shape=(...]
    reshape x5 -> x3, local copies, waits for them, and re-layouts: 14.1 us -> 0.17 us  [the longest x2 0.16 us: links(): both = jnp.concatenate([before.reshape(-1), tail.reshape(-1)])]
    reduce_sum x8 -> x0, other arithmetic: 10.3 us -> none  [the longest x1 3.89 us: on_device(): grad_down_bias = jnp.sum(d_ffn, axis=0, dtype=F32)]
    slice x3 -> x2, local copies, waits for them, and re-layouts: 10.1 us -> 1.55 us  [the longest x1 0.81 us: links(): table.reshape(4, own_blocks, 128)[:, :, :9].reshape(4, own_blocks, 3, 3)]
    unnamed x8 -> x1, other arithmetic: 7.28 us -> 0.71 us
    unnamed x95 -> x22, local copies, waits for them, and re-layouts: 11.8 us -> 7.19 us
where the time goes in v3:
time: 184 us; the launch traced here: 183 us
  Pallas kernels  161 us (88%)
  local copies, waits for them, and re-layouts  18.1 us (10%)
  other arithmetic  2.67 us (1%)
    pallas_call x1, Pallas kernels, layer_tail(): pl.pallas_call(functools.partial(layer_kernel, rows, 128, own_blocks, gro...  121 us
    pallas_call x1, Pallas kernels, gather_project(): pl.pallas_call(functools.partial(gather_kernel, rows, 128), out_shape=(ja...  27.9 us
    pallas_call x1, Pallas kernels, attention_forward(): pl.pallas_call(functools.partial(forward_kernel, own_blocks), out_shape=(...  11.8 us
    unnamed x22, local copies, waits for them, and re-layouts  7.19 us
    another operation x9, local copies, waits for them, and re-layouts, on_device(): jnp.stack([query_bias, value_bias, out_bias, attn_gain, attn_shift, down_...  6.16 us

profile of v3, /device:TPU:0, one launch (start us, length us, event | category | flops | bytes accessed | tf_op | source)
XLA Modules:
  0.0 183.4 jit_solution(5584955940651585680)
XLA Ops:
  1.4 0.1 fusion.4
  1.4 0.1 reshape.123
  1.5 0.6 pad_maximum_fusion.mask_ref
  2.1 0.7 stack.27
  2.8 0.7 stack.28
  3.5 0.7 stack.29
  4.2 0.7 stack.30
  4.9 0.7 stack.31
  5.6 0.7 stack.32
  6.3 0.7 stack.33
  6.9 0.7 stack.34
  7.6 0.6 stack.35.bias_ref
  8.3 0.7 reduce
  9.0 0.1 copy.40
  9.1 0.6 pad.4.tab_ref
  9.7 27.9 %gather_project.1 = (bf16[512,768]{1,0:T(8,128)(2,1)}, bf16[2048,768]{1,0:T(8,128)(2,1)}, bf16[2048,768]{1,0:T(8,128)(2,1)}, bf16[512,768]{1,0:T(8,128)(2,1)}, s32[4,8,128]{2,1,0:T(8,128)}) custom-call(bf16[512,768]{1,0:T(8,128)(2,1)} %x_any.1, s32[32,128]{1,0:T(8,128)} %pad.4.tab_ref, bf16[768,768]{1,0:T(8,128)(2,1)} %wq_any.1, bf16[768,768]{1,0:T(8,128)(2,1)} %wk_any.1, ...), custom_call_target="tpu_custom_call" | custom-call | tf_op jit(solution)/shard_map/gather_project/pallas_call | solution.py:125
  37.7 0.8 copy.41
  38.5 0.1 copy.42
  38.6 0.1 eq.42
  38.7 0.4 select_reduce_fusion.1
  39.1 0.1 reshape.115
  39.2 0.1 select_reduce_fusion
  39.3 0.1 reshape.116
  39.4 0.1 compare_select_fusion
  39.5 0.7 pad_add_fusion.link_ref
  40.1 11.8 %attention_forward.1 = (bf16[512,768]{1,0:T(8,128)(2,1)}, f32[6,8,128]{2,1,0:T(8,128)}) custom-call(s32[4096]{0:T(1024)} %bitcast.37, s32[1]{0:T(128)} %copy.52.filled_ref, f32[96]{0:T(128)} %pad_maximum_fusion.mask_ref, bf16[512,768]{1,0:T(8,128)(2,1)} %get-tuple-element.34.q_ref.q_any, bf16[32,64,768]{2,1,0:T(8,128)(2,1)} %bitcast.32, ...), custom_call_target="tpu_custom_call" | custom-call | tf_op jit(solution)/shard_map/attention_forward/pallas_call | solution.py:224
  51.9 121.5 %layer_tail.1 = (bf16[512,768]{1,0:T(8,128)(2,1)}, f32[512,768]{1,0:T(8,128)}, f32[24,768]{1,0:T(8,128)}, f32[24,768]{1,0:T(8,128)}, f32[24,768]{1,0:T(8,128)}, ...) custom-call(s32[4096]{0:T(1024)} %bitcast.38, s32[673]{0:T(1024)} %pad_add_fusion.link_ref, ...), custom_call_target="tpu_custom_call" | custom-call | tf_op jit(solution)/shard_map/layer_tail/pallas_call | solution.py:1001
  173.4 0.0 copy-start
  173.4 0.9 constant_dynamic-slice_fusion
  174.3 0.7 slice.36
  175.1 0.6 dynamic_slice.7
  175.7 0.5 slice_bitcast_fusion
  176.2 2.1 %copy.53 = bf16[512,768]{1,0:T(8,128)(2,1)} copy(bf16[512,768]{1,0:T(8,128)(2,1)} %get-tuple-element.78) | data formatting | bytes 1572864
  178.3 0.0 copy-done
  178.3 0.0 copy-start.3
  178.3 0.0 copy-start.2
  178.3 0.0 copy-start.1
  178.3 1.1 copy.54
  179.5 0.0 copy-done.6
  179.5 0.6 copy.55
  180.1 0.6 copy.56
  180.7 0.0 copy-done.4
  180.7 0.6 copy.57
  181.4 0.6 copy.58
  182.0 0.0 copy-done.2
  182.0 0.7 copy.59
  182.7 0.0 copy-done.1
  182.7 0.7 copy.60
  (12 shorter events, 0.1 us)
Async XLA Ops:
  173.4 4.9 %copy-start = (f32[512,768]{1,0:T(8,128)S(1)}, f32[512,768]{1,0:T(8,128)}, u32[]{:S(2)}) copy-start(f32[512,768]{1,0:T(8,128)} %get-tuple-element.79) | copy-start | bytes 4718596
  178.3 1.2 copy-start.6
  178.3 1.8 copy-start.5
  178.3 2.5 %copy-start.4 = (f32[24,768]{1,0:T(8,128)S(1)}, f32[24,768]{1,0:T(8,128)}, u32[]{:S(2)}) copy-start(f32[24,768]{1,0:T(8,128)} %get-tuple-element.83) | copy-start | bytes 221188
  178.3 3.1 %copy-start.3 = (f32[24,768]{1,0:T(8,128)S(1)}, f32[24,768]{1,0:T(8,128)}, u32[]{:S(2)}) copy-start(f32[24,768]{1,0:T(8,128)} %get-tuple-element.85) | copy-start | bytes 221188
  178.3 3.7 %copy-start.2 = (f32[24,3072]{1,0:T(8,128)S(1)}, f32[24,3072]{1,0:T(8,128)}, u32[]{:S(2)}) copy-start(f32[24,3072]{1,0:T(8,128)} %get-tuple-element.89) | copy-start | bytes 884740
  178.3 4.4 %copy-start.1 = (f32[96,768]{1,0:T(8,128)S(1)}, f32[96,768]{1,0:T(8,128)}, u32[]{:S(2)}) copy-start(f32[96,768]{1,0:T(8,128)} %get-tuple-element.91) | copy-start | bytes 884740

commit v4 on v3

--- a/solution.py
+++ b/solution.py
@@ -37,9 +37,47 @@
     return lax.dot_general(left, right, (((0,), (0,)), ((), ())), preferred_element_type=F32)
 
 
+def tables_of(tab_out, filled, first_block, each, prev_out, tail_out, mask_out):
+    groups, blocks, width = tab_out.shape
+    slot_blocks = tail_out.shape[1]
+    none = blocks * each
+    lane = lax.broadcasted_iota(jnp.int32, (blocks, width), 1)
+    row = lax.broadcasted_iota(jnp.int32, (blocks, width), 0)
+    pick = lax.rem(lane, each)
+    key_row = lax.broadcasted_iota(jnp.int32, (slot_blocks, width), 0)
+    key_pick = lax.rem(lax.broadcasted_iota(jnp.int32, (slot_blocks, width), 1), each)
+    for g in range(groups):
+        table = tab_out[g]
+        prev = jnp.full((blocks, width), -1, jnp.int32)
+        for shift in range(1 - each, each):
+            moved = pltpu.roll(table, (-shift) % width, axis=1)
+            inside = (pick + shift >= 0) & (pick + shift < each)
+            for i in range(blocks - 1):
+                same = (moved[i:i + 1] == table) & (row > i) & inside
+                prev = jnp.maximum(prev, jnp.where(same, i * each + pick + shift, -1))
+        prev = jnp.where(prev < 0, none, prev)
+        prev_out[g] = jnp.where(lane == width - 1, filled - 1, prev)
+        tail = jnp.full((slot_blocks, width), -1, jnp.int32)
+        for i in range(blocks):
+            tail = jnp.maximum(tail, jnp.where(table[i:i + 1] == key_row, i * each + key_pick, -1))
+        best = tail
+        for shift in range(1, each):
+            best = jnp.maximum(best, pltpu.roll(tail, width - shift, axis=1))
+        tail_out[g] = jnp.where(best < 0, none, best)
+    at = first_block + row
+    window = at + lane - 1
+    ok = jnp.where(
+        lane < 3, ((window >= 0) & (window < filled)).astype(jnp.int32),
+        jnp.where(lane == 3, (at >= 2).astype(jnp.int32),
+                  (jnp.abs(at - (filled - 1)) > 1).astype(jnp.int32)))
+    mask_out[0:blocks, :] = jnp.where(ok == 1, 0.0, MASKED)
+    mask_out[blocks:2 * blocks, :] = (lane == filled - 1).astype(F32)
+
+
 def gather_kernel(
-    rows, width, x_ref, tab_ref, wq_ref, wk_ref, wv_ref, bias_ref,
-    q_ref, k_ref, v_ref, far_ref, tab_out, land, tab_land, sends, recvs, tab_sends, tab_recvs,
+    rows, width, filled_ref, x_ref, picks_ref, wq_ref, wk_ref, wv_ref, qb_ref, vb_ref,
+    q_ref, k_ref, v_ref, far_ref, tab_out, prev_out, tail_out, mask_out,
+    tab_ref, land, tab_land, sends, recvs, tab_sends, tab_recvs,
 ):
     parts = 4
     part = rows // parts
@@ -48,6 +86,11 @@
     barrier = pltpu.get_barrier_semaphore()
     for other in (mate, across, diagonal):
         pl.semaphore_signal(barrier, inc=1, device_id=(dp, other), device_id_type=MESH)
+    chosen = picks_ref[...]
+    heads_here, each = chosen.shape[1:]
+    tab_ref[...] = jnp.concatenate(
+        [chosen[:, h, :] for h in range(heads_here)]
+        + [jnp.zeros((chosen.shape[0], 128 - heads_here * each), jnp.int32)], axis=1)
     pl.semaphore_wait(barrier, 3)
 
     def send(src, dst, slot, target):
@@ -58,11 +101,6 @@
         copy.start()
         return copy
 
-    far = [
-        send(x_ref.at[pl.ds(r * part, part)], land.at[0, pl.ds(r * part, part)], r, across)
-        for r in range(parts)
-    ]
-    near = send(x_ref, land.at[1], parts, mate)
     tables = []
     own_blocks = tab_ref.shape[0] // 4
     for slot, other in enumerate((mate, across, diagonal)):
@@ -73,16 +111,21 @@
         )
         copy.start()
         tables.append(copy)
+    far = [
+        send(x_ref.at[pl.ds(r * part, part)], land.at[0, pl.ds(r * part, part)], r, across)
+        for r in range(parts)
+    ]
+    near = send(x_ref, land.at[1], parts, mate)
 
     def keys_values(x, at):
         k_ref[pl.ds(at, width), :] = dot(x, wk_ref[...]).astype(BF16)
-        v_ref[pl.ds(at, width), :] = (dot(x, wv_ref[...]) + bias_ref[1:2, :]).astype(BF16)
+        v_ref[pl.ds(at, width), :] = (dot(x, wv_ref[...]) + vb_ref[...][None]).astype(BF16)
 
     def own(r, _):
         at = pl.multiple_of(r * width, width)
         x = x_ref[pl.ds(at, width), :]
         q_ref[pl.ds(at, width), :] = (
-            (dot(x, wq_ref[...]) + bias_ref[0:1, :]).astype(BF16) * jnp.asarray(SCALE, BF16)
+            (dot(x, wq_ref[...]) + qb_ref[...][None]).astype(BF16) * jnp.asarray(SCALE, BF16)
         )
         keys_values(x, pl.multiple_of(me * rows + at, width))
         return 0
@@ -99,6 +142,12 @@
 
     near.wait()
     block(1, mate, 0, rows)
+    for copy in tables:
+        copy.wait()
+    tab_out[pl.ds(me, 1)] = tab_ref[pl.ds(pl.multiple_of(me * own_blocks, 8), own_blocks)][None]
+    for slot, other in enumerate((mate, across, diagonal)):
+        tab_out[pl.ds(other, 1)] = tab_land[slot][None]
+    tables_of(tab_out, filled_ref[0], me * own_blocks, each, prev_out, tail_out, mask_out)
     relayed = []
     for r in range(parts):
         far[r].wait()
@@ -109,18 +158,16 @@
             relayed[r - 1].wait()
             block(2, diagonal, (r - 1) * part, part)
     far_ref[...] = land[0]
-    for copy in tables:
-        copy.wait()
     relayed[-1].wait()
     block(2, diagonal, (parts - 1) * part, part)
-    tab_out[pl.ds(me, 1)] = tab_ref[pl.ds(pl.multiple_of(me * own_blocks, 8), own_blocks)][None]
-    for slot, other in enumerate((mate, across, diagonal)):
-        tab_out[pl.ds(other, 1)] = tab_land[slot][None]
-
-
-def gather_project(tokens, table, query_weight, key_weight, value_weight, biases):
+
+
+def gather_project(
+    filled, tokens, chosen, query_weight, key_weight, value_weight, query_bias, value_bias,
+):
     rows, features = tokens.shape
     own_blocks = rows // BLK
+    slot_blocks = chosen.shape[0]
     copies = 4 + 1 + 4
     return pl.pallas_call(
         functools.partial(gather_kernel, rows, 128),
@@ -130,10 +177,14 @@
             jax.ShapeDtypeStruct((4 * rows, features), BF16),
             jax.ShapeDtypeStruct((rows, features), BF16),
             jax.ShapeDtypeStruct((4, own_blocks, 128), jnp.int32),
+            jax.ShapeDtypeStruct((4, own_blocks, 128), jnp.int32),
+            jax.ShapeDtypeStruct((4, slot_blocks, 128), jnp.int32),
+            jax.ShapeDtypeStruct((2 * own_blocks, 128), F32),
         ),
-        in_specs=[whole_vmem()] * 6,
-        out_specs=(whole_vmem(),) * 5,
+        in_specs=[pl.BlockSpec(memory_space=pltpu.SMEM)] + [whole_vmem()] * 7,
+        out_specs=(whole_vmem(),) * 8,
         scratch_shapes=[
+            VMEM((slot_blocks, 128), jnp.int32),
             VMEM((3, rows, features), BF16),
             VMEM((3, own_blocks, 128), jnp.int32),
             pltpu.SemaphoreType.DMA((copies,)),
@@ -145,13 +196,13 @@
             collective_id=0, has_side_effects=True, vmem_limit_bytes=LIMIT
         ),
         name="gather_project",
-    )(tokens, table, query_weight, key_weight, value_weight, biases)
-
-
-def key_blocks(tab_ref, end, pair, i, at, own_blocks, last_row):
+    )(filled, tokens, chosen, query_weight, key_weight, value_weight, query_bias, value_bias)
+
+
+def key_blocks(tab_ref, end, pair, i, at, last_row):
     def chosen(head, t):
         group, inner = lax.div(head, 3), lax.rem(head, 3)
-        return tab_ref[(group * own_blocks + i) * 128 + inner * 3 + t]
+        return tab_ref[group, i, inner * 3 + t]
 
     head = 2 * pair
     both = [(chosen(head, t), chosen(head + 1, t)) for t in range(3)]
@@ -182,7 +233,7 @@
 
 
 def masked_scores(scores, mask_ref, i):
-    parts = [scores[n * BLK:(n + 1) * BLK] + mask_ref[i * 8 + n] for n in range(5)]
+    parts = [scores[n * BLK:(n + 1) * BLK] + mask_ref[i, n] for n in range(5)]
     return jnp.concatenate(parts + [scores[5 * BLK:]], axis=0)
 
 
@@ -195,7 +246,7 @@
 
     def step(i, _):
         at = first_block + i
-        shared, both = key_blocks(tab_ref, filled - 1, pair, i, at, own_blocks, last_row)
+        shared, both = key_blocks(tab_ref, filled - 1, pair, i, at, last_row)
         keys = gathered(k_ref, shared, both, low)
         values = gathered(v_ref, shared, both, low)
         query = split_pair(q_ref[rows_of(i), :], low)
@@ -252,7 +303,7 @@
 
     def step(i, _):
         at = first_block + i
-        shared, both = key_blocks(tab_ref, filled - 1, pair, i, at, own_blocks, last_row)
+        shared, both = key_blocks(tab_ref, filled - 1, pair, i, at, last_row)
         keys = gathered(k_ref, shared, both, low)
         values = gathered(v_ref, shared, both, low)
         query = split_pair(q_ref[rows_of(i), :], low)
@@ -444,32 +495,9 @@
     return jnp.sum(values, axis=0, keepdims=True)
 
 
-def masks(filled, seq, own_blocks):
-    at = seq * own_blocks + jnp.arange(own_blocks, dtype=jnp.int32)[:, None]
-    kind = jnp.arange(8, dtype=jnp.int32)[None, :]
-    window = at + kind - 1
-    ok = jnp.where(
-        kind < 3, (window >= 0) & (window < filled),
-        jnp.where(kind == 3, at >= 2, jnp.abs(at - (filled - 1)) > 1))
-    last = jnp.arange(4 * own_blocks, dtype=jnp.int32) == filled - 1
-    return jnp.concatenate([jnp.where(ok, 0.0, MASKED).astype(F32).reshape(-1), last.astype(F32)])
-
-
-def links(table, filled, own_blocks):
-    mine = table.reshape(4, own_blocks, 128)[:, :, :9].reshape(4, own_blocks, 3, 3)
-    blocks = mine.transpose(0, 2, 1, 3).reshape(12, own_blocks * 3)
-    count = blocks.shape[1]
-    at = jnp.arange(count, dtype=jnp.int32)
-    same = (blocks[:, :, None] == blocks[:, None, :]) & (at[None, None, :] < at[None, :, None])
-    before = jnp.max(jnp.where(same, at[None, None, :], -1), axis=2)
-    where = jnp.arange(32, dtype=jnp.int32)[None, :, None] == blocks[:, None, :]
-    tail = jnp.max(jnp.where(where, at[None, None, :], -1), axis=2)
-    both = jnp.concatenate([before.reshape(-1), tail.reshape(-1)])
-    return jnp.concatenate([jnp.where(both < 0, count, both), (filled - 1)[None]])
-
-
 def layer_kernel(
-    rows, tile, own_blocks, groups, tab_ref, link_ref, mask_ref, bias_ref, bu_ref, lse_ref,
+    rows, tile, own_blocks, groups, tab_ref, prev_ref, tail_ref, mask_ref, bo_ref, g1_ref, s1_ref,
+    bd_ref, g2_ref, s2_ref, bu_ref, lse_ref,
     x_any, merged_any, cot_any, wo_any, wu_any, wd_any, q_any, k_any, v_any, wk_any, wv_any, wq_any,
     far_any,
     result_ref, dx_ref, gq_ref, gk_ref, gv_ref, go_ref, up_ref, down_ref, vec_ref,
@@ -489,7 +517,7 @@
     x, z = lax.rem(dp, 2), dp // 2
     core, y = lax.rem(seq, 2), seq // 2
     mate, across, diagonal = (lax.bitwise_xor(seq, bit) for bit in (1, 2, 3))
-    end = link_ref[2 * pairs * (picks_count + 4 * own_blocks)]
+    end = prev_ref[0, 0, 127]
     first_block = seq * own_blocks
     low = lanes_low(BLK)
     to_mate, to_y = (dp, mate), (dp, across)
@@ -644,17 +672,18 @@
         for target in neighbours:
             pl.semaphore_signal(barrier, inc=1, device_id=target, device_id_type=MESH)
         pl.semaphore_wait(barrier, len(neighbours))
-        bo, g1, s1, bd, g2, s2 = (bias_ref.at[n:n + 1, :] for n in range(2, 8))
+        bo, g1, s1, bd, g2, s2 = (
+            ref[...][None] for ref in (bo_ref, g1_ref, s1_ref, bd_ref, g2_ref, s2_ref))
 
         for name in ("x", "merged", "wo"):
             loading[name].wait()
         ffn[...] = dot(merged_ref[...], wo[...])
 
         def norm_one(at, r):
-            normed, inv_root = normed_rows(x_ref[at, :].astype(F32) + (ffn[at, :] + bo[...]))
+            normed, inv_root = normed_rows(x_ref[at, :].astype(F32) + (ffn[at, :] + bo))
             normed_one[at, :] = normed
             root_one[at, :] = inv_root
-            first_low[at, :] = (normed * g1[...] + s1[...]).astype(BF16)
+            first_low[at, :] = (normed * g1 + s1).astype(BF16)
 
         tiles(norm_one)
 
@@ -682,12 +711,12 @@
         loading["cot"].wait()
 
         def norm_two(at, r):
-            first = normed_one[at, :] * g1[...] + s1[...]
-            normed, inv_root = normed_rows(first + (ffn[at, :] + bd[...]))
-            result_ref[at, :] = (normed * g2[...] + s2[...]).astype(BF16)
+            first = normed_one[at, :] * g1 + s1
+            normed, inv_root = normed_rows(first + (ffn[at, :] + bd))
+            result_ref[at, :] = (normed * g2 + s2).astype(BF16)
             place = lax.broadcasted_iota(jnp.int32, (tile, 1), 0) + r * tile
             grad = cot_ref[at, :].astype(F32) * (place < limit).astype(F32)
-            pulled = norm_pull(grad, normed, inv_root, g2[...])
+            pulled = norm_pull(grad, normed, inv_root, g2)
             rounded = pulled.astype(BF16)
             ffn[at, :] = pulled
             d_ffn[at, :] = rounded
@@ -765,7 +794,7 @@
         def pull_one(at, r):
             grad = ffn[at, :]
             normed = normed_one[at, :]
-            pulled = norm_pull(grad, normed, root_one[at, :], g1[...])
+            pulled = norm_pull(grad, normed, root_one[at, :], g1)
             rounded = pulled.astype(BF16)
             dx_ref[at, :] = pulled
             d_attn_ref[at, :] = rounded
@@ -839,7 +868,7 @@
 
                 def step(i, _):
                     at = first_block + i
-                    shared, both = key_blocks(tab_ref, end, p, i, at, own_blocks, last_row)
+                    shared, both = key_blocks(tab_ref, end, p, i, at, last_row)
                     keys = gathered(k_ref, shared, both, low, lanes)
                     values = gathered(v_ref, shared, both, low, lanes)
                     query = split_pair(q_ref[rows_of(i), lanes], low)
@@ -859,25 +888,26 @@
                         acc[n, BLK:2 * BLK, :] += part[3 * BLK:4 * BLK]
                         last[n] += part[4 * BLK:5 * BLK]
                     for t in range(3):
-                        one = link_ref[2 * p * picks_count + i * 3 + t]
-                        two = link_ref[(2 * p + 1) * picks_count + i * 3 + t]
+                        one, two = (
+                            prev_ref[lax.div(h, 3), i, lax.rem(h, 3) * 3 + t]
+                            for h in (2 * p, 2 * p + 1))
                         for n, part in enumerate(parts):
                             picked[n, i * 3 + t] = part[(5 + t) * BLK:(6 + t) * BLK] + jnp.where(
                                 low, picked[n, one], picked[n, two])
                     return 0
 
                 lax.fori_loop(0, own_blocks, step, 0, unroll=own_blocks)
-                tails = 2 * pairs * picks_count
 
                 def gather(owner, _):
                     for inner in range(own_blocks):
                         block = owner * own_blocks + inner
-                        one = link_ref[tails + 2 * p * (last_row + 1) + block]
-                        two = link_ref[tails + (2 * p + 1) * (last_row + 1) + block]
+                        one, two = (
+                            tail_ref[lax.div(h, 3), block, lax.rem(h, 3) * 3]
+                            for h in (2 * p, 2 * p + 1))
                         for n in range(2):
                             total = acc[n, rows_of(block + 1), :]
                             total = total + jnp.where(low, picked[n, one], picked[n, two])
-                            total = total + last[n] * mask_ref[own_blocks * 8 + block]
+                            total = total + last[n] * mask_ref[own_blocks, block]
                             buf[p, owner, n, inner * BLK:(inner + 1) * BLK] = total.astype(BF16)
                     return 0
 
@@ -984,7 +1014,7 @@
 
 
 def layer_tail(
-    groups, table, link, mask, biases, up_bias, lse, tokens, merged, cotangent, out_weight,
+    groups, table, prev, tail, mask, biases, up_bias, lse, tokens, merged, cotangent, out_weight,
     up_weight, down_weight, query, keys, values, key_weight, value_weight, query_weight, far_tokens,
 ):
     rows, features = tokens.shape
@@ -1007,7 +1037,7 @@
             jax.ShapeDtypeStruct((wide * share, features), F32),
             jax.ShapeDtypeStruct((16, features), F32),
         ),
-        in_specs=[in_smem] * 3 + [whole_vmem()] * 3 + [any_space] * 13,
+        in_specs=[in_smem] * 4 + [whole_vmem()] * 8 + [any_space] * 13,
         out_specs=(whole_vmem(),) * 9,
         scratch_shapes=[
             VMEM((12, 4 * groups) + UNIT, BF16),
@@ -1029,9 +1059,43 @@
         ),
         name="layer_tail",
     )(
-        table, link, mask, biases, up_bias, lse, tokens, merged, cotangent, out_weight, up_weight,
+        table, prev, tail, mask, *biases, up_bias, lse, tokens, merged, cotangent, out_weight, up_weight,
         down_weight, query, keys, values, key_weight, value_weight, query_weight, far_tokens,
     )
+
+
+def finish_kernel(groups, vec_ref, *refs):
+    count = len(refs) - 9
+    given, out, vectors = refs[:count // 2], refs[count // 2:count], refs[count:]
+    for src, dst in zip(given, out):
+        dst[...] = src[...]
+    features = vec_ref.shape[1]
+    share = vectors[0].shape[0]
+    shard = lax.axis_index("dp") * 4 + lax.axis_index("seq")
+    moved = pltpu.roll(vec_ref[...], lax.rem(features - shard * share, features), axis=1)
+    for n in range(8):
+        vectors[n][...] = moved[n, 0:share]
+    wide = vectors[8].shape[0] // share
+    per_row = features // (wide * share)
+    mine = vec_ref[pl.ds(8 + shard // per_row, 1), :]
+    start = lax.rem(shard, per_row) * (wide * share)
+    mine = pltpu.roll(mine, lax.rem(features - start, features), axis=1)
+    vectors[8][...] = mine[0, 0:wide * share]
+
+
+def hand_out(groups, vectors, arrays):
+    features = vectors.shape[1]
+    share = features // (8 * groups)
+    wide = arrays[-1].shape[0] // share
+    shapes = [jax.ShapeDtypeStruct(a.shape, a.dtype) for a in arrays]
+    lines = [jax.ShapeDtypeStruct((share,), F32)] * 8 + [jax.ShapeDtypeStruct((wide * share,), F32)]
+    return pl.pallas_call(
+        functools.partial(finish_kernel, groups),
+        out_shape=tuple(shapes + lines),
+        in_specs=[whole_vmem()] * (1 + len(arrays)),
+        out_specs=(whole_vmem(),) * (len(arrays) + 9),
+        name="hand_out",
+    )(vectors, *arrays)
 
 
 def layer_norm(values, gain, shift):
@@ -1064,34 +1128,22 @@
     place = lax.axis_index("seq") * row_count + jnp.arange(row_count, dtype=jnp.int32)
     live_tokens = (place < filled * BLK).astype(F32)[:, None]
 
-    table = random_blocks[0].reshape(random_blocks.shape[1], -1)
-    table = jnp.pad(table, ((0, 0), (0, 128 - table.shape[1])))
-    biases = jnp.stack([
-        query_bias, value_bias, out_bias, attn_gain, attn_shift, down_bias, ffn_gain, ffn_shift])
-    query, keys, values, far_tokens, table = gather_project(
-        tokens, table, query_weight, key_weight, value_weight, biases
-    )
-    table = table.reshape(-1)
-    mask = masks(filled, lax.axis_index("seq"), row_count // BLK)
+    query, keys, values, far_tokens, table, prev, tail, mask = gather_project(
+        filled_blocks, tokens, random_blocks[0], query_weight, key_weight, value_weight, query_bias,
+        value_bias)
     keys, values = (t.reshape(-1, BLK, feature_count) for t in (keys, values))
     merged, lse = attention_forward(table, filled_blocks, mask, query, keys, values)
 
     if groups:
-        seq = lax.axis_index("seq")
-        result, grad_tokens, gq, gk, gv, go, up, down, vectors = layer_tail(
-            groups, table, links(table, filled, row_count // BLK), mask, biases, up_bias[None], lse,
+        *arrays, vectors = layer_tail(
+            groups, table, prev, tail, mask,
+            (out_bias, attn_gain, attn_shift, down_bias, ffn_gain, ffn_shift), up_bias[None], lse,
             tokens, merged, cotangent, out_weight, up_weight, down_weight, query, keys, values,
             key_weight, value_weight, query_weight, far_tokens)
-        shard = lax.axis_index("dp") * 4 + seq
-        share = gq.shape[0]
-        mine = lax.dynamic_slice(vectors, (0, shard * share), (8, share))
-        wide = up.shape[1] // feature_count
-        up_sum = lax.dynamic_slice(
-            vectors[8:8 + wide].reshape(-1), (shard * wide * share,), (wide * share,))
+        (result, grad_tokens, gq, gk, gv, go, up, down, g2, s2, bd, g1, s1, bo, bq, bv,
+         bu) = hand_out(groups, vectors, arrays)
         return (
-            result, grad_tokens, gq, mine[6], gk, gv, mine[7], go, mine[5], mine[3], mine[4], up,
-            up_sum, down, mine[2], mine[0], mine[1],
-        )
+            result, grad_tokens, gq, bq, gk, gv, bv, go, bo, g1, s1, up, bu, down, bd, g2, s2)
 
     attn = dot(merged, out_weight) + out_bias
     first, normed_one, root_one = layer_norm(tokens.astype(F32) + attn, attn_gain, attn_shift)

time: 184 us -> 170 us (0.924)
  local copies, waits for them, and re-layouts: 18.1 us -> 1.42 us
  Pallas kernels: 161 us -> 166 us
  other arithmetic: 2.67 us -> 0 us
    another operation x11 -> x0, local copies, waits for them, and re-layouts: 6.26 us -> none  [the longest x9 6.16 us: on_device(): jnp.stack([query_bias, value_bias, out_bias, attn_gain, attn_shift, down_...]
    unnamed x22 -> x1, local copies, waits for them, and re-layouts: 7.19 us -> 1.42 us
    pallas_call x0 -> x1, Pallas kernels: none -> 3.72 us  [hand_out(): pl.pallas_call(functools.partial(finish_kernel, groups), out_shape=tuple(...]
where the time goes in v4:
time: 170 us; the launch traced here: 169 us
  Pallas kernels  166 us (98%)
    pallas_call x1, Pallas kernels, layer_tail(): pl.pallas_call(functools.partial(layer_kernel, rows, 128, own_blocks, gro...  123 us
    pallas_call x1, Pallas kernels, gather_project(): pl.pallas_call(functools.partial(gather_kernel, rows, 128), out_shape=(ja...  28.1 us
    pallas_call x1, Pallas kernels, attention_forward(): pl.pallas_call(functools.partial(forward_kernel, own_blocks), out_shape=(...  12 us
    pallas_call x1, Pallas kernels, hand_out(): pl.pallas_call(functools.partial(finish_kernel, groups), out_shape=tuple(...  3.72 us

profile of v4, /device:TPU:0, one launch (start us, length us, event | category | flops | bytes accessed | tf_op | source)
XLA Modules:
  0.0 169.3 jit_solution(8230066722581505453)
XLA Ops:
  1.3 1.4 copy.36
  2.7 28.1 %gather_project.1 = (bf16[512,768]{1,0:T(8,128)(2,1)}, bf16[2048,768]{1,0:T(8,128)(2,1)}, bf16[2048,768]{1,0:T(8,128)(2,1)}, bf16[512,768]{1,0:T(8,128)(2,1)}, s...) custom-call(s32[1]{0:T(128)S(6)} %copy.37.filled_ref, ...), custom_call_target="tpu_custom_call" | custom-call | tf_op jit(solution)/shard_map/gather_project/pallas_call | solution.py:172
  30.8 12.0 %attention_forward.1 = (bf16[512,768]{1,0:T(8,128)(2,1)}, f32[6,8,128]{2,1,0:T(8,128)}) custom-call(s32[4,8,128]{2,1,0:T(8,128)} %get-tuple-element.53.tab_ref, s32[1]{0:T(128)S(6)} %copy.37.filled_ref, f32[16,128]{1,0:T(8,128)} %get-tuple-element.56.mask_ref, bf16[512,768]{1,0:T(8,128)(2,1)} %get-tuple-element.57.q_ref.q_any, bf16[32,64,768]{2,1,0:T(8,128)(2,1)} %bitcast.4, ...), custom_call_target="tpu_custom_call" | custom-call | tf_op jit(solution)/shard_map/attention_forward/pallas_call | solution.py:275
  42.8 122.6 %layer_tail.1 = (bf16[512,768]{1,0:T(8,128)(2,1)}, f32[512,768]{1,0:T(8,128)}, f32[24,768]{1,0:T(8,128)}, f32[24,768]{1,0:T(8,128)}, f32[24,768]{1,0:T(8,128)}, ...) custom-call(s32[4,8,128]{2,1,0:T(8,128)} %get-tuple-element.53.tab_ref, ...), custom_call_target="tpu_custom_call" | custom-call | tf_op jit(solution)/shard_map/layer_tail/pallas_call | solution.py:1031
  165.4 3.7 %hand_out.1 = (bf16[512,768]{1,0:T(8,128)(2,1)}, f32[512,768]{1,0:T(8,128)}, f32[24,768]{1,0:T(8,128)}, f32[24,768]{1,0:T(8,128)}, f32[24,768]{1,0:T(8,128)}, /*...) custom-call(f32[16,768]{1,0:T(8,128)} %get-tuple-element.63.vec_ref,, ...), custom_call_target="tpu_custom_call" | custom-call | tf_op jit(solution)/shard_map/hand_out/pallas_call | solution.py:1092

commit v5 on v4

--- a/solution.py
+++ b/solution.py
@@ -39,7 +39,7 @@
 
 def tables_of(tab_out, filled, first_block, each, prev_out, tail_out, mask_out):
     groups, blocks, width = tab_out.shape
-    slot_blocks = tail_out.shape[1]
+    slot_blocks = width
     none = blocks * each
     lane = lax.broadcasted_iota(jnp.int32, (blocks, width), 1)
     row = lax.broadcasted_iota(jnp.int32, (blocks, width), 0)
@@ -63,7 +63,10 @@
         best = tail
         for shift in range(1, each):
             best = jnp.maximum(best, pltpu.roll(tail, width - shift, axis=1))
-        tail_out[g] = jnp.where(best < 0, none, best)
+        turned = jnp.where(best < 0, none, best).astype(F32).T.astype(jnp.int32)
+        for h in range(3):
+            tail_out[g, h:h + 1, :] = turned[h * each:h * each + 1, :]
+        tail_out[g, 3:blocks, :] = jnp.full((blocks - 3, width), none, jnp.int32)
     at = first_block + row
     window = at + lane - 1
     ok = jnp.where(
@@ -75,22 +78,31 @@
 
 
 def gather_kernel(
-    rows, width, filled_ref, x_ref, picks_ref, wq_ref, wk_ref, wv_ref, qb_ref, vb_ref,
-    q_ref, k_ref, v_ref, far_ref, tab_out, prev_out, tail_out, mask_out,
-    tab_ref, land, tab_land, sends, recvs, tab_sends, tab_recvs,
+    rows, width, filled_ref, x_ref, picks_ref, wq_any, wk_any, wv_any, qb_ref, vb_ref,
+    q_any, k_any, v_any, far_any, tab_out, prev_out, tail_out, mask_out,
+    wq_ref, wk_ref, wv_ref, q_ref, k_ref, v_ref,
+    tab_ref, land, tab_land, loads, stores, sends, recvs, tab_sends, tab_recvs,
 ):
     parts = 4
     part = rows // parts
     dp, me = lax.axis_index("dp"), lax.axis_index("seq")
     mate, across, diagonal = (lax.bitwise_xor(me, bit) for bit in (1, 2, 3))
+    weights = [
+        pltpu.make_async_copy(src, dst, loads.at[n])
+        for n, (src, dst) in enumerate(((wq_any, wq_ref), (wk_any, wk_ref), (wv_any, wv_ref)))
+    ]
+    for copy in weights:
+        copy.start()
     barrier = pltpu.get_barrier_semaphore()
     for other in (mate, across, diagonal):
         pl.semaphore_signal(barrier, inc=1, device_id=(dp, other), device_id_type=MESH)
-    chosen = picks_ref[...]
-    heads_here, each = chosen.shape[1:]
-    tab_ref[...] = jnp.concatenate(
-        [chosen[:, h, :] for h in range(heads_here)]
-        + [jnp.zeros((chosen.shape[0], 128 - heads_here * each), jnp.int32)], axis=1)
+    heads_here, each = 3, picks_ref.shape[0] // 3
+    blocks = picks_ref.shape[2]
+    chosen = picks_ref[...].reshape(heads_here * each, blocks).astype(F32)
+    chosen = jnp.concatenate(
+        [chosen, jnp.zeros((heads_here * each, 128 - blocks), F32)], axis=1)
+    chosen = jnp.concatenate([chosen, jnp.zeros((128 - heads_here * each, 128), F32)], axis=0)
+    tab_ref[...] = chosen.T[0:blocks].astype(jnp.int32)
     pl.semaphore_wait(barrier, 3)
 
     def send(src, dst, slot, target):
@@ -116,10 +128,20 @@
         for r in range(parts)
     ]
     near = send(x_ref, land.at[1], parts, mate)
+    stored = []
+
+    def store(src, dst, start, count):
+        at = pl.ds(pl.multiple_of(start, part), count)
+        copy = pltpu.make_async_copy(src.at[at], dst.at[at], stores.at[len(stored)])
+        copy.start()
+        stored.append(copy)
 
     def keys_values(x, at):
         k_ref[pl.ds(at, width), :] = dot(x, wk_ref[...]).astype(BF16)
         v_ref[pl.ds(at, width), :] = (dot(x, wv_ref[...]) + vb_ref[...][None]).astype(BF16)
+
+    for copy in weights:
+        copy.wait()
 
     def own(r, _):
         at = pl.multiple_of(r * width, width)
@@ -131,6 +153,9 @@
         return 0
 
     lax.fori_loop(0, rows // width, own, 0)
+    store(q_ref, q_any, 0, rows)
+    store(k_ref, k_any, me * rows, rows)
+    store(v_ref, v_any, me * rows, rows)
 
     def block(slot, owner, start, count):
         def step(r, _):
@@ -139,6 +164,8 @@
             return 0
 
         lax.fori_loop(0, count // width, step, 0)
+        store(k_ref, k_any, owner * rows + start, count)
+        store(v_ref, v_any, owner * rows + start, count)
 
     near.wait()
     block(1, mate, 0, rows)
@@ -153,13 +180,15 @@
         far[r].wait()
         piece = pl.ds(r * part, part)
         relayed.append(send(land.at[0, piece], land.at[2, piece], parts + 1 + r, mate))
+        store(land.at[0], far_any, r * part, part)
         block(0, across, r * part, part)
         if r:
             relayed[r - 1].wait()
             block(2, diagonal, (r - 1) * part, part)
-    far_ref[...] = land[0]
     relayed[-1].wait()
     block(2, diagonal, (parts - 1) * part, part)
+    for copy in stored:
+        copy.wait()
 
 
 def gather_project(
@@ -167,30 +196,33 @@
 ):
     rows, features = tokens.shape
     own_blocks = rows // BLK
-    slot_blocks = chosen.shape[0]
+    slot_blocks = chosen.shape[2]
     copies = 4 + 1 + 4
+    any_space = pl.BlockSpec(memory_space=pl.ANY)
+    low = jax.ShapeDtypeStruct((rows, features), BF16)
+    slot = jax.ShapeDtypeStruct((4 * rows, features), BF16)
+    table = jax.ShapeDtypeStruct((4, own_blocks, 128), jnp.int32)
+    dma = pltpu.SemaphoreType.DMA
     return pl.pallas_call(
         functools.partial(gather_kernel, rows, 128),
         out_shape=(
-            jax.ShapeDtypeStruct((rows, features), BF16),
-            jax.ShapeDtypeStruct((4 * rows, features), BF16),
-            jax.ShapeDtypeStruct((4 * rows, features), BF16),
-            jax.ShapeDtypeStruct((rows, features), BF16),
-            jax.ShapeDtypeStruct((4, own_blocks, 128), jnp.int32),
-            jax.ShapeDtypeStruct((4, own_blocks, 128), jnp.int32),
-            jax.ShapeDtypeStruct((4, slot_blocks, 128), jnp.int32),
+            low, slot, slot, low, table, table, table,
             jax.ShapeDtypeStruct((2 * own_blocks, 128), F32),
         ),
-        in_specs=[pl.BlockSpec(memory_space=pltpu.SMEM)] + [whole_vmem()] * 7,
-        out_specs=(whole_vmem(),) * 8,
+        in_specs=[pl.BlockSpec(memory_space=pltpu.SMEM)] + [whole_vmem()] * 2 + [any_space] * 3
+        + [whole_vmem()] * 2,
+        out_specs=(any_space,) * 4 + (whole_vmem(),) * 4,
         scratch_shapes=[
+            VMEM((features, features), BF16),
+            VMEM((features, features), BF16),
+            VMEM((features, features), BF16),
+            VMEM((rows, features), BF16),
+            VMEM((4 * rows, features), BF16),
+            VMEM((4 * rows, features), BF16),
             VMEM((slot_blocks, 128), jnp.int32),
             VMEM((3, rows, features), BF16),
             VMEM((3, own_blocks, 128), jnp.int32),
-            pltpu.SemaphoreType.DMA((copies,)),
-            pltpu.SemaphoreType.DMA((copies,)),
-            pltpu.SemaphoreType.DMA((3,)),
-            pltpu.SemaphoreType.DMA((3,)),
+            dma((3,)), dma((25,)), dma((copies,)), dma((copies,)), dma((3,)), dma((3,)),
         ],
         compiler_params=pltpu.CompilerParams(
             collective_id=0, has_side_effects=True, vmem_limit_bytes=LIMIT
@@ -237,6 +269,16 @@
     return jnp.concatenate(parts + [scores[5 * BLK:]], axis=0)
 
 
+def attend(keys, values, query, mask_ref, i, low):
+    scores = masked_scores(dot_nt(keys, query), mask_ref, i)
+    highest = jnp.max(scores, axis=0, keepdims=True)
+    weights = jnp.exp(scores - highest)
+    total = jnp.sum(weights, axis=0, keepdims=True)
+    share = (weights * (1.0 / total)).astype(BF16)
+    output = dot_tn(share, values)
+    return jnp.where(low, output[:BLK], output[BLK:]), highest + jnp.log(total)
+
+
 def forward_kernel(own_blocks, tab_ref, filled_ref, mask_ref, q_ref, k_ref, v_ref, out_ref, lse_ref):
     pair = pl.program_id(0)
     filled = filled_ref[0]
@@ -250,16 +292,9 @@
         keys = gathered(k_ref, shared, both, low)
         values = gathered(v_ref, shared, both, low)
         query = split_pair(q_ref[rows_of(i), :], low)
-        scores = masked_scores(dot_nt(keys, query), mask_ref, i)
-        highest = jnp.max(scores, axis=0, keepdims=True)
-        weights = jnp.exp(scores - highest)
-        total = jnp.sum(weights, axis=0, keepdims=True)
-        share = (weights * (1.0 / total)).astype(BF16)
-        output = dot_tn(share, values)
-        merged = jnp.where(low, output[:BLK], output[BLK:])
-        merged = jnp.where(at < filled, merged, 0.0)
-        out_ref[rows_of(i), :] = merged.astype(BF16)
-        lse_ref[0, pl.ds(i, 1), :] = highest + jnp.log(total)
+        merged, lse = attend(keys, values, query, mask_ref, i, low)
+        out_ref[rows_of(i), :] = jnp.where(at < filled, merged, 0.0).astype(BF16)
+        lse_ref[0, pl.ds(i, 1), :] = lse
         return 0
 
     lax.fori_loop(0, own_blocks, step, 0, unroll=own_blocks)
@@ -456,22 +491,27 @@
 GELU_A = 0.044715
 GELU_C = 0.7978845608028654
 UNIT = (48, 384)
-KINDS = "ABACABBCBABB"
-AXES = {"A": "yxz", "B": "xyz", "C": "zxy"}
-DOWN, UP, SQUARE = 0, 4, 8
-BETWEEN = (
-    (),
-    ((0, 0), (2, 0)),
-    ((3, 0), (1, 1)),
-    ((5, 0), (6, 0), (4, 0)),
-    ((7, 0), (11, 0), (0, 1), (2, 1)),
-    ((3, 1), (1, 2)),
+ORDERS = (
+    "yzx", "zxy", "yxz", "xzy", "xzy", "yxz", "xyz", "yxz", "yzx", "xyz", "zxy", "xzy",
 )
-AFTER = ((5, 1), (6, 1), (4, 1), (7, 1), (11, 1), (0, 2), (2, 2), (3, 2))
-LAST = (
-    (5, 2), (6, 2), (4, 2), (7, 2), (11, 2), (9, 0), (10, 0), (8, 0), (9, 1), (10, 1), (8, 1),
-    (9, 2), (10, 2), (8, 2),
-)
+UP, SQUARE = 4, 8
+OUT, KEY, VALUE, QUERY = 8, 9, 10, 11
+RIDERS = (OUT, QUERY)
+EVENTS = {
+    "up": ((0, 0), (3, 0)),
+    "dense": (),
+    0: ((2, 0), (4, 0), (1, 0)),
+    1: ((5, 0), (6, 0), (0, 1)),
+    2: ((2, 1), (1, 1), (7, 0), (3, 1)),
+    3: ((5, 1), (0, 2)),
+    4: ((8, 0), (4, 1), (7, 1), (6, 1), (1, 2), (2, 2)),
+    5: ((3, 2), (5, 2), (4, 2)),
+    "sum": (),
+    "far": (),
+    "v": ((8, 1),),
+    "x": ((7, 2), (6, 2)),
+    "end": ((9, 0), (8, 2), (11, 0), (10, 0), ("far", 0), (9, 1), (10, 1), (11, 1), (10, 2), (9, 2), (11, 2)),
+}
 
 
 def normed_rows(values):
@@ -497,13 +537,14 @@
 
 def layer_kernel(
     rows, tile, own_blocks, groups, tab_ref, prev_ref, tail_ref, mask_ref, bo_ref, g1_ref, s1_ref,
-    bd_ref, g2_ref, s2_ref, bu_ref, lse_ref,
-    x_any, merged_any, cot_any, wo_any, wu_any, wd_any, q_any, k_any, v_any, wk_any, wv_any, wq_any,
+    bd_ref, g2_ref, s2_ref, bu_ref,
+    x_any, cot_any, wo_any, wu_any, wd_any, q_any, k_any, v_any, wk_any, wv_any, wq_any,
     far_any,
     result_ref, dx_ref, gq_ref, gk_ref, gv_ref, go_ref, up_ref, down_ref, vec_ref,
-    work, land, core_down, core_up, core_out, pair_in, in_far, small, small_in, small_z,
-    x_ref, merged_ref, d_attn_ref, d_merged_ref,
-    loads, sends, recvs, c_sends, c_recvs, p_sends, p_recvs, s_sends, s_recvs, far_sems,
+    work, land, core_down, core_up, pair_in, in_far, small, late,
+    ride, ride_land, ride_core_in,
+    x_ref, merged_ref, d_attn_ref, d_merged_ref, q_ref, k_ref, v_ref, lse_ref,
+    loads, sends, recvs, c_sends, c_recvs, p_sends, p_recvs, r_sends, r_recvs, far_sems,
 ):
     features = x_ref.shape[1]
     hidden = bu_ref.shape[1]
@@ -563,7 +604,7 @@
     def index_of(u, at_x, at_y, at_z):
         at = {"x": at_x, "y": at_y, "z": at_z}
         flat = 0
-        for axis in AXES[KINDS[u]]:
+        for axis in ORDERS[u]:
             flat = flat * place_of[axis][1] + at[axis]
         return flat
 
@@ -571,9 +612,9 @@
         return s // 4, lax.rem(s // 2, 2), lax.rem(s, 2)
 
     def stage_of(u, stage):
-        sizes = [place_of[axis][1] for axis in AXES[KINDS[u]]] + [1]
+        sizes = [place_of[axis][1] for axis in ORDERS[u]] + [1]
         base, offset, sem, block = 0, 0, 0, shards
-        for n, axis in enumerate(AXES[KINDS[u]]):
+        for n, axis in enumerate(ORDERS[u]):
             block = block // sizes[n]
             if n == stage:
                 return axis, place_of[axis][0], sizes[n], block, base, offset, sem
@@ -591,6 +632,13 @@
                 work.at[u, pl.ds(base + index * block, block)],
                 land.at[u, pl.ds(offset + (step - 1) * block, block)],
                 sends.at[u, sem + step - 1], recvs.at[u, sem + step - 1], device(axis, index)))
+            if u in RIDERS:
+                n = RIDERS.index(u)
+                copies.append(remote(
+                    ride.at[n, core, pl.ds(base + index * block, block)],
+                    ride_land.at[n, pl.ds(offset + (step - 1) * block, block)],
+                    r_sends.at[n, sem + step - 1], r_recvs.at[n, sem + step - 1],
+                    device(axis, index)))
         return copies
 
     def begin(u, stage):
@@ -608,19 +656,32 @@
                 value = value + land[u, offset + step * block + r].astype(F32)
             return value
 
+        if u in RIDERS:
+            n = RIDERS.index(u)
+
+            def ridden(r):
+                value = ride[n, core, base + mine * block + r]
+                for step in range(size - 1):
+                    value = value + ride_land[n, offset + step * block + r]
+                return value
+
         if stage < 2:
             def body(r, _):
                 work[u, base + mine * block + r] = total(r).astype(BF16)
+                if u in RIDERS:
+                    ride[n, core, base + mine * block + r] = ridden(r)
                 return 0
 
             lax.fori_loop(0, block, body, 0)
             begin(u, stage + 1)
             return
         value = total(0)
+        if u in RIDERS:
+            vec_ref[n * 16:(n + 1) * 16, :] = ridden(0)
         if u < UP:
             down_ref[(u // 2) * UNIT[0]:(u // 2 + 1) * UNIT[0], (u % 2) * half:(u % 2 + 1) * half] = value
         else:
-            to = up_ref if u < SQUARE else (gq_ref, gk_ref, gv_ref, go_ref)[u - SQUARE]
+            to = up_ref if u < SQUARE else (go_ref, gk_ref, gv_ref, gq_ref)[u - SQUARE]
             at = (u - UP) * features if u < SQUARE else 0
             to[:, at:at + half] = value[:share]
             to[:, at + half:at + features] = value[share:]
@@ -629,13 +690,13 @@
         return jnp.concatenate(
             [source[pl.ds(at, count), 0:half], source[pl.ds(at, count), half:features]], axis=0)
 
-    def square_pieces(u, source, other):
+    def split_pieces(u, read, other):
         def body(s, _):
             at_z, at_x, at_y = shard_of(s)
             index = index_of(u, at_x, at_y, at_z)
             for own in (True, False):
                 row = 2 * s + (core if own else 1 - core)
-                value = folded(source, pl.multiple_of(row * share, 8), share).astype(BF16)
+                value = read(pl.multiple_of(row * share, 8), share).astype(BF16)
                 if own:
                     work[u, index] = value
                 else:
@@ -653,29 +714,84 @@
 
         lax.fori_loop(0, shards, body, 0)
 
+    def at_point(name):
+        for u, stage in EVENTS[name]:
+            finish(u, stage)
+
+    def vector_pieces(rider):
+        count = 6 if rider == 0 else 2
+        padded = jnp.zeros((16 - 8, 128 - share), F32)
+        for s in range(shards):
+            index = index_of(RIDERS[rider], (s // 2) % 2, s % 2, s // 4)
+            for n in range(2):
+                row = 2 * s + n
+                at = row * share
+                source = small if rider == 0 else late
+                value = source[0:8, at:at + share]
+                ride[rider, n, index, 0:8, :] = jnp.concatenate([value, padded], axis=1)
+                if rider == 0:
+                    start = (row % (2 * groups)) * (wide * share)
+                    ride[rider, n, index, 8:16, :] = jnp.concatenate(
+                        [small[8:16, start:start + wide * share],
+                         jnp.zeros((8, 128 - wide * share), F32)], axis=1)
+                else:
+                    ride[rider, n, index, 8:16, :] = jnp.zeros((8, 128), F32)
+
+    def ride_core(rider):
+        return remote(ride.at[rider, 1 - core], ride_core_in.at[rider], r_sends.at[rider, groups + 1],
+                      r_recvs.at[rider, groups + 1], to_mate)
+
     def core_copy(src, dst, slot):
         return remote(src, dst, c_sends.at[slot], c_recvs.at[slot], to_mate)
 
-    load("x", x_any, x_ref)
-    load("merged", merged_any, merged_ref)
+    load("q", q_any, q_ref)
+    load("k", k_any, k_ref)
+    load("v", v_any, v_ref)
+    barrier = pltpu.get_barrier_semaphore()
+    for target in neighbours:
+        pl.semaphore_signal(barrier, inc=1, device_id=target, device_id_type=MESH)
+    last_row = k_ref.shape[0] - 1
+
+    def forward_pair(p):
+        lanes = lanes_of(p)
+
+        def step(i, _):
+            at = first_block + i
+            shared, both = key_blocks(tab_ref, end, p, i, at, last_row)
+            keys = gathered(k_ref, shared, both, low, lanes)
+            values = gathered(v_ref, shared, both, low, lanes)
+            query = split_pair(q_ref[rows_of(i), lanes], low)
+            merged, lse = attend(keys, values, query, mask_ref, i, low)
+            live = lax.broadcasted_iota(jnp.int32, (BLK, 1), 0) < (end + 1 - at) * BLK
+            merged_ref[rows_of(i), lanes] = jnp.where(live, merged, 0.0).astype(BF16)
+            lse_ref[p, pl.ds(i, 1), :] = lse
+            return 0
+
+        lax.fori_loop(0, own_blocks, step, 0, unroll=own_blocks)
 
 
     def dense(
-        wo, wu, wd, cot_ref, normed_one, root_one, first_low, act, slope, ffn, d_ffn, tmp,
-        other_down, other_up,
+        wo, wu, wd, cot_ref, normed_one, root_one, first_low, act, slope, ffn, tmp, other,
     ):
-        load("wo", wo_any, wo)
-        load("wu", wu_any, wu)
-        load("wd", wd_any, wd)
-        load("cot", cot_any, cot_ref)
-        barrier = pltpu.get_barrier_semaphore()
-        for target in neighbours:
-            pl.semaphore_signal(barrier, inc=1, device_id=target, device_id_type=MESH)
-        pl.semaphore_wait(barrier, len(neighbours))
+        d_ffn = cot_ref
+        for name in ("q", "k", "v"):
+            loading[name].wait()
+        for name, src, dst in (
+            ("x", x_any, x_ref), ("wo", wo_any, wo), ("wu", wu_any, wu), ("wd", wd_any, wd),
+            ("cot", cot_any, cot_ref),
+        ):
+            load(name, src, dst)
+
+        def forward_two(n, _):
+            for inner in range(2):
+                forward_pair(2 * n + inner)
+            return 0
+
+        lax.fori_loop(0, pairs // 2, forward_two, 0)
         bo, g1, s1, bd, g2, s2 = (
             ref[...][None] for ref in (bo_ref, g1_ref, s1_ref, bd_ref, g2_ref, s2_ref))
 
-        for name in ("x", "merged", "wo"):
+        for name in ("x", "wo"):
             loading[name].wait()
         ffn[...] = dot(merged_ref[...], wo[...])
 
@@ -726,6 +842,7 @@
 
         tiles(norm_two)
 
+        pl.semaphore_wait(barrier, len(neighbours))
         down_copies = []
         for j in range(wide):
             tmp[...] = dot_tn(act[j], d_ffn[...])
@@ -742,11 +859,11 @@
                         if own:
                             work[u, index_of(u, at_x, at_y, j)] = value
                         else:
-                            other_down[j, u, n] = value
+                            other[j, u, n] = value
                 return 0
 
             lax.fori_loop(0, 4, pieces, 0)
-            down_copies.append(core_copy(other_down.at[j], core_down.at[j], j))
+            down_copies.append(core_copy(other.at[j], core_down.at[j], j))
             down_copies[-1].start()
 
         def backward(j, _):
@@ -777,19 +894,25 @@
             begin(u, 0)
 
         up_copies = []
-        for j in range(wide):
-            tmp[...] = dot_tn(first_low[...], act[j])
-            square_pieces(UP + j, tmp, other_up.at[j])
-            up_copies.append(core_copy(other_up.at[j], core_up.at[j], wide + j))
-            up_copies[-1].start()
-
-        for j in range(wide):
-            ffn[...] += dot_nt(act[j], wu[:, j * features:(j + 1) * features])
-        for j in range(wide):
+
+        def end_up(j):
             up_copies[j].wait()
             add_core(UP + j, core_up.at[j])
             begin(UP + j, 0)
-        finish(1, 0)
+
+        for j in range(wide):
+            tmp[...] = dot_tn(first_low[...], act[j])
+            split_pieces(UP + j, functools.partial(folded, tmp), other.at[j])
+            up_copies.append(core_copy(other.at[j], core_up.at[j], wide + j))
+            up_copies[-1].start()
+            if j:
+                end_up(j - 1)
+
+        for j in range(wide):
+            ffn[...] += dot_nt(act[j], wu[:, j * features:(j + 1) * features])
+            if j == 1:
+                end_up(wide - 1)
+        at_point("up")
 
         def pull_one(at, r):
             grad = ffn[at, :]
@@ -805,6 +928,7 @@
         tiles(pull_one)
         live = lax.broadcasted_iota(jnp.int32, (rows, 1), 0) < limit
         d_merged_ref[...] = jnp.where(live, dot_nt(d_attn_ref[...], wo[...]), 0.0).astype(BF16)
+        at_point("dense")
 
     low_rows = VMEM((rows, features), BF16)
     full_rows = VMEM((rows, features), F32)
@@ -812,33 +936,34 @@
     pl.run_scoped(
         dense, square_low, VMEM((features, hidden), BF16), VMEM((hidden, features), BF16),
         low_rows, full_rows, VMEM((rows, 1), F32), low_rows, VMEM((wide, rows, features), BF16),
-        VMEM((wide, rows, features), SLOPE), full_rows, low_rows, VMEM((features, features), F32),
-        VMEM((4, 4, 4) + UNIT, BF16), VMEM((4, 4, 4) + UNIT, BF16),
+        VMEM((wide, rows, features), SLOPE), full_rows, VMEM((features, features), F32),
+        VMEM((4, 4, 4) + UNIT, BF16),
     )
 
 
     def attention(
-        k_ref, v_ref, q_ref, dq_ref, far_ref, wk, wv, wq, acc, last, picked, buf, dko, dvo, dkr,
-        dvr, out_far, other, tmp,
+        dq_ref, far_ref, wk, wv, wq, acc, last, picked, buf, dko, dvo, dkr, dvr, out_far, other,
+        tmp,
     ):
         for name, src, dst in (
-            ("q", q_any, q_ref), ("k", k_any, k_ref), ("v", v_any, v_ref), ("wk", wk_any, wk),
-            ("wv", wv_any, wv), ("wq", wq_any, wq), ("far", far_any, far_ref),
+            ("far", far_any, far_ref), ("wk", wk_any, wk), ("wv", wv_any, wv), ("wq", wq_any, wq),
         ):
             load(name, src, dst)
-        square_copies = {
-            u: core_copy(other.at[u - SQUARE],
-                         core_out if u == SQUARE + 3 else core_down.at[u - SQUARE], u)
-            for u in range(SQUARE, SQUARE + 4)
-        }
-
-        def square(u, source):
-            square_pieces(u, source, other.at[u - SQUARE])
-            square_copies[u].start()
+        square_copies = [
+            core_copy(other.at[n], core_down.at[n], SQUARE + n) for n in range(4)
+        ]
+
+        def square(u):
+            split_pieces(u, functools.partial(folded, tmp), other.at[u - SQUARE])
+            square_copies[u - SQUARE].start()
 
         def end_square(u):
-            square_copies[u].wait()
-            add_core(u, core_out if u == SQUARE + 3 else core_down.at[u - SQUARE])
+            square_copies[u - SQUARE].wait()
+            if u in RIDERS:
+                n = RIDERS.index(u)
+                ride_core(n).wait()
+                ride[n, core] = ride[n, core] + ride_core_in[n]
+            add_core(u, core_down.at[u - SQUARE])
             begin(u, 0)
 
         def copy_pair(p, slot, owner):
@@ -857,13 +982,11 @@
         def heads():
             for n in range(2):
                 picked[n, picks_count] = jnp.zeros((BLK, PAIR), F32)
-            last_row = k_ref.shape[0] - 1
-            for name in ("q", "k", "v"):
-                loading[name].wait()
-
+                for edge in (0, own_blocks + 3):
+                    acc[n, edge] = jnp.zeros((BLK, PAIR), F32)
             def one_pair(p, _):
                 lanes = lanes_of(p)
-                acc[...] = jnp.zeros_like(acc)
+                acc[:, 1:own_blocks + 3] = jnp.zeros((2, own_blocks + 2, BLK, PAIR), F32)
                 last[...] = jnp.zeros_like(last)
 
                 def step(i, _):
@@ -884,9 +1007,9 @@
                     parts = (dot(d_scores, query), dot(share_of.astype(BF16), grad))
                     for n, part in enumerate(parts):
                         for slot in range(3):
-                            acc[n, rows_of(at + slot), :] += part[slot * BLK:(slot + 1) * BLK]
-                        acc[n, BLK:2 * BLK, :] += part[3 * BLK:4 * BLK]
-                        last[n] += part[4 * BLK:5 * BLK]
+                            acc[n, i + slot + 1] += part[slot * BLK:(slot + 1) * BLK]
+                        for slot in range(2):
+                            last[n, slot] += part[(3 + slot) * BLK:(4 + slot) * BLK]
                     for t in range(3):
                         one, two = (
                             prev_ref[lax.div(h, 3), i, lax.rem(h, 3) * 3 + t]
@@ -899,15 +1022,19 @@
                 lax.fori_loop(0, own_blocks, step, 0, unroll=own_blocks)
 
                 def gather(owner, _):
+                    first_owner = (owner == 0).astype(F32)
                     for inner in range(own_blocks):
                         block = owner * own_blocks + inner
+                        window = jnp.minimum(
+                            jnp.maximum(block - first_block + 2, 0), own_blocks + 3)
                         one, two = (
-                            tail_ref[lax.div(h, 3), block, lax.rem(h, 3) * 3]
+                            tail_ref[lax.div(h, 3), lax.rem(h, 3), block]
                             for h in (2 * p, 2 * p + 1))
                         for n in range(2):
-                            total = acc[n, rows_of(block + 1), :]
-                            total = total + jnp.where(low, picked[n, one], picked[n, two])
-                            total = total + last[n] * mask_ref[own_blocks, block]
+                            total = acc[n, window] + jnp.where(low, picked[n, one], picked[n, two])
+                            total = total + last[n, 1] * mask_ref[own_blocks, block]
+                            if inner == 0:
+                                total = total + last[n, 0] * first_owner
                             buf[p, owner, n, inner * BLK:(inner + 1) * BLK] = total.astype(BF16)
                     return 0
 
@@ -919,102 +1046,71 @@
                 def _():
                     sum_pair(p - 1)
 
-                for n, events in enumerate(BETWEEN):
+                for n in range(pairs):
                     @pl.when(p == n)
                     def _():
                         if n == 0:
-                            end_square(SQUARE + 3)
-                        for u, stage in events:
-                            finish(u, stage)
+                            end_square(OUT)
+                        at_point(n)
 
                 return 0
 
             lax.fori_loop(0, pairs, one_pair, 0)
 
+        vector_pieces(0)
+        ride_core(0).start()
         tmp[...] = dot_tn(merged_ref[...], d_attn_ref[...])
-        square(SQUARE + 3, tmp)
+        square(OUT)
         heads()
+        for name in ("far", "wk", "wv", "wq"):
+            loading[name].wait()
         sum_pair(pairs - 1)
-
-        loading["wk"].wait()
-        loading["wv"].wait()
+        at_point("sum")
+
+        tmp[...] = dot_tn(x_ref[...], dko[...]) + dot_tn(far_ref[...], dkr[...])
+        square(KEY)
         out_far[...] = (dot_nt(dkr[...], wk[...]) + dot_nt(dvr[...], wv[...])).astype(BF16)
         far = remote(out_far, in_far, far_sems.at[0], far_sems.at[1], to_y)
         far.start()
-        loading["wq"].wait()
-        loading["far"].wait()
-
-        tmp[...] = dot_tn(x_ref[...], dko[...]) + dot_tn(far_ref[...], dkr[...])
-        square(SQUARE + 1, tmp)
-        for u, stage in AFTER[:4]:
-            finish(u, stage)
+        end_square(KEY)
+        at_point("far")
         tmp[...] = dot_tn(x_ref[...], dvo[...]) + dot_tn(far_ref[...], dvr[...])
-        square(SQUARE + 2, tmp)
-        end_square(SQUARE + 1)
+        square(VALUE)
+        at_point("v")
         tmp[...] = dot_tn(x_ref[...], dq_ref[...])
-        square(SQUARE, tmp)
-        end_square(SQUARE + 2)
-        for u, stage in AFTER[4:]:
-            finish(u, stage)
-        end_square(SQUARE)
-
-        small[6:7, :] = column_sum(dq_ref[...].astype(F32))
-        small[7:8, :] = column_sum(dvo[...].astype(F32)) + column_sum(dvr[...].astype(F32))
-
-        def small_copies(stage):
-            axis = ("core", "y", "x", "z")[stage]
-            if axis == "z":
-                return [
-                    remote(small, small_z.at[step - 1], s_sends.at[2 + step], s_recvs.at[2 + step],
-                           device("z", lax.rem(z + step, groups)))
-                    for step in range(1, groups)
-                ]
-            target = {"core": to_mate, "y": to_y, "x": device("x", 1 - x)}[axis]
-            return [remote(small, small_in.at[stage], s_sends.at[stage], s_recvs.at[stage], target)]
-
-        def small_begin(stage):
-            for copy in small_copies(stage):
-                copy.start()
-
-        def small_end(stage):
-            for copy in small_copies(stage):
-                copy.wait()
-            if stage < 3:
-                small[...] += small_in[stage]
-                small_begin(stage + 1)
-            else:
-                total = small[...]
-                for step in range(1, groups):
-                    total = total + small_z[step - 1]
-                vec_ref[...] = total
-
-        small_begin(0)
+        square(QUERY)
+        end_square(VALUE)
+        late[...] = jnp.zeros_like(late)
+        late[0:1, :] = column_sum(dq_ref[...].astype(F32))
+        late[1:2, :] = column_sum(dvo[...].astype(F32)) + column_sum(dvr[...].astype(F32))
+        vector_pieces(1)
+        ride_core(1).start()
+        end_square(QUERY)
         dx_ref[...] += (
-            dot_nt(dq_ref[...], wq[...]) + dot_nt(dko[...], wk[...]) + dot_nt(dvo[...], wv[...])
+            dot_nt(dko[...], wk[...]) + dot_nt(dvo[...], wv[...]) + dot_nt(dq_ref[...], wq[...])
         )
-        for n, (u, stage) in enumerate(LAST):
-            if n in (2, 5, 6, 8):
-                small_end((2, 5, 6, 8).index(n))
-            if n == 6:
+        at_point("x")
+        for u, stage in EVENTS["end"]:
+            if u == "far":
                 far.wait()
                 dx_ref[...] += in_far[...].astype(F32)
-            finish(u, stage)
+            else:
+                finish(u, stage)
 
     pl.run_scoped(
-        attention, VMEM((4 * own_blocks, BLK, features), BF16),
-        VMEM((4 * own_blocks, BLK, features), BF16), low_rows, low_rows, low_rows, square_low, square_low, square_low,
-        VMEM((2, (4 * own_blocks + 2) * BLK, PAIR), F32), VMEM((2, BLK, PAIR), F32),
+        attention, low_rows, low_rows, square_low, square_low, square_low,
+        VMEM((2, own_blocks + 4, BLK, PAIR), F32), VMEM((2, 2, BLK, PAIR), F32),
         VMEM((2, picks_count + 1, BLK, PAIR), F32), VMEM((pairs, 4, 2, rows, PAIR), BF16),
         low_rows, low_rows, low_rows, low_rows, low_rows, VMEM((4, 4, 4) + UNIT, BF16),
         VMEM((features, features), F32),
     )
 
 
-SLOPE = F32
+SLOPE = BF16
 
 
 def layer_tail(
-    groups, table, prev, tail, mask, biases, up_bias, lse, tokens, merged, cotangent, out_weight,
+    groups, table, prev, tail, mask, biases, up_bias, tokens, cotangent, out_weight,
     up_weight, down_weight, query, keys, values, key_weight, value_weight, query_weight, far_tokens,
 ):
     rows, features = tokens.shape
@@ -1024,6 +1120,7 @@
     share = features // (8 * groups)
     wide = hidden // features
     low = VMEM((rows, features), BF16)
+    kv = VMEM((4 * own_blocks, BLK, features), BF16)
     line = jax.ShapeDtypeStruct((share, features), F32)
     any_space = pl.BlockSpec(memory_space=pl.ANY)
     in_smem = pl.BlockSpec(memory_space=pltpu.SMEM)
@@ -1035,31 +1132,33 @@
             jax.ShapeDtypeStruct((rows, features), F32), line, line, line, line,
             jax.ShapeDtypeStruct((share, hidden), F32),
             jax.ShapeDtypeStruct((wide * share, features), F32),
-            jax.ShapeDtypeStruct((16, features), F32),
+            jax.ShapeDtypeStruct((32, 128), F32),
         ),
-        in_specs=[in_smem] * 4 + [whole_vmem()] * 8 + [any_space] * 13,
+        in_specs=[in_smem] * 4 + [whole_vmem()] * 7 + [any_space] * 12,
         out_specs=(whole_vmem(),) * 9,
         scratch_shapes=[
             VMEM((12, 4 * groups) + UNIT, BF16),
             VMEM((12, 4 * groups - 1) + UNIT, BF16),
             VMEM((4, 4, 4) + UNIT, BF16),
             VMEM((4, 4, 4) + UNIT, BF16),
-            VMEM((4, 4) + UNIT, BF16),
             VMEM((pairs, 2, 2, rows, PAIR), BF16),
             low,
             VMEM((16, features), F32),
-            VMEM((3, 16, features), F32),
-            VMEM((groups - 1, 16, features), F32),
-            low, low, low, low,
+            VMEM((8, features), F32),
+            VMEM((2, 2, 4 * groups, 16, 128), F32),
+            VMEM((2, 4 * groups - 1, 16, 128), F32),
+            VMEM((2, 4 * groups, 16, 128), F32),
+            low, low, low, low, low, kv, kv, VMEM((pairs, own_blocks, PAIR), F32),
             dma((13,)), dma((12, groups + 1)), dma((12, groups + 1)), dma((12,)), dma((12,)),
-            dma((pairs, 2)), dma((pairs, 2)), dma((groups + 2,)), dma((groups + 2,)), dma((2,)),
+            dma((pairs, 2)), dma((pairs, 2)), dma((2, groups + 2)), dma((2, groups + 2)),
+            dma((2,)),
         ],
         compiler_params=pltpu.CompilerParams(
             collective_id=3, has_side_effects=True, vmem_limit_bytes=LIMIT
         ),
         name="layer_tail",
     )(
-        table, prev, tail, mask, *biases, up_bias, lse, tokens, merged, cotangent, out_weight, up_weight,
+        table, prev, tail, mask, *biases, up_bias, tokens, cotangent, out_weight, up_weight,
         down_weight, query, keys, values, key_weight, value_weight, query_weight, far_tokens,
     )
 
@@ -1069,31 +1168,37 @@
     given, out, vectors = refs[:count // 2], refs[count // 2:count], refs[count:]
     for src, dst in zip(given, out):
         dst[...] = src[...]
-    features = vec_ref.shape[1]
     share = vectors[0].shape[0]
+    for n in range(8):
+        vectors[n][...] = vec_ref[n if n < 6 else n + 10, 0:share]
     shard = lax.axis_index("dp") * 4 + lax.axis_index("seq")
-    moved = pltpu.roll(vec_ref[...], lax.rem(features - shard * share, features), axis=1)
-    for n in range(8):
-        vectors[n][...] = moved[n, 0:share]
-    wide = vectors[8].shape[0] // share
-    per_row = features // (wide * share)
-    mine = vec_ref[pl.ds(8 + shard // per_row, 1), :]
-    start = lax.rem(shard, per_row) * (wide * share)
-    mine = pltpu.roll(mine, lax.rem(features - start, features), axis=1)
-    vectors[8][...] = mine[0, 0:wide * share]
+    mine = vec_ref[pl.ds(8 + shard // (2 * groups), 1), :]
+    vectors[8][...] = mine[0, 0:vectors[8].shape[0]]
+
+
+STEPS = 2
+
+
+def whole(shape):
+    return pl.BlockSpec(shape, lambda i: (0,) * len(shape))
 
 
 def hand_out(groups, vectors, arrays):
-    features = vectors.shape[1]
+    features = arrays[0].shape[1]
     share = features // (8 * groups)
     wide = arrays[-1].shape[0] // share
     shapes = [jax.ShapeDtypeStruct(a.shape, a.dtype) for a in arrays]
+    specs = [
+        pl.BlockSpec((a.shape[0] // STEPS, a.shape[1]), lambda i: (i, 0))
+        if a.shape[0] % (16 * STEPS) == 0 else whole(a.shape) for a in arrays
+    ]
     lines = [jax.ShapeDtypeStruct((share,), F32)] * 8 + [jax.ShapeDtypeStruct((wide * share,), F32)]
     return pl.pallas_call(
         functools.partial(finish_kernel, groups),
         out_shape=tuple(shapes + lines),
-        in_specs=[whole_vmem()] * (1 + len(arrays)),
-        out_specs=(whole_vmem(),) * (len(arrays) + 9),
+        grid=(STEPS,),
+        in_specs=[whole((32, 128))] + specs,
+        out_specs=tuple(specs) + (whole((share,)),) * 8 + (whole((wide * share,)),),
         name="hand_out",
     )(vectors, *arrays)
 
@@ -1129,22 +1234,22 @@
     live_tokens = (place < filled * BLK).astype(F32)[:, None]
 
     query, keys, values, far_tokens, table, prev, tail, mask = gather_project(
-        filled_blocks, tokens, random_blocks[0], query_weight, key_weight, value_weight, query_bias,
+        filled_blocks, tokens,
+        random_blocks[0].transpose(1, 2, 0).reshape(-1, 1, random_blocks.shape[1]), query_weight, key_weight, value_weight, query_bias,
         value_bias)
     keys, values = (t.reshape(-1, BLK, feature_count) for t in (keys, values))
-    merged, lse = attention_forward(table, filled_blocks, mask, query, keys, values)
-
     if groups:
         *arrays, vectors = layer_tail(
             groups, table, prev, tail, mask,
-            (out_bias, attn_gain, attn_shift, down_bias, ffn_gain, ffn_shift), up_bias[None], lse,
-            tokens, merged, cotangent, out_weight, up_weight, down_weight, query, keys, values,
+            (out_bias, attn_gain, attn_shift, down_bias, ffn_gain, ffn_shift), up_bias[None],
+            tokens, cotangent, out_weight, up_weight, down_weight, query, keys, values,
             key_weight, value_weight, query_weight, far_tokens)
         (result, grad_tokens, gq, gk, gv, go, up, down, g2, s2, bd, g1, s1, bo, bq, bv,
          bu) = hand_out(groups, vectors, arrays)
         return (
             result, grad_tokens, gq, bq, gk, gv, bv, go, bo, g1, s1, up, bu, down, bd, g2, s2)
 
+    merged, lse = attention_forward(table, filled_blocks, mask, query, keys, values)
     attn = dot(merged, out_weight) + out_bias
     first, normed_one, root_one = layer_norm(tokens.astype(F32) + attn, attn_gain, attn_shift)
     first_low = first.astype(BF16)

time: 170 us -> 153 us (0.900)
  Pallas kernels: 166 us -> 150 us
    pallas_call x2 -> x1, Pallas kernels: 40.1 us -> 25.8 us  [gather_project(): pl.pallas_call(functools.partial(gather_kernel, rows, 128), out_shape=(lo...]
    pallas_call x1, Pallas kernels: 123 us -> 120 us  [layer_tail(): pl.pallas_call(functools.partial(layer_kernel, rows, 128, own_blocks, gro...]
where the time goes in v5:
time: 153 us; the launch traced here: 152 us
  Pallas kernels  150 us (98%)
    pallas_call x1, Pallas kernels, layer_tail(): pl.pallas_call(functools.partial(layer_kernel, rows, 128, own_blocks, gro...  120 us
    pallas_call x1, Pallas kernels, gather_project(): pl.pallas_call(functools.partial(gather_kernel, rows, 128), out_shape=(lo...  25.8 us
    pallas_call x1, Pallas kernels, hand_out(): pl.pallas_call(functools.partial(finish_kernel, groups), out_shape=tuple(...  3.52 us

profile of v5, /device:TPU:0, one launch (start us, length us, event | category | flops | bytes accessed | tf_op | source)
XLA Modules:
  0.0 152.3 jit_solution(17866959930574124462)
XLA Ops:
  1.3 0.7 copy.38
  2.0 0.6 reshape.43.picks_ref
  2.6 25.8 %gather_project.1 = (bf16[512,768]{1,0:T(8,128)(2,1)}, bf16[2048,768]{1,0:T(8,128)(2,1)}, bf16[2048,768]{1,0:T(8,128)(2,1)}, bf16[512,768]{1,0:T(8,128)(2,1)}, s...) custom-call(s32[1]{0:T(128)S(6)} %copy.39.filled_ref, ...), custom_call_target="tpu_custom_call" | custom-call | tf_op jit(solution)/shard_map/gather_project/pallas_call | solution.py:206
  28.4 120.2 %layer_tail.1 = (bf16[512,768]{1,0:T(8,128)(2,1)}, f32[512,768]{1,0:T(8,128)}, f32[24,768]{1,0:T(8,128)}, f32[24,768]{1,0:T(8,128)}, f32[24,768]{1,0:T(8,128)}, ...) custom-call(s32[4,8,128]{2,1,0:T(8,128)} %get-tuple-element.51.tab_ref, ...), custom_call_target="tpu_custom_call" | custom-call | tf_op jit(solution)/shard_map/layer_tail/pallas_call | solution.py:1128
  148.6 3.5 %hand_out.1 = (bf16[512,768]{1,0:T(8,128)(2,1)}, f32[512,768]{1,0:T(8,128)}, f32[24,768]{1,0:T(8,128)}, f32[24,768]{1,0:T(8,128)}, f32[24,768]{1,0:T(8,128)}, /*...) custom-call(f32[32,128]{1,0:T(8,128)} %get-tuple-element.59.vec_ref,, ...), custom_call_target="tpu_custom_call" | custom-call | tf_op jit(solution)/shard_map/hand_out/pallas_call | solution.py:1196

commit v6 on v5

--- a/solution.py
+++ b/solution.py
@@ -96,8 +96,7 @@
     barrier = pltpu.get_barrier_semaphore()
     for other in (mate, across, diagonal):
         pl.semaphore_signal(barrier, inc=1, device_id=(dp, other), device_id_type=MESH)
-    heads_here, each = 3, picks_ref.shape[0] // 3
-    blocks = picks_ref.shape[2]
+    heads_here, each, _, blocks = picks_ref.shape
     chosen = picks_ref[...].reshape(heads_here * each, blocks).astype(F32)
     chosen = jnp.concatenate(
         [chosen, jnp.zeros((heads_here * each, 128 - blocks), F32)], axis=1)
@@ -196,7 +195,7 @@
 ):
     rows, features = tokens.shape
     own_blocks = rows // BLK
-    slot_blocks = chosen.shape[2]
+    slot_blocks = chosen.shape[3]
     copies = 4 + 1 + 4
     any_space = pl.BlockSpec(memory_space=pl.ANY)
     low = jax.ShapeDtypeStruct((rows, features), BF16)
@@ -492,25 +491,26 @@
 GELU_C = 0.7978845608028654
 UNIT = (48, 384)
 ORDERS = (
-    "yzx", "zxy", "yxz", "xzy", "xzy", "yxz", "xyz", "yxz", "yzx", "xyz", "zxy", "xzy",
+    "yxz", "yxz", "zxy", "zxy", "yxz", "xzy", "xyz", "xzy", "xyz", "xzy", "xzy", "yxz",
 )
 UP, SQUARE = 4, 8
 OUT, KEY, VALUE, QUERY = 8, 9, 10, 11
 RIDERS = (OUT, QUERY)
 EVENTS = {
-    "up": ((0, 0), (3, 0)),
+    "up": ((0, 0),),
     "dense": (),
-    0: ((2, 0), (4, 0), (1, 0)),
-    1: ((5, 0), (6, 0), (0, 1)),
-    2: ((2, 1), (1, 1), (7, 0), (3, 1)),
-    3: ((5, 1), (0, 2)),
-    4: ((8, 0), (4, 1), (7, 1), (6, 1), (1, 2), (2, 2)),
-    5: ((3, 2), (5, 2), (4, 2)),
-    "sum": (),
-    "far": (),
-    "v": ((8, 1),),
-    "x": ((7, 2), (6, 2)),
-    "end": ((9, 0), (8, 2), (11, 0), (10, 0), ("far", 0), (9, 1), (10, 1), (11, 1), (10, 2), (9, 2), (11, 2)),
+    0: ((5, 0), (1, 0), (2, 0)),
+    1: ((6, 0), (4, 0)),
+    2: (),
+    3: ((7, 0), (3, 0), (0, 1), (6, 1)),
+    4: (),
+    5: ((5, 1), (8, 0)),
+    "sum": ((1, 1),),
+    "far": ((2, 1), (7, 1), (4, 1), (5, 2), (0, 2), (3, 1)),
+    "v": ((8, 1), (6, 2)),
+    "x": (),
+    "y": ((1, 2),),
+    "end": ((11, 0), (9, 0), (4, 2), (8, 2), (10, 0), (11, 1), (9, 1), (10, 1), ("far", 0), (2, 2), (7, 2), (3, 2), (9, 2), (11, 2), (10, 2)),
 }
 
 
@@ -996,15 +996,22 @@
                     values = gathered(v_ref, shared, both, low, lanes)
                     query = split_pair(q_ref[rows_of(i), lanes], low)
                     grad = split_pair(d_merged_ref[rows_of(i), lanes], low)
-                    scores = masked_scores(dot_nt(keys, query), mask_ref, i)
+                    blank = jnp.zeros_like(query)
+                    both_in = jnp.concatenate(
+                        [jnp.concatenate([query, blank], axis=1),
+                         jnp.concatenate([blank, grad], axis=1)], axis=0)
+                    products = dot_nt(jnp.concatenate([keys, values], axis=1), both_in)
+                    scores = masked_scores(products[:, :PAIR], mask_ref, i)
                     share_of = jnp.exp(scores - lse_ref[p, pl.ds(i, 1), :])
-                    d_share = dot_nt(values, grad)
+                    d_share = products[:, PAIR:]
                     centre = jnp.sum(share_of * d_share, axis=0, keepdims=True)
                     d_scores = (share_of * (d_share - centre)).astype(BF16)
                     d_query = dot_tn(d_scores, keys) * SCALE
                     dq_ref[rows_of(i), lanes] = jnp.where(
                         low, d_query[:BLK], d_query[BLK:]).astype(BF16)
-                    parts = (dot(d_scores, query), dot(share_of.astype(BF16), grad))
+                    products = dot(
+                        jnp.concatenate([d_scores, share_of.astype(BF16)], axis=1), both_in)
+                    parts = (products[:, :PAIR], products[:, PAIR:])
                     for n, part in enumerate(parts):
                         for slot in range(3):
                             acc[n, i + slot + 1] += part[slot * BLK:(slot + 1) * BLK]
@@ -1062,13 +1069,20 @@
         tmp[...] = dot_tn(merged_ref[...], d_attn_ref[...])
         square(OUT)
         heads()
+        tmp[...] = dot_tn(x_ref[...], dq_ref[...])
+        square(QUERY)
         for name in ("far", "wk", "wv", "wq"):
             loading[name].wait()
         sum_pair(pairs - 1)
         at_point("sum")
-
         tmp[...] = dot_tn(x_ref[...], dko[...]) + dot_tn(far_ref[...], dkr[...])
         square(KEY)
+        late[...] = jnp.zeros_like(late)
+        late[0:1, :] = column_sum(dq_ref[...].astype(F32))
+        late[1:2, :] = column_sum(dvo[...].astype(F32)) + column_sum(dvr[...].astype(F32))
+        vector_pieces(1)
+        ride_core(1).start()
+        end_square(QUERY)
         out_far[...] = (dot_nt(dkr[...], wk[...]) + dot_nt(dvr[...], wv[...])).astype(BF16)
         far = remote(out_far, in_far, far_sems.at[0], far_sems.at[1], to_y)
         far.start()
@@ -1077,19 +1091,11 @@
         tmp[...] = dot_tn(x_ref[...], dvo[...]) + dot_tn(far_ref[...], dvr[...])
         square(VALUE)
         at_point("v")
-        tmp[...] = dot_tn(x_ref[...], dq_ref[...])
-        square(QUERY)
+        dx_ref[...] += dot_nt(dko[...], wk[...]) + dot_nt(dvo[...], wv[...])
         end_square(VALUE)
-        late[...] = jnp.zeros_like(late)
-        late[0:1, :] = column_sum(dq_ref[...].astype(F32))
-        late[1:2, :] = column_sum(dvo[...].astype(F32)) + column_sum(dvr[...].astype(F32))
-        vector_pieces(1)
-        ride_core(1).start()
-        end_square(QUERY)
-        dx_ref[...] += (
-            dot_nt(dko[...], wk[...]) + dot_nt(dvo[...], wv[...]) + dot_nt(dq_ref[...], wq[...])
-        )
         at_point("x")
+        dx_ref[...] += dot_nt(dq_ref[...], wq[...])
+        at_point("y")
         for u, stage in EVENTS["end"]:
             if u == "far":
                 far.wait()
@@ -1235,7 +1241,7 @@
 
     query, keys, values, far_tokens, table, prev, tail, mask = gather_project(
         filled_blocks, tokens,
-        random_blocks[0].transpose(1, 2, 0).reshape(-1, 1, random_blocks.shape[1]), query_weight, key_weight, value_weight, query_bias,
+        random_blocks.transpose(2, 3, 0, 1), query_weight, key_weight, value_weight, query_bias,
         value_bias)
     keys, values = (t.reshape(-1, BLK, feature_count) for t in (keys, values))
     if groups:

time: 153 us -> 147 us (0.961)
  Pallas kernels: 150 us -> 145 us
    pallas_call x1, Pallas kernels: 120 us -> 115 us  [layer_tail(): pl.pallas_call(functools.partial(layer_kernel, rows, 128, own_blocks, gro...]
where the time goes in v6:
time: 147 us; the launch traced here: 146 us
  Pallas kernels  145 us (99%)
  between operations  1.5 us (1%)
    pallas_call x1, Pallas kernels, layer_tail(): pl.pallas_call(functools.partial(layer_kernel, rows, 128, own_blocks, gro...  115 us
    pallas_call x1, Pallas kernels, gather_project(): pl.pallas_call(functools.partial(gather_kernel, rows, 128), out_shape=(lo...  25.9 us
    pallas_call x1, Pallas kernels, hand_out(): pl.pallas_call(functools.partial(finish_kernel, groups), out_shape=tuple(...  3.52 us

profile of v6, /device:TPU:0, one launch (start us, length us, event | category | flops | bytes accessed | tf_op | source)
XLA Modules:
  0.0 146.2 jit_solution(1514921278452523870)
XLA Ops:
  1.3 25.9 %gather_project.1 = (bf16[512,768]{1,0:T(8,128)(2,1)}, bf16[2048,768]{1,0:T(8,128)(2,1)}, bf16[2048,768]{1,0:T(8,128)(2,1)}, bf16[512,768]{1,0:T(8,128)(2,1)}, s...) custom-call(s32[1]{0:T(128)S(6)} %copy.36.filled_ref, ...), custom_call_target="tpu_custom_call" | custom-call | tf_op jit(solution)/shard_map/gather_project/pallas_call | solution.py:205
  27.2 115.3 %layer_tail.1 = (bf16[512,768]{1,0:T(8,128)(2,1)}, f32[512,768]{1,0:T(8,128)}, f32[24,768]{1,0:T(8,128)}, f32[24,768]{1,0:T(8,128)}, f32[24,768]{1,0:T(8,128)}, ...) custom-call(s32[4,8,128]{2,1,0:T(8,128)} %get-tuple-element.51.tab_ref, ...), custom_call_target="tpu_custom_call" | custom-call | tf_op jit(solution)/shard_map/layer_tail/pallas_call | solution.py:1134
  142.5 3.5 %hand_out.1 = (bf16[512,768]{1,0:T(8,128)(2,1)}, f32[512,768]{1,0:T(8,128)}, f32[24,768]{1,0:T(8,128)}, f32[24,768]{1,0:T(8,128)}, f32[24,768]{1,0:T(8,128)}, /*...) custom-call(f32[32,128]{1,0:T(8,128)} %get-tuple-element.59.vec_ref,, ...), custom_call_target="tpu_custom_call" | custom-call | tf_op jit(solution)/shard_map/hand_out/pallas_call | solution.py:1202

commit v7 on v6

--- a/solution.py
+++ b/solution.py
@@ -491,26 +491,25 @@
 GELU_C = 0.7978845608028654
 UNIT = (48, 384)
 ORDERS = (
-    "yxz", "yxz", "zxy", "zxy", "yxz", "xzy", "xyz", "xzy", "xyz", "xzy", "xzy", "yxz",
+    "xyz", "zyx", "yxz", "zxy", "yxz", "xyz", "yzx", "yxz", "yzx", "yxz", "xzy", "xzy",
 )
 UP, SQUARE = 4, 8
 OUT, KEY, VALUE, QUERY = 8, 9, 10, 11
-RIDERS = (OUT, QUERY)
+RIDERS = (OUT, VALUE)
 EVENTS = {
-    "up": ((0, 0),),
+    "up": ((0, 0), (2, 0)),
     "dense": (),
-    0: ((5, 0), (1, 0), (2, 0)),
-    1: ((6, 0), (4, 0)),
-    2: (),
-    3: ((7, 0), (3, 0), (0, 1), (6, 1)),
-    4: (),
-    5: ((5, 1), (8, 0)),
-    "sum": ((1, 1),),
-    "far": ((2, 1), (7, 1), (4, 1), (5, 2), (0, 2), (3, 1)),
-    "v": ((8, 1), (6, 2)),
+    0: ((4, 0), (5, 0), (1, 0), (2, 1)),
+    1: ((6, 0),),
+    2: ((4, 1),),
+    3: ((7, 0), (3, 0)),
+    4: ((0, 1), (2, 2)),
+    5: ((7, 1),),
+    "sum": ((8, 0), (6, 1), (3, 1)),
+    "far": ((5, 1), (1, 1), (4, 2), (6, 2), (3, 2), (0, 2), (7, 2)),
     "x": (),
-    "y": ((1, 2),),
-    "end": ((11, 0), (9, 0), (4, 2), (8, 2), (10, 0), (11, 1), (9, 1), (10, 1), ("far", 0), (2, 2), (7, 2), (3, 2), (9, 2), (11, 2), (10, 2)),
+    "y": (),
+    "end": ((11, 0), (8, 1), (9, 0), (10, 0), (5, 2), (1, 2), (8, 2), (9, 1), (11, 1), (10, 1), ("far", 0), (11, 2), (9, 2), (10, 2)),
 }
 
 
@@ -1077,22 +1076,21 @@
         at_point("sum")
         tmp[...] = dot_tn(x_ref[...], dko[...]) + dot_tn(far_ref[...], dkr[...])
         square(KEY)
+        end_square(QUERY)
+        tmp[...] = dot_tn(x_ref[...], dvo[...]) + dot_tn(far_ref[...], dvr[...])
+        square(VALUE)
+        end_square(KEY)
         late[...] = jnp.zeros_like(late)
         late[0:1, :] = column_sum(dq_ref[...].astype(F32))
         late[1:2, :] = column_sum(dvo[...].astype(F32)) + column_sum(dvr[...].astype(F32))
         vector_pieces(1)
         ride_core(1).start()
-        end_square(QUERY)
         out_far[...] = (dot_nt(dkr[...], wk[...]) + dot_nt(dvr[...], wv[...])).astype(BF16)
         far = remote(out_far, in_far, far_sems.at[0], far_sems.at[1], to_y)
         far.start()
-        end_square(KEY)
+        end_square(VALUE)
         at_point("far")
-        tmp[...] = dot_tn(x_ref[...], dvo[...]) + dot_tn(far_ref[...], dvr[...])
-        square(VALUE)
-        at_point("v")
         dx_ref[...] += dot_nt(dko[...], wk[...]) + dot_nt(dvo[...], wv[...])
-        end_square(VALUE)
         at_point("x")
         dx_ref[...] += dot_nt(dq_ref[...], wq[...])
         at_point("y")

time: 147 us -> 146 us (level)
  no operation moved by 1% of the time
where the time goes in v7:
time: 146 us; the launch traced here: 145 us
  Pallas kernels  144 us (99%)
  between operations  1.5 us (1%)
    pallas_call x1, Pallas kernels, layer_tail(): pl.pallas_call(functools.partial(layer_kernel, rows, 128, own_blocks, gro...  114 us
    pallas_call x1, Pallas kernels, gather_project(): pl.pallas_call(functools.partial(gather_kernel, rows, 128), out_shape=(lo...  25.9 us
    pallas_call x1, Pallas kernels, hand_out(): pl.pallas_call(functools.partial(finish_kernel, groups), out_shape=tuple(...  3.52 us

profile of v7, /device:TPU:0, one launch (start us, length us, event | category | flops | bytes accessed | tf_op | source)
XLA Modules:
  0.0 145.3 jit_solution(17448400516705212088)
XLA Ops:
  1.3 25.9 %gather_project.1 = (bf16[512,768]{1,0:T(8,128)(2,1)}, bf16[2048,768]{1,0:T(8,128)(2,1)}, bf16[2048,768]{1,0:T(8,128)(2,1)}, bf16[512,768]{1,0:T(8,128)(2,1)}, s...) custom-call(s32[1]{0:T(128)S(6)} %copy.36.filled_ref, ...), custom_call_target="tpu_custom_call" | custom-call | tf_op jit(solution)/shard_map/gather_project/pallas_call | solution.py:205
  27.2 114.4 %layer_tail.1 = (bf16[512,768]{1,0:T(8,128)(2,1)}, f32[512,768]{1,0:T(8,128)}, f32[24,768]{1,0:T(8,128)}, f32[24,768]{1,0:T(8,128)}, f32[24,768]{1,0:T(8,128)}, ...) custom-call(s32[4,8,128]{2,1,0:T(8,128)} %get-tuple-element.51.tab_ref, ...), custom_call_target="tpu_custom_call" | custom-call | tf_op jit(solution)/shard_map/layer_tail/pallas_call | solution.py:1132
  141.6 3.5 %hand_out.1 = (bf16[512,768]{1,0:T(8,128)(2,1)}, f32[512,768]{1,0:T(8,128)}, f32[24,768]{1,0:T(8,128)}, f32[24,768]{1,0:T(8,128)}, f32[24,768]{1,0:T(8,128)}, /*...) custom-call(f32[32,128]{1,0:T(8,128)} %get-tuple-element.59.vec_ref,, ...), custom_call_target="tpu_custom_call" | custom-call | tf_op jit(solution)/shard_map/hand_out/pallas_call | solution.py:1200

commit v8 on v7

--- a/solution.py
+++ b/solution.py
@@ -503,13 +503,13 @@
     1: ((6, 0),),
     2: ((4, 1),),
     3: ((7, 0), (3, 0)),
-    4: ((0, 1), (2, 2)),
+    4: ((0, 1),),
     5: ((7, 1),),
     "sum": ((8, 0), (6, 1), (3, 1)),
-    "far": ((5, 1), (1, 1), (4, 2), (6, 2), (3, 2), (0, 2), (7, 2)),
+    "far": ((5, 1), (1, 1)),
     "x": (),
-    "y": (),
-    "end": ((11, 0), (8, 1), (9, 0), (10, 0), (5, 2), (1, 2), (8, 2), (9, 1), (11, 1), (10, 1), ("far", 0), (11, 2), (9, 2), (10, 2)),
+    "y": ((2, 2), (4, 2), (6, 2), (3, 2), (0, 2)),
+    "end": ((11, 0), (8, 1), (9, 0), (10, 0), (9, 1), (11, 1), (7, 2), (5, 2), (1, 2), (8, 2), (10, 1), ("far", 0), (11, 2), (9, 2), (10, 2)),
 }
 
 

time: 146 us -> 146 us (level)
  no operation moved by 1% of the time
where the time goes in v8:
time: 146 us; the launch traced here: 145 us
  Pallas kernels  144 us (99%)
  between operations  1.5 us (1%)
    pallas_call x1, Pallas kernels, layer_tail(): pl.pallas_call(functools.partial(layer_kernel, rows, 128, own_blocks, gro...  114 us
    pallas_call x1, Pallas kernels, gather_project(): pl.pallas_call(functools.partial(gather_kernel, rows, 128), out_shape=(lo...  25.9 us
    pallas_call x1, Pallas kernels, hand_out(): pl.pallas_call(functools.partial(finish_kernel, groups), out_shape=tuple(...  3.52 us

profile of v8, /device:TPU:0, one launch (start us, length us, event | category | flops | bytes accessed | tf_op | source)
XLA Modules:
  0.0 145.1 jit_solution(3960333432000124364)
XLA Ops:
  1.3 25.9 %gather_project.1 = (bf16[512,768]{1,0:T(8,128)(2,1)}, bf16[2048,768]{1,0:T(8,128)(2,1)}, bf16[2048,768]{1,0:T(8,128)(2,1)}, bf16[512,768]{1,0:T(8,128)(2,1)}, s...) custom-call(s32[1]{0:T(128)S(6)} %copy.36.filled_ref, ...), custom_call_target="tpu_custom_call" | custom-call | tf_op jit(solution)/shard_map/gather_project/pallas_call | solution.py:205
  27.2 114.3 %layer_tail.1 = (bf16[512,768]{1,0:T(8,128)(2,1)}, f32[512,768]{1,0:T(8,128)}, f32[24,768]{1,0:T(8,128)}, f32[24,768]{1,0:T(8,128)}, f32[24,768]{1,0:T(8,128)}, ...) custom-call(s32[4,8,128]{2,1,0:T(8,128)} %get-tuple-element.51.tab_ref, ...), custom_call_target="tpu_custom_call" | custom-call | tf_op jit(solution)/shard_map/layer_tail/pallas_call | solution.py:1132
  141.4 3.5 %hand_out.1 = (bf16[512,768]{1,0:T(8,128)(2,1)}, f32[512,768]{1,0:T(8,128)}, f32[24,768]{1,0:T(8,128)}, f32[24,768]{1,0:T(8,128)}, f32[24,768]{1,0:T(8,128)}, /*...) custom-call(f32[32,128]{1,0:T(8,128)} %get-tuple-element.59.vec_ref,, ...), custom_call_target="tpu_custom_call" | custom-call | tf_op jit(solution)/shard_map/hand_out/pallas_call | solution.py:1200
